TPU v7x, 32 devices: a whole 2x2x4 slice. The times are simulated.
32 devices in a mesh: dp: 16 (over z, y, x), tensor: 2 (over core).
Axes of the slice: x: 2, y: 2, z: 4, core: 2. Of those that a mesh axis runs over, the one named last changes fastest.
Arguments:
- tokens: bfloat16 [16384, 1280], P('dp'), may hold values from -6 to 6
- cotangent: bfloat16 [16384, 1280], P('dp'), may hold values from -6 to 6
- segment_ids: int32 [32, 512], P('dp'), may hold values from 0 to 7, never falling along the last dimension, each value on 1 to 256 neighbouring positions
- pad_mask: int32 [32, 512], P('dp'), may hold values 0 or 1
- inward_master: float32 [3, 1280, 1280], P(None, 'dp', 'tensor'), may hold values from -8 to 8
- inward_first: bfloat16 [3, 1280, 1280], P(None, 'dp', 'tensor'), may hold values from -3 to 3
- inward_second: float32 [3, 1280, 1280], P(None, 'dp', 'tensor'), may hold values from 0.16384 to 0.65536
- outward_master: float32 [1280, 1280], P('tensor', 'dp'), may hold values from -8 to 8
- outward_first: bfloat16 [1280, 1280], P('tensor', 'dp'), may hold values from -3 to 3
- outward_second: float32 [1280, 1280], P('tensor', 'dp'), may hold values from 0.16384 to 0.65536
- expand_master: float32 [2, 1280, 5120], P(None, 'dp', 'tensor'), may hold values from -8 to 8
- expand_first: bfloat16 [2, 1280, 5120], P(None, 'dp', 'tensor'), may hold values from -1 to 1
- expand_second: float32 [2, 1280, 5120], P(None, 'dp', 'tensor'), may hold values from 0.0262144 to 0.1048576
- shrink_master: float32 [5120, 1280], P('tensor', 'dp'), may hold values from -8 to 8
- shrink_first: bfloat16 [5120, 1280], P('tensor', 'dp'), may hold values from -1 to 1
- shrink_second: float32 [5120, 1280], P('tensor', 'dp'), may hold values from 0.0262144 to 0.1048576
- alpha_master: float32 [2, 1280], P(None, 'dp'), may hold values from 0.15 to 0.6
- alpha_first: bfloat16 [2, 1280], P(None, 'dp'), may hold values from -160 to 160
- alpha_second: float32 [2, 1280], P(None, 'dp'), may hold values from 3276.8 to 13107.2
- scale_master: float32 [9, 1280], P(None, 'dp'), may hold values from 0.4 to 1.6
- scale_first: bfloat16 [9, 1280], P(None, 'dp'), may hold values from -24 to 24
- scale_second: float32 [9, 1280], P(None, 'dp'), may hold values from 81.92 to 327.68
Outputs:
- block_output: bfloat16 [16384, 1280], P('dp')
- input_grad: float32 [16384, 1280], P('dp', 'tensor')
- inward_gradient: float32 [3, 1280, 1280], P(None, 'dp', 'tensor')
- inward_variance: float32 [3, 1280, 1280], P(None, 'dp', 'tensor')
- inward_updated: float32 [3, 1280, 1280], P(None, 'dp', 'tensor')
- outward_gradient: float32 [1280, 1280], P('tensor', 'dp')
- outward_variance: float32 [1280, 1280], P('tensor', 'dp')
- outward_updated: float32 [1280, 1280], P('tensor', 'dp')
- expand_gradient: float32 [2, 1280, 5120], P(None, 'dp', 'tensor')
- expand_variance: float32 [2, 1280, 5120], P(None, 'dp', 'tensor')
- expand_updated: float32 [2, 1280, 5120], P(None, 'dp', 'tensor')
- shrink_gradient: float32 [5120, 1280], P('tensor', 'dp')
- shrink_variance: float32 [5120, 1280], P('tensor', 'dp')
- shrink_updated: float32 [5120, 1280], P('tensor', 'dp')
- alpha_gradient: float32 [2, 1280], P(None, 'dp')
- alpha_variance: float32 [2, 1280], P(None, 'dp')
- alpha_updated: float32 [2, 1280], P(None, 'dp')
- scale_gradient: float32 [9, 1280], P(None, 'dp')
- scale_variance: float32 [9, 1280], P(None, 'dp')
- scale_updated: float32 [9, 1280], P(None, 'dp')
All inputs are finite; a program needn't handle non-finite values. No bound on the sum of `pad_mask` on one device may be relied on, other than what follows from the above.
Results may differ from a plain program's by a relative error of at most 0.015.
The roundings to bfloat16 on the way count: a program that leaves them out, or rounds other values in their place, can miss the bound.
Values may be sent and summed in bfloat16 or wider, within the bound.
A program may use at most 256 MiB of HBM per device.

v0:
```python
import jax
import jax.numpy as jnp
from jax import lax
from jax.sharding import PartitionSpec as P

D = 1280
HEADS = 20
HD = 64
FF = 5120
STEP = 10


EPS_NORM = 1e-06
BETA_ONE = 0.9
BETA_TWO = 0.95
ADAM_EPS = 1e-08
RATE_MATRIX = 0.3
RATE_ALPHA = 0.08
RATE_SCALE = 0.25
MASKED = -1e30


def row_norm(values):
    factor = lax.rsqrt(jnp.mean(values * values, axis=-1, keepdims=True) + EPS_NORM)
    return (values * factor, factor)


def row_norm_back(upstream, normed, factor):
    return factor * (upstream - normed * jnp.mean(upstream * normed, axis=-1, keepdims=True))


def head_unit(values, gains):
    factor = lax.rsqrt(jnp.sum(values * values, axis=-1, keepdims=True) + EPS_NORM)
    unit_vec = values * factor
    return (gains * unit_vec, unit_vec, factor)


def head_unit_back(upstream, gains, unit_vec, factor):
    scaled = upstream * gains
    return factor * (scaled - unit_vec * jnp.sum(scaled * unit_vec, axis=-1, keepdims=True))


def allowed_mask(segment_row, pad_row):
    positions = jnp.arange(segment_row.shape[0])
    same_doc = segment_row[:, None] == segment_row[None, :]
    earlier = positions[None, :] <= positions[:, None]
    live_key = pad_row[None, :] == 0
    return same_doc & earlier & live_key | (positions[:, None] == positions[None, :])


def head_scores(queries, keys_low, allowed):
    scores = (
        jnp.einsum("qhe,khe->hqk", queries, keys_low, preferred_element_type=jnp.float32) * HD**0.5
    )
    return jnp.where(allowed[None], scores, MASKED)


def adam_step(master, first_moment, second_moment, gradient, rate):
    first_new = BETA_ONE * first_moment.astype(jnp.float32) + (1.0 - BETA_ONE) * gradient
    second_new = BETA_TWO * second_moment + (1.0 - BETA_TWO) * gradient * gradient
    ratio = (
        first_new
        / (1.0 - BETA_ONE**STEP)
        / (jnp.sqrt(second_new / (1.0 - BETA_TWO**STEP)) + ADAM_EPS)
    )
    return (master - rate * ratio, second_new)


def arrange_params(gathered, core_index):
    w_inward, w_outward, w_expand, w_shrink, alpha_copy, scale_copy = gathered
    heads_here = w_inward.shape[2] // HD
    unit_count = w_expand.shape[2]
    scale_rows = scale_copy.astype(jnp.float32)
    ratio_rows = FF // D
    query_gain = lax.dynamic_slice_in_dim(
        scale_rows[0].reshape(HEADS, HD), core_index * heads_here, heads_here, 0
    )
    gain_up = lax.dynamic_slice_in_dim(
        scale_rows[1 : 1 + ratio_rows].reshape(FF), core_index * unit_count, unit_count, 0
    )
    gain_gate = lax.dynamic_slice_in_dim(
        scale_rows[1 + ratio_rows :].reshape(FF), core_index * unit_count, unit_count, 0
    )
    return (
        w_inward,
        w_outward,
        w_expand,
        w_shrink,
        alpha_copy.astype(jnp.float32),
        query_gain,
        gain_up,
        gain_gate,
    )


def micro_step(params, tokens_in, cot_in, segment_row, pad_row, core_index):
    w_inward, w_outward, w_expand, w_shrink, alphas, query_gain, gain_up, gain_gate = params
    row_count = tokens_in.shape[0]
    heads_here = query_gain.shape[0]
    unit_count = gain_up.shape[0]
    inv_root = D ** (-0.5)
    allowed = allowed_mask(segment_row, pad_row)
    inputs = tokens_in.astype(jnp.float32)
    raw_proj = (
        jnp.einsum("rd,jdc->jrc", tokens_in, w_inward, preferred_element_type=jnp.float32)
        * inv_root
    )
    split_heads = raw_proj.reshape(3, row_count, heads_here, HD)
    query_val, query_unit, query_factor = head_unit(split_heads[0], query_gain)
    key_val, key_unit, key_factor = head_unit(split_heads[1], query_gain)
    queries = query_val.astype(jnp.bfloat16)
    keys_low = key_val.astype(jnp.bfloat16)
    values_low = split_heads[2].astype(jnp.bfloat16)
    scores = head_scores(queries, keys_low, allowed)
    top_score = jnp.max(scores, axis=-1, keepdims=True)
    expo = jnp.exp(scores - top_score)
    exp_total = jnp.sum(expo, axis=-1, keepdims=True)
    probs = expo / exp_total
    log_total = top_score + jnp.log(exp_total)
    mixed = jnp.einsum(
        "hqk,khe->qhe", probs.astype(jnp.bfloat16), values_low, preferred_element_type=jnp.float32
    )
    mixed = mixed.astype(jnp.bfloat16).reshape(row_count, heads_here * HD)
    branch = lax.psum(jnp.dot(mixed, w_outward, preferred_element_type=jnp.float32), "tensor")
    h_attn, attn_factor = row_norm(branch)
    first, first_factor = row_norm(inputs + alphas[0] * (h_attn - inputs))
    first_low = first.astype(jnp.bfloat16)
    expand_proj = (
        jnp.einsum("rd,jdf->jrf", first_low, w_expand, preferred_element_type=jnp.float32)
        * inv_root
    )
    up_branch = gain_up * expand_proj[0]
    gate_branch = gain_gate * expand_proj[1]
    sigmoid_gate = jax.nn.sigmoid(gate_branch)
    activation = gate_branch * sigmoid_gate
    hidden = (up_branch * activation).astype(jnp.bfloat16)
    shrunk = lax.psum(jnp.dot(hidden, w_shrink, preferred_element_type=jnp.float32), "tensor")
    h_mlp, mlp_factor = row_norm(shrunk)
    output, out_factor = row_norm(first + alphas[1] * (h_mlp - first))
    keep_rows = (1 - pad_row).astype(jnp.float32)[:, None]
    d_two = row_norm_back(cot_in.astype(jnp.float32) * keep_rows, output, out_factor)
    alpha_mlp_grad = jnp.sum(d_two * (h_mlp - first), axis=0)
    d_shrunk = row_norm_back(alphas[1] * d_two, h_mlp, mlp_factor).astype(jnp.bfloat16)
    shrink_grad = jnp.einsum("rf,rd->fd", hidden, d_shrunk, preferred_element_type=jnp.float32)
    d_hidden = jnp.einsum("rd,fd->rf", d_shrunk, w_shrink, preferred_element_type=jnp.float32)
    d_up = d_hidden * activation
    d_gate = d_hidden * up_branch * sigmoid_gate * (1.0 + gate_branch * (1.0 - sigmoid_gate))
    up_gain_grad = jnp.sum(d_up * expand_proj[0], axis=0)
    gate_gain_grad = jnp.sum(d_gate * expand_proj[1], axis=0)
    d_expand = jnp.stack([d_up * gain_up, d_gate * gain_gate]).astype(jnp.bfloat16)
    expand_grad = (
        jnp.einsum("rd,jrf->jdf", first_low, d_expand, preferred_element_type=jnp.float32)
        * inv_root
    )
    first_part = (
        jnp.einsum("jrf,jdf->rd", d_expand, w_expand, preferred_element_type=jnp.float32) * inv_root
    )
    d_first = (1.0 - alphas[1]) * d_two + lax.psum(first_part, "tensor")
    d_one = row_norm_back(d_first, first, first_factor)
    alpha_attn_grad = jnp.sum(d_one * (h_attn - inputs), axis=0)
    d_branch = row_norm_back(alphas[0] * d_one, h_attn, attn_factor).astype(jnp.bfloat16)
    outward_grad = jnp.einsum("rc,rd->cd", mixed, d_branch, preferred_element_type=jnp.float32)
    d_mixed = jnp.einsum("rd,cd->rc", d_branch, w_outward, preferred_element_type=jnp.float32)
    d_mixed = d_mixed.astype(jnp.bfloat16).reshape(row_count, heads_here, HD)
    probs_again = jnp.exp(head_scores(queries, keys_low, allowed) - log_total)
    d_probs = jnp.einsum("qhe,khe->hqk", d_mixed, values_low, preferred_element_type=jnp.float32)
    d_values = jnp.einsum(
        "hqk,qhe->khe",
        probs_again.astype(jnp.bfloat16),
        d_mixed,
        preferred_element_type=jnp.float32,
    )
    d_scores = probs_again * (d_probs - jnp.sum(probs_again * d_probs, axis=-1, keepdims=True))
    d_scores = d_scores.astype(jnp.bfloat16)
    d_queries = (
        jnp.einsum("hqk,khe->qhe", d_scores, keys_low, preferred_element_type=jnp.float32) * HD**0.5
    )
    d_keys = (
        jnp.einsum("hqk,qhe->khe", d_scores, queries, preferred_element_type=jnp.float32) * HD**0.5
    )
    query_gain_grad = jnp.sum(d_queries * query_unit + d_keys * key_unit, axis=0)
    d_raw = jnp.stack(
        [
            head_unit_back(d_queries, query_gain, query_unit, query_factor),
            head_unit_back(d_keys, query_gain, key_unit, key_factor),
            d_values,
        ]
    )
    d_raw = d_raw.astype(jnp.bfloat16).reshape(3, row_count, heads_here * HD)
    inward_grad = (
        jnp.einsum("rd,jrc->jdc", tokens_in, d_raw, preferred_element_type=jnp.float32) * inv_root
    )
    input_part = (
        jnp.einsum("jrc,jdc->rd", d_raw, w_inward, preferred_element_type=jnp.float32) * inv_root
    )
    own_width = D // lax.axis_size("tensor")
    residual_part = lax.dynamic_slice_in_dim(
        (1.0 - alphas[0]) * d_one, core_index * own_width, own_width, 1
    )
    input_grad = (
        lax.psum_scatter(
            input_part.astype(jnp.bfloat16), "tensor", scatter_dimension=1, tiled=True
        ).astype(jnp.float32)
        + residual_part
    )
    query_full = lax.dynamic_update_slice_in_dim(
        jnp.zeros((HEADS, HD), jnp.float32), query_gain_grad, core_index * heads_here, 0
    )
    up_full = lax.dynamic_update_slice_in_dim(
        jnp.zeros((FF,), jnp.float32), up_gain_grad, core_index * unit_count, 0
    )
    gate_full = lax.dynamic_update_slice_in_dim(
        jnp.zeros((FF,), jnp.float32), gate_gain_grad, core_index * unit_count, 0
    )
    scale_grad = jnp.concatenate(
        [query_full.reshape(1, D), up_full.reshape(FF // D, D), gate_full.reshape(FF // D, D)],
        axis=0,
    )
    owner = (core_index == 0).astype(jnp.float32)
    alpha_grad = jnp.stack([alpha_attn_grad, alpha_mlp_grad]) * owner
    return (
        output.astype(jnp.bfloat16),
        input_grad,
        (inward_grad, outward_grad, expand_grad, shrink_grad, alpha_grad, scale_grad),
    )


def per_device(
    tokens,
    cotangent,
    segment_ids,
    pad_mask,
    inward_master,
    inward_first,
    inward_second,
    outward_master,
    outward_first,
    outward_second,
    expand_master,
    expand_first,
    expand_second,
    shrink_master,
    shrink_first,
    shrink_second,
    alpha_master,
    alpha_first,
    alpha_second,
    scale_master,
    scale_first,
    scale_second,
):
    core_index = lax.axis_index("tensor")
    micro_count = segment_ids.shape[0]
    positions = segment_ids.shape[1]
    outputs = []
    input_grads = []
    totals = None
    for micro_index in range(micro_count):
        gathered = (
            lax.all_gather(inward_master.astype(jnp.bfloat16), "dp", axis=1, tiled=True),
            lax.all_gather(outward_master.astype(jnp.bfloat16), "dp", axis=1, tiled=True),
            lax.all_gather(expand_master.astype(jnp.bfloat16), "dp", axis=1, tiled=True),
            lax.all_gather(shrink_master.astype(jnp.bfloat16), "dp", axis=1, tiled=True),
            lax.all_gather(alpha_master.astype(jnp.bfloat16), "dp", axis=1, tiled=True),
            lax.all_gather(scale_master.astype(jnp.bfloat16), "dp", axis=1, tiled=True),
        )
        params = arrange_params(gathered, core_index)
        tokens_in = lax.slice_in_dim(
            tokens, micro_index * positions, (micro_index + 1) * positions, axis=0
        )
        cot_in = lax.slice_in_dim(
            cotangent, micro_index * positions, (micro_index + 1) * positions, axis=0
        )
        result = micro_step(
            params, tokens_in, cot_in, segment_ids[micro_index], pad_mask[micro_index], core_index
        )
        outputs.append(result[0])
        input_grads.append(result[1])
        grad_parts = result[2]
        totals = (
            grad_parts
            if totals is None
            else tuple(
                (earlier_sum + later_sum for earlier_sum, later_sum in zip(totals, grad_parts))
            )
        )
    totals = (
        lax.psum_scatter(totals[0], "dp", scatter_dimension=1, tiled=True),
        lax.psum_scatter(totals[1], "dp", scatter_dimension=1, tiled=True),
        lax.psum_scatter(totals[2], "dp", scatter_dimension=1, tiled=True),
        lax.psum_scatter(totals[3], "dp", scatter_dimension=1, tiled=True),
        lax.psum_scatter(totals[4], "dp", scatter_dimension=1, tiled=True),
        lax.psum_scatter(totals[5], "dp", scatter_dimension=1, tiled=True),
    )
    alpha_grad, scale_grad = lax.psum((totals[4], totals[5]), "tensor")
    inward_pre, inward_var = adam_step(
        inward_master, inward_first, inward_second, totals[0], RATE_MATRIX
    )
    outward_pre, outward_var = adam_step(
        outward_master, outward_first, outward_second, totals[1], RATE_MATRIX
    )
    expand_pre, expand_var = adam_step(
        expand_master, expand_first, expand_second, totals[2], RATE_MATRIX
    )
    shrink_pre, shrink_var = adam_step(
        shrink_master, shrink_first, shrink_second, totals[3], RATE_MATRIX
    )
    alpha_new, alpha_var = adam_step(
        alpha_master, alpha_first, alpha_second, alpha_grad, RATE_ALPHA
    )
    scale_new, scale_var = adam_step(
        scale_master, scale_first, scale_second, scale_grad, RATE_SCALE
    )
    squares = lax.psum(
        (
            jnp.sum(inward_pre * inward_pre, axis=1),
            jnp.sum(outward_pre * outward_pre, axis=1),
            jnp.sum(expand_pre * expand_pre, axis=1),
            jnp.sum(shrink_pre * shrink_pre, axis=1),
        ),
        "dp",
    )
    inward_new = inward_pre * lax.rsqrt(squares[0][:, None, :] / D + EPS_NORM)
    outward_new = outward_pre * lax.rsqrt(squares[1][:, None] / D + EPS_NORM)
    expand_new = expand_pre * lax.rsqrt(squares[2][:, None, :] / D + EPS_NORM)
    shrink_new = shrink_pre * lax.rsqrt(squares[3][:, None] / D + EPS_NORM)
    return (
        jnp.concatenate(outputs, axis=0),
        jnp.concatenate(input_grads, axis=0),
        totals[0],
        inward_var,
        inward_new,
        totals[1],
        outward_var,
        outward_new,
        totals[2],
        expand_var,
        expand_new,
        totals[3],
        shrink_var,
        shrink_new,
        alpha_grad,
        alpha_var,
        alpha_new,
        scale_grad,
        scale_var,
        scale_new,
    )


def solution(mesh):
    in_specs = (
        P("dp", None),
        P("dp", None),
        P("dp", None),
        P("dp", None),
        P(None, "dp", "tensor"),
        P(None, "dp", "tensor"),
        P(None, "dp", "tensor"),
        P("tensor", "dp"),
        P("tensor", "dp"),
        P("tensor", "dp"),
        P(None, "dp", "tensor"),
        P(None, "dp", "tensor"),
        P(None, "dp", "tensor"),
        P("tensor", "dp"),
        P("tensor", "dp"),
        P("tensor", "dp"),
        P(None, "dp"),
        P(None, "dp"),
        P(None, "dp"),
        P(None, "dp"),
        P(None, "dp"),
        P(None, "dp"),
    )
    out_specs = (
        P("dp", None),
        P("dp", "tensor"),
        P(None, "dp", "tensor"),
        P(None, "dp", "tensor"),
        P(None, "dp", "tensor"),
        P("tensor", "dp"),
        P("tensor", "dp"),
        P("tensor", "dp"),
        P(None, "dp", "tensor"),
        P(None, "dp", "tensor"),
        P(None, "dp", "tensor"),
        P("tensor", "dp"),
        P("tensor", "dp"),
        P("tensor", "dp"),
        P(None, "dp"),
        P(None, "dp"),
        P(None, "dp"),
        P(None, "dp"),
        P(None, "dp"),
        P(None, "dp"),
    )
    return jax.shard_map(
        per_device, mesh=mesh, in_specs=in_specs, out_specs=out_specs, check_vma=False
    )
```

profile of v0, /device:TPU:0, one launch (start us, length us, event | category | flops | bytes accessed | tf_op | source)
XLA Modules:
  0.0 2360.6 jit_solution(18223711685083529491)
XLA Ops:
  11.7 43.1 %all-gather.1 = bf16[16,80,9]{1,2,0:T(8,128)(2,1)S(1)} all-gather(bf16[1,80,9]{1,2,0:T(8,128)(2,1)S(1)} %convert_bitcast_fusion), channel_id=1, replica_groups=mesh['dp'=16,'tensor'=2] {'dp'}, dimensions={0}, use_global_device_ids=true | all-gather | bytes 24480 | tf_op jit(solution)/shard_map/all_gather | solution.py:265
  58.0 38.1 %all-gather.7.cloned.1.call-done = bf16[3,1280,640]{2,1,0:T(8,128)(2,1)} async-done(((bf16[3,80,640]{2,1,0:T(8,128)(2,1)}), bf16[3,1280,640]{2,1,0:T(8,128)(2,1)}) %all-gather.7.cloned.1.call-update) | async-done | bytes 4915216 | tf_op jit(solution)/shard_map/all_gather | solution.py:260
  127.6 28.5 %all-gather.9.cloned.1.call-done = bf16[640,1280]{0,1:T(8,128)(2,1)} async-done(((bf16[640,80]{0,1:T(8,128)(2,1)}), bf16[640,1280]{0,1:T(8,128)(2,1)}) %all-gather.9.cloned.1.call-update) | async-done | bytes 1638416 | tf_op jit(solution)/shard_map/all_gather | solution.py:261
  166.5 38.3 %all-gather = bf16[16,80,2]{1,2,0:T(2,128)(2,1)S(1)} all-gather(bf16[1,80,2]{1,2,0:T(2,128)(2,1)S(1)} %convert_bitcast_fusion.1), channel_id=1, replica_groups=mesh['dp'=16,'tensor'=2] {'dp'}, dimensions={0}, use_global_device_ids=true | all-gather | bytes 5440 | tf_op jit(solution)/shard_map/all_gather | solution.py:264
  213.7 140.3 %all-gather.11.cloned.1.call-done = bf16[2,1280,2560]{2,1,0:T(8,128)(2,1)} async-done(((bf16[2,80,2560]{2,1,0:T(8,128)(2,1)}), bf16[2,1280,2560]{2,1,0:T(8,128)(2,1)}) %all-gather.11.cloned.1.call-update) | async-done | bytes 13107216 | tf_op jit(solution)/shard_map/all_gather | solution.py:262
  354.0 10.3 multiply_bitcast_fusion.1
  364.3 16.4 multiply_bitcast_fusion.2
  388.3 64.0 %all-gather.13.cloned.1.call-done = bf16[2560,1280]{0,1:T(8,128)(2,1)} async-done(((bf16[2560,80]{0,1:T(8,128)(2,1)}), bf16[2560,1280]{0,1:T(8,128)(2,1)}) %all-gather.13.cloned.1.call-update) | async-done | bytes 6553616 | tf_op jit(solution)/shard_map/all_gather | solution.py:263
  452.4 8.9 fusion.140
  467.0 27.9 %all-reduce.19.cloned.1.call-done = (f32[512,1280]{1,0:T(8,128)}, f32[512,1280]{1,0:T(8,128)}) async-done(((f32[512,1280]{1,0:T(8,128)}, f32[512,1280]{1,0:T(8,128)}), (f32[512,1280]{1,0:T(8,128)}, f32[512,1280]{1,0:T(8,128)})) %all-reduce.19.cloned.1.call-update) | async-done | bytes 5242896 | tf_op jit(solution)/shard_map/psum | solution.py:137
  510.1 9.1 fusion.143
  519.2 19.3 multiply_reduce_fusion.3
  545.3 14.2 fusion.30
  559.5 13.8 fusion.28
  579.2 25.6 %all-reduce.17.cloned.1.call-done = (f32[512,1280]{1,0:T(8,128)}, f32[512,1280]{1,0:T(8,128)}) async-done(((f32[512,1280]{1,0:T(8,128)}, f32[512,1280]{1,0:T(8,128)}), (f32[512,1280]{1,0:T(8,128)}, f32[512,1280]{1,0:T(8,128)})) %all-reduce.17.cloned.1.call-update) | async-done | bytes 5242896 | tf_op jit(solution)/shard_map/psum | solution.py:158
  727.0 14.7 copy.166
  742.1 15.0 fusion.23
  757.1 17.1 multiply_bitcast_fusion
  774.2 38.8 %copy.172 = f32[2,1280,2560]{2,0,1:T(2,128)} copy(f32[2,1280,2560]{1,2,0:T(8,128)} %multiply_bitcast_fusion) | data formatting | bytes 52428800 | tf_op jit(solution)/shard_map/add | solution.py:284
  844.3 83.2 %reduce-scatter.15.cloned.1.call-done = f32[640,80]{0,1:T(8,128)} async-done(((f32[640,1280]{0,1:T(8,128)}), f32[640,80]{0,1:T(8,128)}) %reduce-scatter.15.cloned.1.call-update) | async-done | bytes 204816 | tf_op jit(solution)/shard_map/reduce_scatter | solution.py:289
  929.2 375.4 %all-reduce.13.cloned.1.call-done = f32[3,1280,640]{2,0,1:T(4,128)} async-done(((f32[3,1280,640]{2,0,1:T(4,128)}), f32[3,1280,640]{2,0,1:T(4,128)}) %all-reduce.13.cloned.1.call-update) | async-done | bytes 9830416
  1307.4 685.2 %all-reduce.15.cloned.1.call-done = f32[2,1280,2560]{2,0,1:T(2,128)} async-done(((f32[2,1280,2560]{2,0,1:T(2,128)}), f32[2,1280,2560]{2,0,1:T(2,128)}) %all-reduce.15.cloned.1.call-update) | async-done | bytes 26214416
  1998.7 268.3 %reduce-scatter.17.cloned.1.call-done = f32[2560,80]{0,1:T(8,128)} async-done(((f32[2560,1280]{0,1:T(8,128)}), f32[2560,80]{0,1:T(8,128)}) %reduce-scatter.17.cloned.1.call-update) | async-done | bytes 819216 | tf_op jit(solution)/shard_map/reduce_scatter | solution.py:291
  2270.3 79.3 %all-reduce.2 = (f32[3,640]{1,0:T(4,128)S(1)}, f32[640]{0:T(1024)S(1)}, f32[2,2560]{1,0:T(2,128)S(1)}, f32[2560]{0:T(1024)S(1)}) all-reduce(f32[3,640]{1,0:T(4,128)S(1)} %get-tuple-element.154, f32[640]{0:T(1024)S(1)} %get-tuple-element.151, f32[2,2560]{1,0:T(2,128)S(1)} %get-tuple-element.147, ...), channel_id=1, replica_groups=mesh['dp'=16,'tensor'=2] {'dp'}, use_global_device_ids=true, to_apply=%region_40.41 | all-reduce | flops 10240 | bytes 81920 | tf_op jit(solution)/shard_map/psum | solution.py:314
  (451 shorter events, 269.0 us)
Async XLA Ops:
  7.2 88.9 %copy-start.27 = (bf16[1024,1280]{1,0:T(8,128)(2,1)S(1)}, bf16[1024,1280]{1,0:T(8,128)(2,1)}, u32[]{:S(2)}) copy-start(bf16[1024,1280]{1,0:T(8,128)(2,1)} %param.22) | copy-start | bytes 7864324
  7.2 88.9 %all-gather.7.cloned.1.call-start = ((), (), s32[]{:S(2)}) async-start(), calls=%async_computation.6 | async-start | bytes 5222400 | tf_op jit(solution)/shard_map/all_gather | solution.py:260
  9.2 146.9 %all-gather.9.cloned.1.call-start = ((), (), s32[]{:S(2)}) async-start(), calls=%async_computation.7 | async-start | bytes 1740800 | tf_op jit(solution)/shard_map/all_gather | solution.py:261
  10.9 194.9 %all-reduce.21.cloned.1.call-start = ((), (), s32[]{:S(2)}) async-start(), calls=%async_computation.20 | async-start | bytes 10485760 | tf_op jit(solution)/shard_map/psum | solution.py:124
  163.2 190.7 %all-gather.11.cloned.1.call-start = ((), (), s32[]{:S(2)}) async-start(), calls=%async_computation.8 | async-start | bytes 13926400 | tf_op jit(solution)/shard_map/all_gather | solution.py:262
  165.6 286.8 %all-gather.13.cloned.1.call-start = ((), (), s32[]{:S(2)}) async-start(), calls=%async_computation.9 | async-start | bytes 6963200 | tf_op jit(solution)/shard_map/all_gather | solution.py:263
  166.5 328.4 %all-reduce.19.cloned.1.call-start = ((), (), s32[]{:S(2)}) async-start(), calls=%async_computation.19 | async-start | bytes 10485760 | tf_op jit(solution)/shard_map/psum | solution.py:137
  213.7 397.1 %copy-start.2 = (f32[512,1280]{1,0:T(8,128)}, f32[512,1280]{1,0:T(8,128)S(1)}, u32[]{:S(2)}) copy-start(f32[512,1280]{1,0:T(8,128)S(1)} %get-tuple-element.182) | copy-start | bytes 7864324
  466.3 138.5 %all-reduce.17.cloned.1.call-start = ((), (), s32[]{:S(2)}) async-start(), calls=%async_computation.18 | async-start | bytes 10485760 | tf_op jit(solution)/shard_map/psum | solution.py:158
  573.4 256.9 %reduce-scatter.23.cloned.1.call-start = ((), (), s32[]{:S(2)}) async-start(), calls=%async_computation.14 | async-start | bytes 696320
  665.4 165.8 %reduce-scatter.25.cloned.1.call-start = ((), (), s32[]{:S(2)}) async-start(), calls=%async_computation.15 | async-start | bytes 696320
  676.0 159.9 %reduce-scatter.21.cloned.1.call-start = ((), (), s32[]{:S(2)}) async-start(), calls=%async_computation.13 | async-start | bytes 1966080
  685.2 153.4 %reduce-scatter.19.cloned.1.call-start = ((), (), s32[]{:S(2)}) async-start(), calls=%async_computation.12 | async-start | bytes 1966080
  708.3 219.1 %reduce-scatter.15.cloned.1.call-start = ((), (), s32[]{:S(2)}) async-start(), calls=%async_computation.10 | async-start | bytes 3481600 | tf_op jit(solution)/shard_map/reduce_scatter | solution.py:289
  713.9 590.7 %all-reduce.13.cloned.1.call-start = ((), (), s32[]{:S(2)}) async-start(), calls=%async_computation.16 | async-start | bytes 26214400
  741.8 1250.8 %all-reduce.15.cloned.1.call-start = ((), (), s32[]{:S(2)}) async-start(), calls=%async_computation.17 | async-start | bytes 52428800
  813.1 1453.9 %reduce-scatter.17.cloned.1.call-start = ((), (), s32[]{:S(2)}) async-start(), calls=%async_computation.11 | async-start | bytes 13926400 | tf_op jit(solution)/shard_map/reduce_scatter | solution.py:291
  842.6 84.9 %copy-start.70 = (f32[640,80]{0,1:T(8,128)S(1)}, f32[640,80]{0,1:T(8,128)}, u32[]{:S(2)}) copy-start(f32[640,80]{0,1:T(8,128)} %param.29) | copy-start | bytes 614404
  842.6 84.9 %copy-start.88 = (f32[640,80]{0,1:T(8,128)S(1)}, f32[640,80]{0,1:T(8,128)}, u32[]{:S(2)}) copy-start(f32[640,80]{0,1:T(8,128)} %param.31) | copy-start | bytes 614404
  842.6 84.9 %copy-start.93 = (bf16[640,80]{0,1:T(8,128)(2,1)S(1)}, bf16[640,80]{0,1:T(8,128)(2,1)}, u32[]{:S(2)}) copy-start(bf16[640,80]{0,1:T(8,128)(2,1)} %param.30) | copy-start | bytes 307204
  844.3 461.7 %copy-start.64 = (f32[3,80,640]{2,1,0:T(8,128)S(1)}, f32[3,80,640]{2,1,0:T(8,128)}, u32[]{:S(2)}) copy-start(f32[3,80,640]{2,1,0:T(8,128)} %param.26) | copy-start | bytes 1843204
  844.3 461.7 %copy-start.76 = (f32[3,80,640]{2,1,0:T(8,128)S(1)}, f32[3,80,640]{2,1,0:T(8,128)}, u32[]{:S(2)}) copy-start(f32[3,80,640]{2,1,0:T(8,128)} %param.28) | copy-start | bytes 1843204
  844.3 461.7 %copy-start.81 = (bf16[3,80,640]{2,1,0:T(8,128)(2,1)S(1)}, bf16[3,80,640]{2,1,0:T(8,128)(2,1)}, u32[]{:S(2)}) copy-start(bf16[3,80,640]{2,1,0:T(8,128)(2,1)} %param.27) | copy-start | bytes 921604
  1307.4 686.9 %copy-start.39 = (f32[2,80,2560]{2,1,0:T(8,128)S(1)}, f32[2,80,2560]{2,1,0:T(8,128)}, u32[]{:S(2)}) copy-start(f32[2,80,2560]{2,1,0:T(8,128)} %param.32) | copy-start | bytes 4915204
  (117 other events, 742.6 us)
Sparse Core Ops, SparseCore 0:
  11.3 84.7 all-gather.6
  99.3 56.7 all-gather.8
  163.3 28.9 all-reduce.20
  195.9 158.0 all-gather.10
  357.4 94.8 all-gather.12
  466.5 28.3 all-reduce.18
  573.5 31.2 all-reduce.16
  665.6 77.9 reduce-scatter.22
  745.8 73.1 reduce-scatter.24
  821.2 5.0 reduce-scatter.20
  828.6 9.9 reduce-scatter.18
  841.5 85.9 reduce-scatter.14
  935.0 369.5 all-reduce.12
  1312.1 680.4 all-reduce.14
  1995.3 271.6 reduce-scatter.16
where the time goes:
time: 2370 us; the launch traced here: 2360 us
  waiting for transfers between devices  1740 us (73%)
  matrix products  228 us (10%)
  blocking collectives  163 us (7%)
  local copies, waits for them, and re-layouts  114 us (5%)
  other arithmetic  98.9 us (4%)
    unnamed x21, waiting for transfers between devices  1060 us
    reduce_scatter x1, waiting for transfers between devices, per_device(): lax.psum_scatter(totals[3], 'dp', scatter_dimension=1, tiled=True)  268 us
    all_gather x1, waiting for transfers between devices, per_device(): lax.all_gather(expand_master.astype(jnp.bfloat16), 'dp', axis=1, tiled=True)  140 us
    reduce_scatter x1, waiting for transfers between devices, per_device(): lax.psum_scatter(totals[1], 'dp', scatter_dimension=1, tiled=True)  83.2 us
    psum x1, blocking collectives, per_device(): lax.psum((jnp.sum(inward_pre * inward_pre, axis=1), jnp.sum(outward_pre *...  79.3 us
    all_gather x1, waiting for transfers between devices, per_device(): lax.all_gather(shrink_master.astype(jnp.bfloat16), 'dp', axis=1, tiled=True)  64 us
    add x2, local copies, waits for them, and re-layouts, per_device(): earlier_sum + later_sum  53.6 us
  transfers between devices with their start and end apart: 15, of which 11 were waited for; matrix products, arithmetic and copies ran while one was open for 11% of the time, Pallas kernels for 0%

commit v1 on v0

v1 whole, which is shorter than its diff:
```python
import functools

import jax
import jax.numpy as jnp
from jax import lax
from jax.experimental import pallas as pl
from jax.experimental.pallas import tpu as pltpu
from jax.sharding import PartitionSpec as P

D = 1280
HEADS = 20
HD = 64
FF = 5120
STEP = 10
LONGEST = 256


EPS_NORM = 1e-06
BETA_ONE = 0.9
BETA_TWO = 0.95
ADAM_EPS = 1e-08
RATE_MATRIX = 0.3
RATE_ALPHA = 0.08
RATE_SCALE = 0.25
MASKED = -1e30
F32 = jnp.float32
BF16 = jnp.bfloat16


def row_norm(values):
    factor = lax.rsqrt(jnp.mean(values * values, axis=-1, keepdims=True) + EPS_NORM)
    return (values * factor, factor)


def row_norm_back(upstream, normed, factor):
    return factor * (upstream - normed * jnp.mean(upstream * normed, axis=-1, keepdims=True))


def adam_step(master, first_moment, second_moment, gradient, rate):
    first_new = BETA_ONE * first_moment.astype(F32) + (1.0 - BETA_ONE) * gradient
    second_new = BETA_TWO * second_moment + (1.0 - BETA_TWO) * gradient * gradient
    ratio = (
        first_new
        / (1.0 - BETA_ONE**STEP)
        / (jnp.sqrt(second_new / (1.0 - BETA_TWO**STEP)) + ADAM_EPS)
    )
    return (master - rate * ratio, second_new)


LANES = 128
PLACES = (2, 1, 4, 8)
ROUTES = ((3, 2, 1, 0), (3, 2, 0, 1), (1, 0, 3, 2), (0, 1, 3, 2))
EVERY = 4
LAG = 2
RING = 4


def partner_of(me, bit):
    return me + bit - 2 * bit * ((me // bit) % 2)


def greet(me):
    barrier = pltpu.get_barrier_semaphore()
    for bit in PLACES:
        pl.semaphore_signal(
            barrier,
            inc=1,
            device_id={"dp": partner_of(me, bit)},
            device_id_type=pl.DeviceIdType.MESH,
        )
    pl.semaphore_wait(barrier, len(PLACES))


def tile_plan(columns):
    tiles = columns // LANES
    rare = tiles // 10
    often = (tiles - 2 * rare) // 2
    return (
        (0, 2, often, 1),
        (1, 2, often, 1),
        (2 * often, 1, rare, EVERY),
        (2 * often + rare, 1, rare, EVERY),
    )


def for_tiles(step, hop, plan, body):
    for route, (_, _, number, every) in enumerate(plan):
        if number == 0:
            continue
        at = step - hop * LAG
        due = (at >= 0) & (at < number * every)
        if every > 1:
            due = due & (at % every == 0)

        @pl.when(due)
        def _():
            body(route, at // every)


def lanes_of(plan, route, tile):
    first, stride, _, _ = plan[route]
    return pl.ds(pl.multiple_of((first + stride * tile) * LANES, LANES), LANES)


def steps_of(plan, hops):
    return max((number - 1) * every + 1 for _, _, number, every in plan if number) + hops * LAG


def gather_kernel(plan, block, out, own_sem, send_sem, recv_sem):
    me = lax.axis_index("dp")
    own = pltpu.make_async_copy(block, out.at[0, 0, 0, 0], own_sem)
    own.start()
    greet(me)

    def piece(hop, route, tile):
        lanes = lanes_of(plan, route, tile)
        crossed, place = ROUTES[route][:hop], ROUTES[route][hop]
        source = [slice(None) if axis in crossed else 0 for axis in range(4)]
        target = [1 if axis == place else source[axis] for axis in range(4)]
        if hop == 0:
            source_ref = block.at[:, lanes]
        else:
            source_ref = out.at[(*source, slice(None), lanes)]
        return pltpu.make_async_remote_copy(
            src_ref=source_ref,
            dst_ref=out.at[(*target, slice(None), lanes)],
            send_sem=send_sem.at[hop, route, tile % RING],
            recv_sem=recv_sem.at[hop, route, tile],
            device_id={"dp": partner_of(me, PLACES[place])},
            device_id_type=pl.DeviceIdType.MESH,
        )

    def step(index, _):
        for hop in range(5):

            def body(route, tile, hop=hop):
                if hop > 0:
                    piece(hop - 1, route, tile).wait_recv()
                if hop < 4:

                    @pl.when(tile >= RING)
                    def _():
                        piece(hop, route, tile - RING).wait_send()

                    piece(hop, route, tile).start()

            for_tiles(index, hop, plan, body)
        return 0

    lax.fori_loop(0, LAG, step, 0)
    own.wait()
    lax.fori_loop(LAG, steps_of(plan, 4), step, 0)
    for route, (_, _, number, _) in enumerate(plan):
        for tile in range(max(0, number - RING), number):
            for hop in range(4):
                piece(hop, route, tile).wait_send()


def gather_columns(block, collective_id):
    rows, columns = block.shape
    plan = tile_plan(columns)
    most = max(number for _, _, number, _ in plan)
    out = pl.pallas_call(
        functools.partial(gather_kernel, plan),
        out_shape=jax.ShapeDtypeStruct((2, 2, 2, 2, rows, columns), BF16),
        in_specs=[pl.BlockSpec(memory_space=pltpu.VMEM)],
        out_specs=pl.BlockSpec(memory_space=pl.ANY),
        scratch_shapes=[
            pltpu.SemaphoreType.DMA,
            pltpu.SemaphoreType.DMA((4, 4, RING)),
            pltpu.SemaphoreType.DMA((4, 4, most)),
        ],
        compiler_params=pltpu.CompilerParams(
            collective_id=collective_id, has_side_effects=True, vmem_limit_bytes=16 << 20
        ),
        name="gather_columns",
    )(block)
    return out.reshape(16 * rows, columns)


def sum_kernel(plan, left_of, scale, left, right, out, work, arrived, send_sem, recv_sem):
    me = lax.axis_index("dp")
    greet(me)
    rows = out.shape[0]

    def piece(hop, route, tile):
        place = ROUTES[route][3 - hop]
        slot = tile % RING
        return pltpu.make_async_remote_copy(
            src_ref=work[hop].at[route, slot, 1],
            dst_ref=arrived[hop].at[route, tile],
            send_sem=send_sem.at[hop, route, slot],
            recv_sem=recv_sem.at[hop, route, tile],
            device_id={"dp": partner_of(me, PLACES[place])},
            device_id_type=pl.DeviceIdType.MESH,
        )

    def send(hop, route, tile, fill):
        @pl.when(tile >= RING)
        def _():
            piece(hop, route, tile - RING).wait_send()

        fill(work[hop].at[route, tile % RING])
        piece(hop, route, tile).start()

    def product(route, tile):
        part = (
            lax.dot_general(
                left[left_of(route, tile)],
                right[:, lanes_of(plan, route, tile)],
                (((1,), (0,)), ((), ())),
                preferred_element_type=F32,
            )
            * scale
        ).astype(BF16)

        def fill(slot):
            axes = ROUTES[route][::-1]
            for block in range(16):
                bits = [(block >> (3 - axis)) & 1 for axis in axes]
                index = bits[1] * 4 + bits[2] * 2 + bits[3]
                slot[bits[0], index * rows : (index + 1) * rows, :] = part[
                    block * rows : (block + 1) * rows
                ]

        send(0, route, tile, fill)

    def add(hop, route, tile):
        piece(hop - 1, route, tile).wait_recv()
        kept = work[hop - 1][route, tile % RING, 0].astype(F32)
        total = kept + arrived[hop - 1][route, tile].astype(F32)
        if hop == 4:
            out[:, lanes_of(plan, route, tile)] = total
            return
        half = total.shape[0] // 2

        def fill(slot):
            slot[0] = total[:half].astype(BF16)
            slot[1] = total[half:].astype(BF16)

        send(hop, route, tile, fill)

    def step(index, _):
        for hop in range(4, 0, -1):
            for_tiles(index, hop, plan, functools.partial(add, hop))
        for_tiles(index, 0, plan, product)
        return 0

    lax.fori_loop(0, steps_of(plan, 4), step, 0)
    for route, (_, _, number, _) in enumerate(plan):
        for tile in range(max(0, number - RING), number):
            for hop in range(4):
                piece(hop, route, tile).wait_send()


def sum_products(left, right, left_of, scale, collective_id):
    rows = left.shape[1] // 16
    columns = right.shape[1]
    plan = tile_plan(columns)
    most = max(number for _, _, number, _ in plan)
    halves = [rows * 8 >> hop for hop in range(4)]
    return pl.pallas_call(
        functools.partial(sum_kernel, plan, left_of, scale),
        out_shape=jax.ShapeDtypeStruct((rows, columns), F32),
        in_specs=[pl.BlockSpec(memory_space=pltpu.VMEM)] * 2,
        out_specs=pl.BlockSpec(memory_space=pltpu.VMEM),
        scratch_shapes=[
            [pltpu.VMEM((4, RING, 2, half, LANES), BF16) for half in halves],
            [pltpu.VMEM((4, most, half, LANES), BF16) for half in halves],
            pltpu.SemaphoreType.DMA((4, 4, RING)),
            pltpu.SemaphoreType.DMA((4, 4, most)),
        ],
        compiler_params=pltpu.CompilerParams(
            collective_id=collective_id, has_side_effects=True, vmem_limit_bytes=56 << 20
        ),
        name="sum_products",
    )(left, right)


def extra_bits(count):
    return [bit for bit in (1 << k for k in range(4, count.bit_length() - 1))]


def exchange(array, bit, count):
    return lax.ppermute(array, "dp", [(i, i ^ bit) for i in range(count)])


def swap_cores(array):
    return lax.ppermute(array, "tensor", [(0, 1), (1, 0)])


def gather(block, count, collective_id):
    for bit in extra_bits(count)[::-1]:
        block = jnp.concatenate([block, exchange(block, bit, count)], axis=0)
    return gather_columns(block, collective_id)


def scatter_rest(partial, count):
    for bit in extra_bits(count):
        half = partial.shape[0] // 2
        partial = partial[:half] + exchange(partial[half:], bit, count)
    return partial


def butterfly_sum(array, count):
    for bit in list(PLACES) + extra_bits(count):
        array = array + exchange(array, bit, count)
    return array


def scatter_sum(partial, count):
    for bit in PLACES:
        half = partial.shape[0] // 2
        partial = partial[:half] + exchange(partial[half:], bit, count)
    return scatter_rest(partial, count)


def place_matrix(me, count):
    places = list(PLACES) + extra_bits(count)
    width = D // count
    natural = lax.broadcasted_iota(jnp.int32, (D, D), 0)
    placed = lax.broadcasted_iota(jnp.int32, (D, D), 1)
    position, offset = placed // width, placed % width
    relative = jnp.zeros_like(position)
    for axis, bit in enumerate(places):
        value = (position >> (len(places) - 1 - axis)) & 1
        relative = relative + value * bit
    return (natural == (relative ^ me) * width + offset).astype(BF16)


def nn(a, b):
    return lax.dot_general(a, b, (((1,), (0,)), ((), ())), preferred_element_type=F32)


def nt(a, b):
    return lax.dot_general(a, b, (((1,), (1,)), ((), ())), preferred_element_type=F32)


def tn(a, b):
    return lax.dot_general(a, b, (((0,), (0,)), ((), ())), preferred_element_type=F32)


def head_factors(raw, low_lanes):
    squares = raw * raw
    low = jnp.sum(jnp.where(low_lanes, squares, 0.0), axis=-1, keepdims=True)
    high = jnp.sum(jnp.where(low_lanes, 0.0, squares), axis=-1, keepdims=True)
    return jnp.where(low_lanes, lax.rsqrt(low + EPS_NORM), lax.rsqrt(high + EPS_NORM))


def head_sums(values, low_lanes):
    low = jnp.sum(jnp.where(low_lanes, values, 0.0), axis=-1, keepdims=True)
    high = jnp.sum(jnp.where(low_lanes, 0.0, values), axis=-1, keepdims=True)
    return jnp.where(low_lanes, low, high)


Q_TILE = 128


def key_range(tile):
    start = max(0, tile * Q_TILE - LONGEST)
    return start, (tile + 1) * Q_TILE


def attend_kernel(raw_q, raw_k, raw_v, gain, bias, mixed):
    length = raw_q.shape[0]
    low_lanes = lax.broadcasted_iota(jnp.int32, (1, 2 * HD), 1) < HD
    query = raw_q[...]
    key = raw_k[...]
    query = (gain[...] * (query * head_factors(query, low_lanes))).astype(BF16) * 8
    key = (gain[...] * (key * head_factors(key, low_lanes))).astype(BF16)
    value = raw_v[...].astype(BF16)
    zero = jnp.zeros_like(query)
    parts = (jnp.where(low_lanes, query, zero), jnp.where(low_lanes, zero, query))
    for tile in range(length // Q_TILE):
        start, end = key_range(tile)
        rows = slice(tile * Q_TILE, (tile + 1) * Q_TILE)
        tile_bias = bias[0, rows, start:end]
        results = []
        for part in parts:
            expo = jnp.exp(nt(part[rows], key[start:end]) + tile_bias)
            total = jnp.sum(expo, axis=-1, keepdims=True)
            results.append(nn(expo.astype(BF16), value[start:end]) * (1.0 / total))
        mixed[rows, :] = jnp.where(low_lanes, results[0], results[1]).astype(BF16)


def attend_back_kernel(
    raw_q, raw_k, raw_v, d_mixed, gain, bias, d_raw_q, d_raw_k, d_raw_v, gain_grad, sum_k, sum_v
):
    length = raw_q.shape[0]
    low_lanes = lax.broadcasted_iota(jnp.int32, (1, 2 * HD), 1) < HD
    gains = gain[...]
    key_raw = raw_k[...]
    key_factor = head_factors(key_raw, low_lanes)
    key_unit = key_raw * key_factor
    key = (gains * key_unit).astype(BF16)
    key_eight = key * 8
    value = raw_v[...].astype(BF16)
    sum_k[...] = jnp.zeros_like(sum_k)
    sum_v[...] = jnp.zeros_like(sum_v)
    gain_total = jnp.zeros((1, 2 * HD), F32)

    def back(upstream, unit, factor):
        scaled = gains * upstream
        return (factor * (scaled - unit * head_sums(scaled * unit, low_lanes))).astype(BF16)

    for tile in range(length // Q_TILE):
        start, end = key_range(tile)
        rows = slice(tile * Q_TILE, (tile + 1) * Q_TILE)
        query_raw = raw_q[rows, :]
        query_factor = head_factors(query_raw, low_lanes)
        query_unit = query_raw * query_factor
        query = (gains * query_unit).astype(BF16) * 8
        upstream = d_mixed[rows, :].astype(F32)
        tile_bias = bias[0, rows, start:end]
        d_query = []
        for low in (True, False):
            lanes = low_lanes if low else jnp.logical_not(low_lanes)
            own_query = jnp.where(lanes, query, jnp.zeros_like(query))
            expo = jnp.exp(nt(own_query, key[start:end]) + tile_bias)
            inverse = 1.0 / jnp.sum(expo, axis=-1, keepdims=True)
            expo_low = expo.astype(BF16)
            result = nn(expo_low, value[start:end]) * inverse
            own_up = jnp.where(lanes, upstream, 0.0)
            delta = jnp.sum(result * own_up, axis=-1, keepdims=True) * inverse
            own_up = (own_up * inverse).astype(BF16)
            sum_v[start:end, :] += tn(expo_low, own_up)
            d_scores = (expo * (nt(own_up, value[start:end]) - delta)).astype(BF16)
            d_query.append(nn(d_scores, key_eight[start:end]))
            sum_k[start:end, :] += tn(d_scores, own_query)
        d_query = jnp.where(low_lanes, d_query[0], d_query[1])
        gain_total += jnp.sum(d_query * query_unit, axis=0, keepdims=True)
        d_raw_q[rows, :] = back(d_query, query_unit, query_factor)
    d_key = sum_k[...]
    gain_total += jnp.sum(d_key * key_unit, axis=0, keepdims=True)
    d_raw_k[...] = back(d_key, key_unit, key_factor)
    d_raw_v[...] = sum_v[...].astype(BF16)
    gain_grad[...] = jnp.broadcast_to(gain_total[None], gain_grad.shape)


def attend_specs(length):
    lanes = pl.BlockSpec((length, 2 * HD), lambda s, h: (s, h))
    gain = pl.BlockSpec((1, 2 * HD), lambda s, h: (0, h))
    bias = pl.BlockSpec((1, length, length), lambda s, h: (s, 0, 0))
    return lanes, gain, bias


def attend(raw, gain, bias):
    count, length, _ = bias.shape
    rows, columns = raw[0].shape
    lanes, gain_spec, bias_spec = attend_specs(length)
    return pl.pallas_call(
        attend_kernel,
        grid=(count, columns // (2 * HD)),
        in_specs=[lanes, lanes, lanes, gain_spec, bias_spec],
        out_specs=lanes,
        out_shape=jax.ShapeDtypeStruct((rows, columns), BF16),
        compiler_params=pltpu.CompilerParams(vmem_limit_bytes=40 << 20),
        cost_estimate=pl.CostEstimate(
            flops=4 * rows * length * columns, bytes_accessed=14 * rows * columns, transcendentals=0
        ),
        name="attend",
    )(*raw, gain, bias)


def attend_back(raw, d_mixed, gain, bias):
    count, length, _ = bias.shape
    rows, columns = raw[0].shape
    lanes, gain_spec, bias_spec = attend_specs(length)
    out = jax.ShapeDtypeStruct((rows, columns), BF16)
    result = pl.pallas_call(
        attend_back_kernel,
        grid=(count, columns // (2 * HD)),
        in_specs=[lanes, lanes, lanes, lanes, gain_spec, bias_spec],
        out_specs=[lanes, lanes, lanes, pl.BlockSpec((1, 8, 2 * HD), lambda s, h: (s, 0, h))],
        out_shape=[out, out, out, jax.ShapeDtypeStruct((count, 8, columns), F32)],
        scratch_shapes=[pltpu.VMEM((length, 2 * HD), F32)] * 2,
        compiler_params=pltpu.CompilerParams(vmem_limit_bytes=40 << 20),
        cost_estimate=pl.CostEstimate(
            flops=12 * rows * length * columns, bytes_accessed=20 * rows * columns, transcendentals=0
        ),
        name="attend_back",
    )(*raw, d_mixed, gain, bias)
    return result[:3], jnp.sum(result[3][:, 0, :], axis=0)


def bias_of(segment_ids, pad_mask):
    positions = jnp.arange(segment_ids.shape[1])
    key_code = jnp.where(pad_mask == 0, segment_ids, -1)
    earlier = positions[None, :] <= positions[:, None]
    same = positions[None, :] == positions[:, None]
    allowed = (segment_ids[:, :, None] == key_code[:, None, :]) & earlier[None] | same[None]
    return jnp.where(allowed, 0.0, MASKED).astype(F32)


def one_left(route, tile):
    return 0


def attention_left_of(route, tile):
    if route < 2:
        return jnp.where(tile < 2, 0, 1)
    return jnp.where(tile < 1, 0, 1) if route == 2 else 1


def per_device(
    tokens,
    cotangent,
    segment_ids,
    pad_mask,
    inward_master,
    inward_first,
    inward_second,
    outward_master,
    outward_first,
    outward_second,
    expand_master,
    expand_first,
    expand_second,
    shrink_master,
    shrink_first,
    shrink_second,
    alpha_master,
    alpha_first,
    alpha_second,
    scale_master,
    scale_first,
    scale_second,
):
    count = lax.axis_size("dp")
    me = lax.axis_index("dp")
    core = lax.axis_index("tensor")
    inv_root = D ** (-0.5)
    rows = tokens.shape[0]
    own_rows = rows // 2
    heads_width = inward_master.shape[2]
    units = expand_master.shape[2]

    small = jnp.concatenate([alpha_master, scale_master], axis=0).astype(BF16)
    small_count = small.shape[0]
    small = jnp.pad(small, ((0, 128 - small_count), (0, 0))).T
    attention_copies = jnp.concatenate(
        [
            inward_master[0].astype(BF16),
            inward_master[1].astype(BF16),
            inward_master[2].astype(BF16),
            outward_master.astype(BF16).T,
            jnp.pad(small, ((0, 0), (0, 128))),
        ],
        axis=1,
    )
    attention_copies = gather(attention_copies, count, 0)
    w_inward = attention_copies[:, : 3 * heads_width]
    w_outward = attention_copies[:, 3 * heads_width : 4 * heads_width]
    small = attention_copies[:, 4 * heads_width : 4 * heads_width + 128]

    places = place_matrix(me, count)
    tokens_in = nn(tokens, places).astype(BF16)
    cot_own = lax.dynamic_slice_in_dim(cotangent, core * own_rows, own_rows, 0)
    cot_own = nn(cot_own, places)
    keep = (1 - pad_mask).astype(F32).reshape(rows, 1)
    cot_own = cot_own * lax.dynamic_slice_in_dim(keep, core * own_rows, own_rows, 0)
    tokens_own = lax.dynamic_slice_in_dim(tokens_in, core * own_rows, own_rows, 0).astype(F32)
    alphas = small[:, :2].T.astype(F32)
    scale_rows = tn(small, places.T)[2:small_count]
    query_gain = lax.dynamic_slice_in_dim(scale_rows[0], core * heads_width, heads_width, 0)[None]
    ratio_rows = FF // D
    gain_up = lax.dynamic_slice_in_dim(
        scale_rows[1 : 1 + ratio_rows].reshape(FF), core * units, units, 0
    )
    gain_gate = lax.dynamic_slice_in_dim(
        scale_rows[1 + ratio_rows :].reshape(FF), core * units, units, 0
    )
    bias = bias_of(segment_ids, pad_mask)

    def sum_own(partial):
        send = lax.dynamic_slice_in_dim(partial, (1 - core) * own_rows, own_rows, 0)
        kept = lax.dynamic_slice_in_dim(partial, core * own_rows, own_rows, 0)
        return kept + swap_cores(send)

    def both(own):
        other = swap_cores(own)
        full = jnp.zeros((rows, own.shape[1]), own.dtype)
        full = lax.dynamic_update_slice_in_dim(full, own, core * own_rows, 0)
        return lax.dynamic_update_slice_in_dim(full, other, (1 - core) * own_rows, 0)

    raw = nn(tokens_in, w_inward) * inv_root
    raw = [raw[:, k * heads_width : (k + 1) * heads_width] for k in range(3)]
    mixed = attend(raw, query_gain, bias)
    branch = sum_own(nt(mixed, w_outward))
    h_attn, attn_factor = row_norm(branch)
    first, first_factor = row_norm(tokens_own + alphas[0] * (h_attn - tokens_own))
    first_low = both(first.astype(BF16))
    unit_copies = jnp.concatenate(
        [
            expand_master[0].astype(BF16),
            expand_master[1].astype(BF16),
            shrink_master.astype(BF16).T,
        ],
        axis=1,
    )
    unit_copies, first_low = lax.optimization_barrier((unit_copies, first_low))
    unit_copies = gather(unit_copies, count, 1)
    w_up = unit_copies[:, :units]
    w_gate = unit_copies[:, units : 2 * units]
    w_shrink = unit_copies[:, 2 * units :]
    proj_up = nn(first_low, w_up) * inv_root
    proj_gate = nn(first_low, w_gate) * inv_root
    up_branch = gain_up * proj_up
    gate_branch = gain_gate * proj_gate
    sigmoid_gate = jax.nn.sigmoid(gate_branch)
    activation = gate_branch * sigmoid_gate
    hidden = (up_branch * activation).astype(BF16)
    shrunk = sum_own(nt(hidden, w_shrink))
    h_mlp, mlp_factor = row_norm(shrunk)
    output, out_factor = row_norm(first + alphas[1] * (h_mlp - first))

    d_two = row_norm_back(cot_own, output, out_factor)
    alpha_mlp_grad = jnp.sum(d_two * (h_mlp - first), axis=0)
    d_shrunk = both(row_norm_back(alphas[1] * d_two, h_mlp, mlp_factor).astype(BF16))
    shrink_grad = sum_products(d_shrunk.T[None], hidden, one_left, 1.0, 2)
    shrink_grad = scatter_rest(shrink_grad, count).T
    d_hidden = nn(d_shrunk, w_shrink)
    d_up = d_hidden * activation
    d_gate = d_hidden * up_branch * sigmoid_gate * (1.0 + gate_branch * (1.0 - sigmoid_gate))
    up_gain_grad = jnp.sum(d_up * proj_up, axis=0)
    gate_gain_grad = jnp.sum(d_gate * proj_gate, axis=0)
    d_proj_up = (d_up * gain_up).astype(BF16)
    d_proj_gate = (d_gate * gain_gate).astype(BF16)
    d_expand = jnp.concatenate([d_proj_up, d_proj_gate], axis=1)
    expand_grad = sum_products(first_low.T[None], d_expand, one_left, inv_root, 3)
    expand_grad = scatter_rest(expand_grad, count)
    expand_grad = jnp.stack([expand_grad[:, :units], expand_grad[:, units:]])
    first_part = sum_own((nt(d_proj_up, w_up) + nt(d_proj_gate, w_gate)) * inv_root)
    d_first = (1.0 - alphas[1]) * d_two + first_part
    d_one = row_norm_back(d_first, first, first_factor)
    alpha_attn_grad = jnp.sum(d_one * (h_attn - tokens_own), axis=0)
    d_branch = both(row_norm_back(alphas[0] * d_one, h_attn, attn_factor).astype(BF16))
    d_mixed = nn(d_branch, w_outward).astype(BF16)
    d_raw, query_gain_grad = attend_back(raw, d_mixed, query_gain, bias)
    attention_right = jnp.concatenate(
        [mixed[:, :512], *d_raw[:2], d_raw[2][:, :256], mixed[:, 512:], d_raw[2][:, 256:]], axis=1
    )
    attention_left = jnp.stack([d_branch.T, tokens_in.T])
    attention_grad = sum_products(attention_left, attention_right, attention_left_of, 1.0, 4)
    attention_grad = scatter_rest(attention_grad, count)
    input_part = (nt(jnp.concatenate(d_raw, axis=1), w_inward)) * inv_root

    block_output = both(nt(output.astype(BF16), places).astype(BF16))
    residual = (1.0 - alphas[0]) * d_one
    residual_high = residual.astype(BF16)
    residual_low = (residual - residual_high.astype(F32)).astype(BF16)
    residual = nt(residual_high, places) + nt(residual_low, places)
    own_width = D // lax.axis_size("tensor")
    input_part = nt(input_part.astype(BF16), places)
    input_part = lax.dynamic_update_slice_in_dim(
        input_part,
        lax.dynamic_slice_in_dim(input_part, core * own_rows, own_rows, 0) + residual,
        core * own_rows,
        0,
    )
    input_grad = lax.dynamic_slice_in_dim(input_part, core * own_width, own_width, 1) + swap_cores(
        lax.dynamic_slice_in_dim(input_part, (1 - core) * own_width, own_width, 1)
    )

    alpha_grad = jnp.stack([alpha_attn_grad, alpha_mlp_grad])
    query_full = lax.dynamic_update_slice_in_dim(
        jnp.zeros((D,), F32), query_gain_grad, core * heads_width, 0
    )
    up_full = lax.dynamic_update_slice_in_dim(jnp.zeros((FF,), F32), up_gain_grad, core * units, 0)
    gate_full = lax.dynamic_update_slice_in_dim(
        jnp.zeros((FF,), F32), gate_gain_grad, core * units, 0
    )
    scale_grad = jnp.concatenate(
        [query_full.reshape(1, D), up_full.reshape(FF // D, D), gate_full.reshape(FF // D, D)],
        axis=0,
    )
    alpha_grad = alpha_grad + swap_cores(alpha_grad)
    scale_grad = scale_grad + swap_cores(scale_grad)
    width = D // count
    alpha_grad = scatter_sum(alpha_grad.T, count).T
    scale_grad = lax.dynamic_slice_in_dim(butterfly_sum(scale_grad, count), me * width, width, 1)

    outward_grad = jnp.concatenate(
        [attention_grad[:, :512], attention_grad[:, 2048:2176]], axis=1
    ).T
    inward_grad = jnp.stack(
        [
            attention_grad[:, 512:1152],
            attention_grad[:, 1152:1792],
            jnp.concatenate([attention_grad[:, 1792:2048], attention_grad[:, 2176:]], axis=1),
        ]
    ) * inv_root
    inward_pre, inward_var = adam_step(
        inward_master, inward_first, inward_second, inward_grad, RATE_MATRIX
    )
    outward_pre, outward_var = adam_step(
        outward_master, outward_first, outward_second, outward_grad, RATE_MATRIX
    )
    expand_pre, expand_var = adam_step(
        expand_master, expand_first, expand_second, expand_grad, RATE_MATRIX
    )
    shrink_pre, shrink_var = adam_step(
        shrink_master, shrink_first, shrink_second, shrink_grad, RATE_MATRIX
    )
    alpha_new, alpha_var = adam_step(
        alpha_master, alpha_first, alpha_second, alpha_grad, RATE_ALPHA
    )
    scale_new, scale_var = adam_step(
        scale_master, scale_first, scale_second, scale_grad, RATE_SCALE
    )

    def renormed(pre, axis):
        squares = butterfly_sum(jnp.sum(pre * pre, axis=axis), count)
        return pre * lax.rsqrt(jnp.expand_dims(squares, axis) / D + EPS_NORM)

    return (
        block_output,
        input_grad,
        inward_grad,
        inward_var,
        renormed(inward_pre, 1),
        outward_grad,
        outward_var,
        renormed(outward_pre, 1),
        expand_grad,
        expand_var,
        renormed(expand_pre, 1),
        shrink_grad,
        shrink_var,
        renormed(shrink_pre, 1),
        alpha_grad,
        alpha_var,
        alpha_new,
        scale_grad,
        scale_var,
        scale_new,
    )


def solution(mesh):
    rows = P("dp", None)
    deep = P(None, "dp", "tensor")
    flat = P("tensor", "dp")
    vector = P(None, "dp")
    in_specs = (rows,) * 4 + (deep,) * 3 + (flat,) * 3 + (deep,) * 3 + (flat,) * 3 + (vector,) * 6
    out_specs = (
        (rows, P("dp", "tensor"))
        + (deep,) * 3
        + (flat,) * 3
        + (deep,) * 3
        + (flat,) * 3
        + (vector,) * 6
    )
    return jax.shard_map(
        per_device, mesh=mesh, in_specs=in_specs, out_specs=out_specs, check_vma=False
    )
```

time: 2370 us -> 851 us (0.36)
  waiting for transfers between devices: 1740 us -> 35.1 us
  Pallas kernels: 0 us -> 533 us
  blocking collectives: 163 us -> 0 us
  matrix products: 228 us -> 137 us
  local copies, waits for them, and re-layouts: 114 us -> 53.6 us
  other arithmetic: 98.9 us -> 56.7 us
    unnamed x21 -> x0, waiting for transfers between devices: 1060 us -> none
    pallas_call x0 -> x7, Pallas kernels: none -> 533 us  [the longest x3 252 us: sum_products(): pl.pallas_call(functools.partial(sum_kernel, plan, left_of, scale), out_s...]
    reduce_scatter x2 -> x0, waiting for transfers between devices: 351 us -> none  [the longest x1 268 us: per_device(): lax.psum_scatter(totals[3], 'dp', scatter_dimension=1, tiled=True)]
    all_gather x4 -> x0, waiting for transfers between devices: 271 us -> none  [the longest x1 140 us: per_device(): lax.all_gather(expand_master.astype(jnp.bfloat16), 'dp', axis=1, tiled=True)]
    dot_general x36 -> x17, matrix products: 228 us -> 137 us  [the longest x7 77 us: nn(): lax.dot_general(a, b, (((1,), (0,)), ((), ())), preferred_element_type=F32)]
    psum x2 -> x0, blocking collectives: 81.8 us -> none  [the longest x1 79.3 us: per_device(): lax.psum((jnp.sum(inward_pre * inward_pre, axis=1), jnp.sum(outward_pre *...]
    all_gather x2 -> x0, blocking collectives: 81.4 us -> none  [the longest x1 43.1 us: per_device(): lax.all_gather(scale_master.astype(jnp.bfloat16), 'dp', axis=1, tiled=True)]
    add x2 -> x0, local copies, waits for them, and re-layouts: 53.6 us -> none  [per_device(): earlier_sum + later_sum]
  transfers between devices with their start and end apart: 15 -> 34, of which waited for: 11 -> 16; matrix products, arithmetic and copies ran while one was open for 11% -> 15% of each run, Pallas kernels for 0% -> 34%
where the time goes in v1:
time: 851 us; the launch traced here: 842 us
  Pallas kernels  533 us (63%)
  matrix products  137 us (16%)
  other arithmetic  56.7 us (7%)
  local copies, waits for them, and re-layouts  53.6 us (6%)
  waiting for transfers between devices  35.1 us (4%)
  starting transfers between devices  24.8 us (3%)
    pallas_call x3, Pallas kernels, sum_products(): pl.pallas_call(functools.partial(sum_kernel, plan, left_of, scale), out_s...  252 us
    pallas_call x2, Pallas kernels, gather_columns(): pl.pallas_call(functools.partial(gather_kernel, plan), out_shape=jax.Shap...  227 us
    dot_general x7, matrix products, nn(): lax.dot_general(a, b, (((1,), (0,)), ((), ())), preferred_element_type=F32)  77 us
    dot_general x9, matrix products, nt(): lax.dot_general(a, b, (((1,), (1,)), ((), ())), preferred_element_type=F32)  57.1 us
    pallas_call x1, Pallas kernels, attend_back(): pl.pallas_call(attend_back_kernel, grid=(count, columns // (2 * HD)), in_...  37 us
    unnamed x178, local copies, waits for them, and re-layouts  30.5 us
    ppermute x24, waiting for transfers between devices, exchange(): return lax.ppermute(array, 'dp', [(i, i ^ bit) for i in range(count)])  27.7 us
    ppermute x24, starting transfers between devices, exchange(): return lax.ppermute(array, 'dp', [(i, i ^ bit) for i in range(count)])  23.4 us
  transfers between devices with their start and end apart: 34, of which 16 were waited for; matrix products, arithmetic and copies ran while one was open for 15% of the time, Pallas kernels for 34%

profile of v1, /device:TPU:0, one launch (start us, length us, event | category | flops | bytes accessed | tf_op | source)
XLA Modules:
  0.0 841.9 jit_solution(5803857626532853239)
XLA Ops:
  5.3 71.4 %gather_columns.2 = bf16[2,2,2,2,80,2816]{5,4,3,2,1,0:T(8,128)(2,1)S(1)} custom-call(bf16[80,2816]{1,0:T(8,128)(2,1)S(1)} %pad_dynamic-update-slice_fusion.block), custom_call_target="tpu_custom_call" | custom-call | tf_op jit(solution)/shard_map/gather_columns/pallas_call | solution.py:163
  88.5 5.7 convolution_multiply_fusion
  102.2 16.4 %attend.1 = bf16[1024,640]{1,0:T(8,128)(2,1)S(1)} custom-call(f32[1024,640]{1,0:T(8,128)S(1)} %get-tuple-element.149.raw_q, f32[1024,640]{1,0:T(8,128)S(1)} %copy-done.4, f32[1024,640]{1,0:T(8,128)S(1)} %copy-done.3, f32[1,640]{1,0:T(1,128)S(1)} %constant_dynamic-slice_fusion.5.gain, f32[2,512,512]{2,1,0:T(8,128)S(1)} %or_select_fusion.bias), custom_call_target="tpu_custom_call" | custom-call | flops 1342177280 | bytes 9175040 | tf_op jit(solution)/shard_map/attend/pallas_call | solution.py:451
  119.8 6.0 fusion.42
  147.7 155.4 %gather_columns.3 = bf16[2,2,2,2,80,7680]{5,4,3,2,1,0:T(8,128)(2,1)S(1)} custom-call(bf16[80,7680]{1,0:T(8,128)(2,1)S(1)} %pad_maximum_fusion.3.block), custom_call_target="tpu_custom_call" | custom-call | tf_op jit(solution)/shard_map/gather_columns/pallas_call | solution.py:163
  303.1 9.9 %fusion.21 = f32[1024,2560]{1,0:T(8,128)} fusion(bf16[1024,1280]{0,1:T(8,128)(2,1)S(1)} %copy-done.23, bf16[1280,7680]{1,0:T(8,128)(2,1)S(1)} %bitcast.80), kind=kOutput, calls=%fused_computation.33 | convolution fusion | flops 6710886400 | bytes 19660800 | tf_op jit(solution)/shard_map/dot_general | solution.py:332
  313.0 27.8 %multiply_convert_fusion.2 = (bf16[1024,2560]{1,0:T(8,128)(2,1)S(1)}, f32[1024,2560]{1,0:T(8,128)}) fusion(f32[2560]{0:T(1024)S(1)} %get-tuple-element.138, f32[1024,2560]{1,0:T(8,128)} %fusion.21, f32[2560]{0:T(1024)S(1)} %get-tuple-element.136, bf16[1024,1280]{0,1:T(8,128)(2,1)S(1)} %copy-done.23, bf16[1280,7680]{1,0:T(8,128)(2,1)} %bitcast.81), kind=kOutput, calls=%fused_computation.10 | convolution fusion | flops 6731857920 | bytes 35409920 | tf_op jit(solution)/shard_map/dot_general | solution.py:332
  340.8 11.0 %fusion.17 = f32[1024,1280]{0,1:T(8,128)S(1)} fusion(bf16[1024,2560]{1,0:T(8,128)(2,1)S(1)} %get-tuple-element.160.right, bf16[1280,7680]{1,0:T(8,128)(2,1)} %bitcast.82), kind=kOutput, calls=%fused_computation.29 | convolution fusion | flops 6710886400 | bytes 17039360 | tf_op jit(solution)/shard_map/dot_general | solution.py:336
  352.3 4.9 collective-permute-done.2
  369.5 23.7 %multiply_reduce_fusion.1 = (f32[2560]{0:T(1024)S(1)}, f32[2560]{0:T(1024)}, f32[1024,2560]{1,0:T(8,128)}, bf16[1024,2560]{1,0:T(8,128)(2,1)}) fusion(f32[1024,2560]{1,0:T(8,128)} %get-tuple-element.161, f32[1024,2560]{1,0:T(8,128)} %fusion.21, f32[2560]{0:T(1024)S(1)} %get-tuple-element.136, f32[2560]{0:T(1024)S(1)} %get-tuple-element.138, ...), kind=kOutput, calls=%fused_computation.6 | convolution fusion | flops 6765931520 | bytes 45926400 | tf_op jit(solution)/shard_map/dot_general | solution.py:332
  393.3 5.4 multiply_convert_fusion
  398.7 9.2 %fusion.19 = f32[1024,1280]{0,1:T(8,128)S(1)} fusion(bf16[1024,2560]{1,0:T(8,128)(2,1)S(1)} %multiply_convert_fusion, bf16[1280,7680]{1,0:T(8,128)(2,1)} %bitcast.84), kind=kOutput, calls=%fused_computation.31 | convolution fusion | flops 6710886400 | bytes 17039360 | tf_op jit(solution)/shard_map/dot_general | solution.py:336
  407.9 6.8 pad_maximum_fusion.right
  414.8 9.1 %add_multiply_fusion.1 = f32[1024,1280]{0,1:T(8,128)S(1)} fusion(f32[1024,1280]{0,1:T(8,128)S(1)} %fusion.19, bf16[1024,2560]{1,0:T(8,128)(2,1)S(1)} %bitcast.98, bf16[1280,7680]{1,0:T(8,128)(2,1)} %bitcast.85), kind=kOutput, calls=%fused_computation.41 | convolution fusion | flops 6713507840 | bytes 22282240 | tf_op jit(solution)/shard_map/dot_general | solution.py:336
  428.4 70.1 %sum_products.5 = f32[80,2560]{1,0:T(8,128)} custom-call(bf16[1,1280,1024]{2,1,0:T(8,128)(2,1)} %bitcast.94, bf16[1024,2560]{1,0:T(8,128)(2,1)} %copy-done.33), custom_call_target="tpu_custom_call" | custom-call | tf_op jit(solution)/shard_map/sum_products/pallas_call | solution.py:262
  502.0 114.4 %sum_products.4 = f32[80,5120]{1,0:T(8,128)} custom-call(bf16[1,1280,1024]{2,1,0:T(8,128)(2,1)} %bitcast.93, bf16[1024,5120]{1,0:T(8,128)(2,1)} %pad_maximum_fusion.right), custom_call_target="tpu_custom_call" | custom-call | tf_op jit(solution)/shard_map/sum_products/pallas_call | solution.py:262
  618.0 4.0 multiply_reduce_fusion.12
  632.8 4.6 copy.76
  647.1 4.1 multiply_reduce_fusion.5
  672.6 37.0 %attend_back.1 = (bf16[1024,640]{1,0:T(8,128)(2,1)S(1)}, bf16[1024,640]{1,0:T(8,128)(2,1)S(1)}, bf16[1024,640]{1,0:T(8,128)(2,1)S(1)}, f32[2,8,640]{2,1,0:T(8,128)S(1)}) custom-call(f32[1024,640]{1,0:T(8,128)S(1)} %copy-done.7, f32[1024,640]{1,0:T(8,128)S(1)} %copy-done.5, f32[1024,640]{1,0:T(8,128)} %get-tuple-element.147.raw_v, ...), custom_call_target="tpu_custom_call" | custom-call | flops 4026531840 | bytes 13107200 | tf_op jit(solution)/shard_map/attend_back/pallas_call | solution.py:470
  718.6 68.0 %sum_products.3 = f32[80,2560]{1,0:T(8,128)} custom-call(bf16[2,1280,1024]{2,1,0:T(8,128)(2,1)} %pad_maximum_fusion.1.left, bf16[1024,2560]{1,0:T(8,128)(2,1)} %slice_dynamic-update-slice_fusion.1.right), custom_call_target="tpu_custom_call" | custom-call | tf_op jit(solution)/shard_map/sum_products/pallas_call | solution.py:262
  787.7 8.9 %multiply_convert_fusion.3 = bf16[1024,1280]{0,1:T(8,128)(2,1)S(1)} fusion(bf16[1280,2816]{1,0:T(8,128)(2,1)} %bitcast.90, bf16[1024,640]{1,0:T(8,128)(2,1)S(1)} %get-tuple-element.30, bf16[1024,640]{1,0:T(8,128)(2,1)S(1)} %get-tuple-element.29, bf16[1024,640]{1,0:T(8,128)(2,1)S(1)} %get-tuple-element.28), kind=kOutput, calls=%fused_computation.40 | convolution fusion | flops 5047582720 | bytes 11468800 | tf_op jit(solution)/shard_map/dot_general | solution.py:336
  828.2 4.1 collective-permute-done.32
  834.4 4.0 collective-permute-done.33
  (373 shorter events, 157.8 us)
Async XLA Ops:
  129.4 5.3 collective-permute-start
  352.1 5.0 collective-permute-start.2
  368.0 261.1 %collective-permute-start.3 = (bf16[512,1280]{0,1:T(8,128)(2,1)}, bf16[512,1280]{0,1:T(8,128)(2,1)}, u32[]{:S(2)}, u32[]{:S(2)}) collective-permute-start(bf16[512,1280]{0,1:T(8,128)(2,1)} %get-tuple-element.163), channel_id=1, source_target_pairs={{0,1},{1,0},{2,3},{3,2},{4,5},{5,4},{6,7},{7,6},{8,9},{9,8},{10,11... | collective-permute-start | bytes 3932168 | tf_op jit(solution)/shard_map/ppermute | solution.py:289
  428.0 219.0 %collective-permute-start.5 = (f32[512,1280]{0,1:T(8,128)}, f32[512,1280]{0,1:T(8,128)}, u32[]{:S(2)}, u32[]{:S(2)}) collective-permute-start(f32[512,1280]{0,1:T(8,128)} %constant_dynamic-slice_fusion.1), channel_id=1, source_target_pairs={{0,1},{1,0},{2,3},{3,2},{4,5},{5,4},{6,7},{7,6},{8,9},{9,8},{10,11... | collective-permute-start | bytes 7864328 | tf_op jit(solution)/shard_map/ppermute | solution.py:289
  501.1 116.8 %collective-permute-start.20 = (f32[2560]{0:T(1024)S(1)}, f32[2560]{0:T(1024)S(1)}, u32[]{:S(2)}, u32[]{:S(2)}) collective-permute-start(f32[2560]{0:T(1024)S(1)} %get-tuple-element.109), channel_id=1, source_target_pairs={{0,4},{2,6},{4,0},{6,2},{8,12},{10,14},{12,8},{14,10},{16,20},{18,... | collective-permute-start | bytes 30728 | tf_op jit(solution)/shard_map/ppermute | solution.py:285
  617.9 5.5 collective-permute-start.21
  622.0 3.9 collective-permute-start.16
  623.4 5.4 collective-permute-start.22
  626.7 10.7 %collective-permute-start.17 = (f32[2,2560]{1,0:T(2,128)S(1)}, f32[2,2560]{1,0:T(2,128)}, u32[]{:S(2)}, u32[]{:S(2)}) collective-permute-start(f32[2,2560]{1,0:T(2,128)S(1)} %add.361), channel_id=1, source_target_pairs={{0,2},{2,0},{4,6},{6,4},{8,10},{10,8},{12,14},{14,12},{16,18},{18,... | collective-permute-start | bytes 61448 | tf_op jit(solution)/shard_map/ppermute | solution.py:285
  628.8 10.1 %collective-permute-start.23 = (f32[2560]{0:T(1024)S(1)}, f32[2560]{0:T(1024)}, u32[]{:S(2)}, u32[]{:S(2)}) collective-permute-start(f32[2560]{0:T(1024)S(1)} %add.373), channel_id=1, source_target_pairs={{0,16},{2,18},{4,20},{6,22},{8,24},{10,26},{12,28},{14,30},{16,0},... | collective-permute-start | bytes 30728 | tf_op jit(solution)/shard_map/ppermute | solution.py:285
  642.0 5.0 collective-permute-start.19
  659.5 9.0 %collective-permute-start.6 = (bf16[512,1280]{0,1:T(8,128)(2,1)S(1)}, bf16[512,1280]{0,1:T(8,128)(2,1)S(1)}, u32[]{:S(2)}, u32[]{:S(2)}) collective-permute-start(bf16[512,1280]{0,1:T(8,128)(2,1)S(1)} %get-tuple-element.125), channel_id=1, source_target_pairs={{0,1},{1,0},{2,3},{3,2},{4,5},{5,4},{6,7},{7,6},{8,9},{9,8},{10,11... | collective-permute-start | bytes 3932168 | tf_op jit(solution)/shard_map/ppermute | solution.py:289
  662.2 4.3 collective-permute-start.27
  666.6 148.1 %collective-permute-start.28 = (f32[80,2]{0,1:T(2,128)S(1)}, f32[80,2]{0,1:T(2,128)S(1)}, u32[]{:S(2)}, u32[]{:S(2)}) collective-permute-start(f32[80,2]{0,1:T(2,128)S(1)} %slice.207), channel_id=1, source_target_pairs={{0,16},{2,18},{4,20},{6,22},{8,24},{10,26},{12,28},{14,30},{16,0},... | collective-permute-start | bytes 1928 | tf_op jit(solution)/shard_map/ppermute | solution.py:285
  797.5 11.3 %collective-permute-start.12 = (f32[640]{0:T(1024)S(1)}, f32[640]{0:T(1024)S(1)}, u32[]{:S(2)}, u32[]{:S(2)}) collective-permute-start(f32[640]{0:T(1024)S(1)} %get-tuple-element.116), channel_id=1, source_target_pairs={{0,4},{2,6},{4,0},{6,2},{8,12},{10,14},{12,8},{14,10},{16,20},{18,... | collective-permute-start | bytes 7688 | tf_op jit(solution)/shard_map/ppermute | solution.py:285
  804.3 34.8 %collective-permute-start.7 = (f32[1024,640]{1,0:T(8,128)S(1)}, f32[1024,640]{1,0:T(8,128)S(1)}, u32[]{:S(2)}, u32[]{:S(2)}) collective-permute-start(f32[1024,640]{1,0:T(8,128)S(1)} %constant_dynamic-slice_fusion), channel_id=1, source_target_pairs={{0,1},{1,0},{2,3},{3,2},{4,5},{5,4},{6,7},{7,6},{8,9},{9,8},{10,11... | collective-permute-start | bytes 7864328 | tf_op jit(solution)/shard_map/ppermute | solution.py:289
  807.0 6.2 collective-permute-start.8
  809.4 9.3 %collective-permute-start.29 = (f32[9,1280]{1,0:T(8,128)S(1)}, f32[9,1280]{1,0:T(8,128)S(1)}, u32[]{:S(2)}, u32[]{:S(2)}) collective-permute-start(f32[9,1280]{1,0:T(8,128)S(1)} %pad_maximum_fusion.5), channel_id=1, source_target_pairs={{0,1},{1,0},{2,3},{3,2},{4,5},{5,4},{6,7},{7,6},{8,9},{9,8},{10,11... | collective-permute-start | bytes 138248 | tf_op jit(solution)/shard_map/ppermute | solution.py:289
  816.0 4.5 collective-permute-start.15
  818.8 4.5 collective-permute-start.30
  820.7 7.5 collective-permute-start.11
  823.3 4.5 collective-permute-start.31
  827.8 4.5 collective-permute-start.32
  832.3 6.1 collective-permute-start.33
  (97 other events, 2607.2 us)

commit v2 on v1

v2 whole, which is shorter than its diff:
```python
import functools

import jax
import jax.numpy as jnp
import numpy as np
from jax import lax
from jax.experimental import pallas as pl
from jax.experimental.pallas import tpu as pltpu
from jax.sharding import PartitionSpec as P

D = 1280
HEADS = 20
HD = 64
FF = 5120
STEP = 10
LONGEST = 256


EPS_NORM = 1e-06
BETA_ONE = 0.9
BETA_TWO = 0.95
ADAM_EPS = 1e-08
RATE_MATRIX = 0.3
RATE_ALPHA = 0.08
RATE_SCALE = 0.25
MASKED = -1e30
F32 = jnp.float32
BF16 = jnp.bfloat16


def row_norm(values):
    factor = lax.rsqrt(jnp.mean(values * values, axis=-1, keepdims=True) + EPS_NORM)
    return (values * factor, factor)


def row_norm_back(upstream, normed, factor):
    return factor * (upstream - normed * jnp.mean(upstream * normed, axis=-1, keepdims=True))


def adam_step(master, first_moment, second_moment, gradient, rate):
    first_new = BETA_ONE * first_moment.astype(F32) + (1.0 - BETA_ONE) * gradient
    second_new = BETA_TWO * second_moment + (1.0 - BETA_TWO) * gradient * gradient
    ratio = (
        first_new
        / (1.0 - BETA_ONE**STEP)
        / (jnp.sqrt(second_new / (1.0 - BETA_TWO**STEP)) + ADAM_EPS)
    )
    return (master - rate * ratio, second_new)


LANES = 128
PLACES = (2, 1, 4, 8)
ROUTES = ((3, 2, 1, 0), (3, 2, 0, 1), (1, 0, 3, 2), (0, 1, 3, 2))
EVERY = 4
LAG = 2
RING = 4


def partner_of(me, bit):
    return me + bit - 2 * bit * ((me // bit) % 2)


def greet(me, core=None):
    barrier = pltpu.get_barrier_semaphore()
    partners = [{"dp": partner_of(me, bit)} for bit in PLACES]
    if core is not None:
        partners.append({"tensor": 1 - core})
    for partner in partners:
        pl.semaphore_signal(
            barrier, inc=1, device_id=partner, device_id_type=pl.DeviceIdType.MESH
        )
    pl.semaphore_wait(barrier, len(partners))


def tile_plan(columns):
    tiles = columns // LANES
    rare = tiles // 10
    often = (tiles - 2 * rare) // 2
    return (
        (0, 2, often, 1),
        (1, 2, often, 1),
        (2 * often, 1, rare, EVERY),
        (2 * often + rare, 1, rare, EVERY),
    )


def for_tiles(step, hop, plan, body):
    for route, (_, _, number, every) in enumerate(plan):
        if number == 0:
            continue
        at = step - hop * LAG
        due = (at >= 0) & (at < number * every)
        if every > 1:
            due = due & (at % every == 0)

        @pl.when(due)
        def _():
            body(route, at // every)


def lanes_of(plan, route, tile):
    first, stride, _, _ = plan[route]
    return pl.ds(pl.multiple_of((first + stride * tile) * LANES, LANES), LANES)


def steps_of(plan, hops):
    return max((number - 1) * every + 1 for _, _, number, every in plan if number) + hops * LAG


def extra_bits(count):
    return [bit for bit in (1 << k for k in range(4, count.bit_length() - 1))]


def exchange(array, bit, count):
    return lax.ppermute(array, "dp", [(i, i ^ bit) for i in range(count)])


def swap_cores(array):
    return lax.ppermute(array, "tensor", [(0, 1), (1, 0)])


def gather_rest(block, count):
    for bit in extra_bits(count)[::-1]:
        block = jnp.concatenate([block, exchange(block, bit, count)], axis=0)
    return block


def scatter_rest(partial, count):
    for bit in extra_bits(count):
        half = partial.shape[0] // 2
        partial = partial[:half] + exchange(partial[half:], bit, count)
    return partial


def butterfly_sum(array, count):
    for bit in list(PLACES) + extra_bits(count):
        array = array + exchange(array, bit, count)
    return array


def scatter_sum(partial, count):
    for bit in PLACES:
        half = partial.shape[0] // 2
        partial = partial[:half] + exchange(partial[half:], bit, count)
    return scatter_rest(partial, count)


def place_row_of(me, count):
    places = list(PLACES) + extra_bits(count)
    width = D // count
    placed = np.arange(D, dtype=np.int32)
    position, offset = placed // width, placed % width
    relative = np.zeros_like(position)
    for axis, bit in enumerate(places):
        relative = relative + ((position >> (len(places) - 1 - axis)) & 1) * bit
    return ((jnp.asarray(relative) ^ me) * width + jnp.asarray(offset))[None]


def place_matrix(place_row):
    natural = lax.broadcasted_iota(jnp.int32, (D, D), 0)
    return (natural == place_row).astype(BF16)


def nn(a, b):
    return lax.dot_general(a, b, (((1,), (0,)), ((), ())), preferred_element_type=F32)


def nt(a, b):
    return lax.dot_general(a, b, (((1,), (1,)), ((), ())), preferred_element_type=F32)


def tn(a, b):
    return lax.dot_general(a, b, (((0,), (0,)), ((), ())), preferred_element_type=F32)


def head_factors(raw, low_lanes):
    squares = raw * raw
    low = jnp.sum(jnp.where(low_lanes, squares, 0.0), axis=-1, keepdims=True)
    high = jnp.sum(jnp.where(low_lanes, 0.0, squares), axis=-1, keepdims=True)
    return jnp.where(low_lanes, lax.rsqrt(low + EPS_NORM), lax.rsqrt(high + EPS_NORM))


def head_sums(values, low_lanes):
    low = jnp.sum(jnp.where(low_lanes, values, 0.0), axis=-1, keepdims=True)
    high = jnp.sum(jnp.where(low_lanes, 0.0, values), axis=-1, keepdims=True)
    return jnp.where(low_lanes, low, high)


Q_TILE = 128


def key_range(tile):
    start = max(0, tile * Q_TILE - LONGEST)
    return start, (tile + 1) * Q_TILE


def attend_pair(query, key, value, gain, bias, mixed):
    length = query.shape[0]
    low_lanes = lax.broadcasted_iota(jnp.int32, (1, 2 * HD), 1) < HD
    query = (gain * (query * head_factors(query, low_lanes))).astype(BF16) * 8
    key = (gain * (key * head_factors(key, low_lanes))).astype(BF16)
    value = value.astype(BF16)
    zero = jnp.zeros_like(query)
    parts = (jnp.where(low_lanes, query, zero), jnp.where(low_lanes, zero, query))
    for tile in range(length // Q_TILE):
        start, end = key_range(tile)
        rows = slice(tile * Q_TILE, (tile + 1) * Q_TILE)
        tile_bias = bias[rows, start:end]
        results = []
        for part in parts:
            expo = jnp.exp(nt(part[rows], key[start:end]) + tile_bias)
            total = jnp.sum(expo, axis=-1, keepdims=True)
            results.append(nn(expo.astype(BF16), value[start:end]) * (1.0 / total))
        mixed[rows, :] = jnp.where(low_lanes, results[0], results[1]).astype(BF16)


def attend_pair_back(
    raw_q, raw_k, raw_v, d_mixed, gains, bias, d_raw_q, d_raw_k, d_raw_v, sum_k, sum_v
):
    length = raw_q.shape[0]
    low_lanes = lax.broadcasted_iota(jnp.int32, (1, 2 * HD), 1) < HD
    key_raw = raw_k[...]
    key_factor = head_factors(key_raw, low_lanes)
    key_unit = key_raw * key_factor
    key = (gains * key_unit).astype(BF16)
    key_eight = key * 8
    value = raw_v[...].astype(BF16)
    sum_k[...] = jnp.zeros_like(sum_k)
    sum_v[...] = jnp.zeros_like(sum_v)
    gain_total = jnp.zeros((1, 2 * HD), F32)

    def back(upstream, unit, factor):
        scaled = gains * upstream
        return (factor * (scaled - unit * head_sums(scaled * unit, low_lanes))).astype(BF16)

    for tile in range(length // Q_TILE):
        start, end = key_range(tile)
        rows = slice(tile * Q_TILE, (tile + 1) * Q_TILE)
        query_raw = raw_q[rows, :]
        query_factor = head_factors(query_raw, low_lanes)
        query_unit = query_raw * query_factor
        query = (gains * query_unit).astype(BF16) * 8
        upstream = d_mixed[rows].astype(F32)
        tile_bias = bias[rows, start:end]
        d_query = []
        for low in (True, False):
            lanes = low_lanes if low else jnp.logical_not(low_lanes)
            own_query = jnp.where(lanes, query, jnp.zeros_like(query))
            expo = jnp.exp(nt(own_query, key[start:end]) + tile_bias)
            inverse = 1.0 / jnp.sum(expo, axis=-1, keepdims=True)
            expo_low = expo.astype(BF16)
            result = nn(expo_low, value[start:end]) * inverse
            own_up = jnp.where(lanes, upstream, 0.0)
            delta = jnp.sum(result * own_up, axis=-1, keepdims=True) * inverse
            own_up = (own_up * inverse).astype(BF16)
            sum_v[start:end, :] += tn(expo_low, own_up)
            d_scores = (expo * (nt(own_up, value[start:end]) - delta)).astype(BF16)
            d_query.append(nn(d_scores, key_eight[start:end]))
            sum_k[start:end, :] += tn(d_scores, own_query)
        d_query = jnp.where(low_lanes, d_query[0], d_query[1])
        gain_total += jnp.sum(d_query * query_unit, axis=0, keepdims=True)
        d_raw_q[rows, :] = back(d_query, query_unit, query_factor)
    d_key = sum_k[...]
    gain_total += jnp.sum(d_key * key_unit, axis=0, keepdims=True)
    d_raw_k[...] = back(d_key, key_unit, key_factor)
    d_raw_v[...] = sum_v[...].astype(BF16)
    return gain_total


def bias_of(segment_ids, pad_mask):
    positions = jnp.arange(segment_ids.shape[1])
    key_code = jnp.where(pad_mask == 0, segment_ids, -1)
    earlier = positions[None, :] <= positions[:, None]
    same = positions[None, :] == positions[:, None]
    allowed = (segment_ids[:, :, None] == key_code[:, None, :]) & earlier[None] | same[None]
    return jnp.where(allowed, 0.0, MASKED).astype(F32)


ARRIVE = 4 * LAG
UNIT_GROUP = 4
FIRST_UNIT_PAIR = 8
RARE_UNITS = 3


def head_tiles():
    return HEADS * HD // 2 // LANES


def unit_tiles():
    return FF // 2 // LANES


def forward_plan():
    groups = unit_tiles() // UNIT_GROUP
    return tile_plan((2 * (FIRST_UNIT_PAIR + 5 * groups) + 2 * (RARE_UNITS + groups)) * LANES)


def pair_tile(unit):
    return 2 * (FIRST_UNIT_PAIR + 5 * (unit // UNIT_GROUP) + unit % UNIT_GROUP)


def shrink_tile_static(unit):
    plan = forward_plan()
    group, place = unit // UNIT_GROUP, unit % UNIT_GROUP
    if place < 2:
        return plan[2][0] + place * plan[2][2] + RARE_UNITS + group
    return 2 * (FIRST_UNIT_PAIR + 5 * group + UNIT_GROUP) + place - 2


def shrink_tile(unit):
    plan = forward_plan()
    group, place = unit // UNIT_GROUP, unit % UNIT_GROUP
    rare = plan[2][0] + place * plan[2][2] + RARE_UNITS + group
    often = 2 * (FIRST_UNIT_PAIR + 5 * group + UNIT_GROUP) + place - 2
    return jnp.where(place < 2, rare, often)


def forward_columns(inward, outward, expand, shrink, small):
    rows = small.shape[0]
    groups = unit_tiles() // UNIT_GROUP
    heads = 3 * head_tiles() - 1
    units = jnp.stack([expand[0], expand[1]], axis=1).reshape(
        rows, 2, groups, UNIT_GROUP, LANES
    )
    units = units.transpose(0, 2, 3, 1, 4).reshape(rows, groups, 2 * UNIT_GROUP, LANES)
    shrink = shrink.reshape(rows, groups, UNIT_GROUP, LANES)
    units = jnp.concatenate([units, shrink[:, :, 2:]], axis=2).reshape(rows, -1)
    return jnp.concatenate(
        [
            inward[:, : heads * LANES],
            outward[:, 2 * LANES : 4 * LANES],
            units,
            inward[:, heads * LANES :],
            outward[:, :LANES],
            outward[:, 4 * LANES :],
            shrink[:, :, 0].reshape(rows, -1),
            small,
            outward[:, LANES : 2 * LANES],
            jnp.zeros((rows, LANES), BF16),
            shrink[:, :, 1].reshape(rows, -1),
        ],
        axis=1,
    )


def forward_kernel(
    plan,
    block,
    tokens,
    place_row,
    bias,
    out,
    tokens_out,
    raw_out,
    mixed_out,
    h_attn_out,
    first_out,
    first_low_out,
    tokens_turned_out,
    first_turned_out,
    proj_out,
    hidden_out,
    factors,
    alphas,
    scales,
    gains,
    shrunk,
    place,
    tokens_in,
    raw,
    stage_pair,
    stage_one,
    stage_outward,
    mixed,
    branch_in,
    h_attn,
    first,
    first_low,
    stage_proj,
    stage_hidden,
    own_sem,
    send_sem,
    recv_sem,
    pair_sem,
    one_sem,
    outward_sem,
    proj_sem,
    hidden_sem,
    result_sem,
    core_send,
    core_recv,
):
    me = lax.axis_index("dp")
    core = lax.axis_index("tensor")
    inv_root = D ** (-0.5)
    rows = tokens.shape[0]
    own_rows = rows // 2
    own_at = pl.multiple_of(core * own_rows, own_rows)
    other_at = pl.multiple_of((1 - core) * own_rows, own_rows)
    heads = head_tiles()
    units = unit_tiles()
    attend_at = 3 * heads // 2 + ARRIVE + 1
    pairs_each = 2
    sequences = bias.shape[0]
    length = bias.shape[1]
    head_pairs = sequences * heads
    branch_at = attend_at + -(-head_pairs // pairs_each)
    units_at = branch_at + 2

    own = pltpu.make_async_copy(block, out.at[0, 0, 0, 0], own_sem)
    own.start()
    greet(me, core)

    def piece(hop, route, tile):
        lanes = lanes_of(plan, route, tile)
        crossed, axis = ROUTES[route][:hop], ROUTES[route][hop]
        source = [slice(None) if k in crossed else 0 for k in range(4)]
        target = [1 if k == axis else source[k] for k in range(4)]
        if hop == 0:
            source_ref = block.at[:, lanes]
        else:
            source_ref = out.at[(*source, slice(None), lanes)]
        return pltpu.make_async_remote_copy(
            src_ref=source_ref,
            dst_ref=out.at[(*target, slice(None), lanes)],
            send_sem=send_sem.at[hop, route, tile % RING],
            recv_sem=recv_sem.at[hop, route, tile],
            device_id={"dp": partner_of(me, PLACES[axis])},
            device_id_type=pl.DeviceIdType.MESH,
        )

    def forward_hop(hop, route, tile):
        if hop > 0:
            piece(hop - 1, route, tile).wait_recv()
        if hop < 4:

            @pl.when(tile >= RING)
            def _():
                piece(hop, route, tile - RING).wait_send()

            piece(hop, route, tile).start()

    def staged(tile, width, target, sem):
        lanes = pl.ds(pl.multiple_of(tile * LANES, LANES), width * LANES)
        return pltpu.make_async_copy(out.at[:, :, :, :, :, lanes], target, sem)

    def pair_copy(tile, slot):
        return staged(tile, 2, stage_pair.at[slot], pair_sem.at[slot])

    def one_copy(tile, slot):
        return staged(tile, 1, stage_one.at[slot], one_sem.at[slot])

    rare = plan[2][0]
    rarer = plan[3][0]

    def outward_copies():
        return [
            staged(tile, width, stage_outward.at[:, :, :, :, :, pl.ds(at * LANES, width * LANES)], outward_sem.at[k])
            for k, (tile, width, at) in enumerate(
                ((rare + 1, 1, 0), (rarer + 1, 1, 1), (3 * heads - 1, 2, 2), (rare + 2, 1, 4))
            )
        ]

    def core_copy(source, target, which):
        return pltpu.make_async_remote_copy(
            src_ref=source,
            dst_ref=target,
            send_sem=core_send.at[which],
            recv_sem=core_recv.at[which],
            device_id={"tensor": 1 - core},
            device_id_type=pl.DeviceIdType.MESH,
        )

    def branch_copy():
        return core_copy(shrunk.at[pl.ds(0, own_rows)], branch_in, 0)

    def first_copy():
        return core_copy(
            first_low.at[pl.ds(own_at, own_rows)], first_low.at[pl.ds(own_at, own_rows)], 1
        )

    result_pairs = (
        (tokens_in, tokens_out),
        (raw, raw_out),
        (mixed, mixed_out),
        (h_attn, h_attn_out),
        (first, first_out),
        (first_low, first_low_out),
        (place.at[:, pl.ds(0, rows)], tokens_turned_out),
        (place.at[:, pl.ds(0, rows)], first_turned_out),
    )

    def result(k):
        return pltpu.make_async_copy(*result_pairs[k], result_sem.at[k])

    def chunks(total, size, body):
        def one(k, _):
            body(pl.ds(pl.multiple_of(k * size, size), size))
            return 0

        lax.fori_loop(0, total // size, one, 0)

    def in_order():
        natural = place_row[...]

        def fill(at):
            here = lax.broadcasted_iota(jnp.int32, (LANES, D), 0) + at.start
            place[at, :] = jnp.where(here == natural, 1.0, 0.0).astype(BF16)

        chunks(D, LANES, fill)

        def move(at):
            tokens_in[at, :] = nn(tokens[at, :], place[...]).astype(BF16)

        chunks(rows, 256, move)
        result(0).start()

    def turn(source):
        def some(at):
            place[:, at] = source[at, :].astype(F32).T.astype(BF16)

        chunks(rows, LANES, some)

    def project(weights, lanes):
        def some(at):
            raw[at, lanes] = nn(tokens_in[at, :], weights) * inv_root

        chunks(rows, 256, some)

    def small_vectors():
        small = stage_one[1].reshape(D, LANES).astype(F32).T
        alphas[...] = small[: alphas.shape[0]]
        scales[...] = nt(small.astype(BF16), place[...])[: scales.shape[0]]
        each = units * LANES // D
        for row in range(2):
            for k in range(each):
                at = 3 + row * 2 * each + k
                gains[row : row + 1, k * D : (k + 1) * D] = jnp.where(
                    core == 0, scales[at : at + 1, :], scales[at + each : at + each + 1, :]
                )

    def attend_one(number):
        sequence, head = number // heads, number % heads
        at = pl.ds(pl.multiple_of(sequence * length, length), length)
        lanes = [
            pl.ds(pl.multiple_of((k * heads + head) * LANES, LANES), LANES) for k in range(3)
        ]
        gain_lanes = pl.ds(pl.multiple_of((core * heads + head) * LANES, LANES), LANES)
        attend_pair(
            raw[at, lanes[0]],
            raw[at, lanes[1]],
            raw[at, lanes[2]],
            scales[2:3, gain_lanes],
            bias.at[sequence],
            mixed.at[at, lanes[0]],
        )

    def branch():
        weights = stage_outward[...].reshape(D, heads * LANES)
        for target, source in ((0, other_at), (own_rows, own_at)):
            for k in range(2):
                half = own_rows // 2
                at = pl.ds(pl.multiple_of(source + k * half, half), half)
                shrunk[pl.ds(target + k * half, half), :] = nt(mixed[at, :], weights)
            if target == 0:
                branch_copy().start()

    def norms():
        branch_copy().wait()
        alpha = alphas[0:1, :]

        def some(at):
            total = shrunk[pl.ds(pl.multiple_of(own_rows + at.start, 64), 64), :] + branch_in[at, :]
            normed, factor = row_norm(total)
            here = pl.ds(pl.multiple_of(own_at + at.start, 64), 64)
            inputs = tokens_in[here, :].astype(F32)
            result, result_factor = row_norm(inputs + alpha * (normed - inputs))
            h_attn[at, :] = normed
            first[at, :] = result
            first_low[here, :] = result.astype(BF16)
            factors[at, :LANES] = jnp.broadcast_to(factor, (64, LANES))
            factors[at, LANES:] = jnp.broadcast_to(result_factor, (64, LANES))

        chunks(own_rows, 64, some)
        first_copy().start()
        for k in (3, 4):
            result(k).start()

    def gain_of(unit, row):
        return gains[row : row + 1, pl.ds(pl.multiple_of(unit * LANES, LANES), LANES)]

    def proj_copy(unit):
        lanes = pl.ds(pl.multiple_of(unit * 2 * LANES, 2 * LANES), 2 * LANES)
        slot = unit % 2
        return pltpu.make_async_copy(stage_proj.at[slot], proj_out.at[:, lanes], proj_sem.at[slot])

    def hidden_copy(unit):
        lanes = pl.ds(pl.multiple_of(unit * LANES, LANES), LANES)
        slot = unit % 2
        return pltpu.make_async_copy(
            stage_hidden.at[slot], hidden_out.at[:, lanes], hidden_sem.at[slot]
        )

    def fetch_unit(unit):
        pair_copy(pair_tile(unit), unit % 2).start()
        one_copy(shrink_tile(unit), unit % 2).start()

    def one_unit(unit):
        slot = unit % 2

        @pl.when(unit == 0)
        def _():
            first_copy().wait()
            result(5).start()
            shrunk[...] = jnp.zeros_like(shrunk)

        @pl.when(unit >= 2)
        def _():
            proj_copy(unit - 2).wait()
            hidden_copy(unit - 2).wait()

        pair_copy(0, slot).wait()
        one_copy(0, slot).wait()
        weights = stage_pair[slot].reshape(D, 2 * LANES)
        down = stage_one[slot].reshape(D, LANES)
        gain_up = gain_of(unit, 0)
        gain_gate = gain_of(unit, 1)

        def some(at):
            proj = nn(first_low[at, :], weights) * inv_root
            stage_proj[slot, at, :] = proj
            gate = gain_gate * proj[:, LANES:]
            hidden = (gain_up * proj[:, :LANES] * (gate * jax.nn.sigmoid(gate))).astype(BF16)
            stage_hidden[slot, at, :] = hidden
            shrunk[at, :] += nt(hidden, down)

        chunks(rows, 256, some)
        proj_copy(unit).start()
        hidden_copy(unit).start()

    def step(index, _):
        for hop in range(5):
            for_tiles(index, hop, plan, functools.partial(forward_hop, hop))

        @pl.when(index == 0)
        def _():
            in_order()

        @pl.when(index == LAG - 1)
        def _():
            own.wait()

        pair = index - ARRIVE

        @pl.when((pair >= 0) & (pair < 3 * heads // 2))
        def _():
            pair_copy(2 * pair, pair % 2).start()

        @pl.when(pair == 0)
        def _():
            one_copy(rare, 0).start()
            one_copy(rarer, 1).start()

        @pl.when((pair >= 1) & (pair <= 3 * heads // 2))
        def _():
            done = pair - 1
            pair_copy(0, done % 2).wait()
            lanes = pl.ds(pl.multiple_of(done * 2 * LANES, 2 * LANES), 2 * LANES)
            project(stage_pair[done % 2].reshape(D, 2 * LANES), lanes)

        @pl.when(pair == 1)
        def _():
            one_copy(0, 0).wait()
            one_copy(0, 1).wait()
            project(stage_one[0].reshape(D, LANES), pl.ds((3 * heads - 1) * LANES, LANES))
            small_vectors()

        @pl.when(pair == 2)
        def _():
            turn(tokens_in)
            result(6).start()

        @pl.when(index == units_at + 1)
        def _():
            result(6).wait()
            turn(first_low)
            result(7).start()

        @pl.when(index == attend_at)
        def _():
            result(1).start()
            for copy in outward_copies():
                copy.start()

        @pl.when((index >= attend_at) & (index < branch_at))
        def _():
            for k in range(pairs_each):
                attend_one((index - attend_at) * pairs_each + k)

        @pl.when(index == branch_at)
        def _():
            result(2).start()
            for copy in outward_copies():
                copy.wait()
            branch()

        @pl.when(index == branch_at + 1)
        def _():
            norms()

        unit = index - units_at

        @pl.when((unit >= -1) & (unit < units - 1))
        def _():
            fetch_unit(unit + 1)

        @pl.when((unit >= 0) & (unit < units))
        def _():
            one_unit(unit)

        return 0

    lax.fori_loop(0, max(steps_of(plan, 4), units_at + units), step, 0)
    for unit in (units - 2, units - 1):
        proj_copy(unit).wait()
        hidden_copy(unit).wait()
    for k in range(len(result_pairs)):
        if k != 6:
            result(k).wait()
    for route, (_, _, number, _) in enumerate(plan):
        for tile in range(max(0, number - RING), number):
            for hop in range(4):
                piece(hop, route, tile).wait_send()


def forward_pass(block, tokens, place_row, bias, collective_id):
    plan = forward_plan()
    rows, columns = block.shape
    count = tokens.shape[0]
    own = count // 2
    heads = head_tiles() * LANES
    units = unit_tiles() * LANES
    most = max(number for _, _, number, _ in plan)
    place = (2, 2, 2, 2, rows)
    hbm = pl.BlockSpec(memory_space=pl.ANY)
    vmem = pl.BlockSpec(memory_space=pltpu.VMEM)
    dma = pltpu.SemaphoreType.DMA
    return pl.pallas_call(
        functools.partial(forward_kernel, plan),
        out_shape=[
            jax.ShapeDtypeStruct((*place, columns), BF16),
            jax.ShapeDtypeStruct((count, D), BF16),
            jax.ShapeDtypeStruct((count, 3 * heads), F32),
            jax.ShapeDtypeStruct((count, heads), BF16),
            jax.ShapeDtypeStruct((own, D), F32),
            jax.ShapeDtypeStruct((own, D), F32),
            jax.ShapeDtypeStruct((count, D), BF16),
            jax.ShapeDtypeStruct((D, count), BF16),
            jax.ShapeDtypeStruct((D, count), BF16),
            jax.ShapeDtypeStruct((count, 2 * units), F32),
            jax.ShapeDtypeStruct((count, units), BF16),
            jax.ShapeDtypeStruct((own, 2 * LANES), F32),
            jax.ShapeDtypeStruct((8, D), F32),
            jax.ShapeDtypeStruct((16, D), F32),
            jax.ShapeDtypeStruct((8, units), F32),
            jax.ShapeDtypeStruct((count, D), F32),
        ],
        in_specs=[vmem] * 4,
        out_specs=[hbm] * 11 + [vmem] * 5,
        scratch_shapes=[
            pltpu.VMEM((D, D), BF16),
            pltpu.VMEM((count, D), BF16),
            pltpu.VMEM((count, 3 * heads), F32),
            pltpu.VMEM((2, *place, 2 * LANES), BF16),
            pltpu.VMEM((2, *place, LANES), BF16),
            pltpu.VMEM((*place, heads), BF16),
            pltpu.VMEM((count, heads), BF16),
            pltpu.VMEM((own, D), F32),
            pltpu.VMEM((own, D), F32),
            pltpu.VMEM((own, D), F32),
            pltpu.VMEM((count, D), BF16),
            pltpu.VMEM((2, count, 2 * LANES), F32),
            pltpu.VMEM((2, count, LANES), BF16),
            dma,
            dma((4, 4, RING)),
            dma((4, 4, most)),
            dma((2,)),
            dma((2,)),
            dma((4,)),
            dma((2,)),
            dma((2,)),
            dma((8,)),
            dma((2,)),
            dma((2,)),
        ],
        compiler_params=pltpu.CompilerParams(
            collective_id=collective_id, has_side_effects=True, vmem_limit_bytes=60 << 20
        ),
        name="forward_pass",
    )(block, tokens, place_row, bias)


SLOTS = 2 * RING + 4


def backward_plan():
    return tile_plan((4 * head_tiles() + 3 * unit_tiles()) * LANES)


def slot_of(route, tile):
    if route < 2:
        return route * RING + tile % RING
    return 2 * RING + (route - 2) * 2 + tile % 2


def ring_of(route):
    return RING if route < 2 else 2


def backward_kernel(
    plan,
    copies,
    d_shrunk,
    d_shrunk_turned,
    first_turned,
    tokens_turned,
    hidden,
    proj,
    raw,
    mixed,
    d_two,
    h_attn,
    first,
    tokens_in,
    factors,
    alphas,
    scales,
    gains,
    bias,
    d_raw_out,
    d_one_out,
    grads,
    alpha_grad,
    unit_grad,
    query_grad,
    work,
    arrived,
    lefts,
    d_low,
    d_proj,
    first_part,
    core_in,
    stage_hidden,
    stage_rows,
    wide,
    outward,
    right,
    sum_k,
    sum_v,
    send_sem,
    recv_sem,
    load_sem,
    unit_sem,
    raw_sem,
    result_sem,
    core_send,
    core_recv,
):
    me = lax.axis_index("dp")
    core = lax.axis_index("tensor")
    inv_root = D ** (-0.5)
    rows = tokens_in.shape[0]
    own_rows = rows // 2
    own_at = pl.multiple_of(core * own_rows, own_rows)
    other_at = pl.multiple_of((1 - core) * own_rows, own_rows)
    heads = head_tiles()
    units = unit_tiles()
    block = D // 16
    unit_steps = units // 2
    shrink_steps = unit_steps - 1
    late_units = units // 4
    expand_steps = units - late_units
    attention_at = shrink_steps + expand_steps
    rare_units = 1 + late_units
    exchange_at = unit_steps
    attend_at = exchange_at + 3
    sequences = bias.shape[0]
    length = bias.shape[1]
    head_pairs = sequences * heads

    greet(me, core)

    def copy(source, target, sem):
        return pltpu.make_async_copy(source, target, sem)

    def chunks(total, size, body):
        def one(k, _):
            body(pl.ds(pl.multiple_of(k * size, size), size))
            return 0

        lax.fori_loop(0, total // size, one, 0)


    def piece(hop, route, tile):
        axis = ROUTES[route][3 - hop]
        slot = slot_of(route, tile)
        return pltpu.make_async_remote_copy(
            src_ref=work[hop].at[slot, 1],
            dst_ref=arrived[hop].at[slot],
            send_sem=send_sem.at[hop, slot],
            recv_sem=recv_sem.at[hop, slot],
            device_id={"dp": partner_of(me, PLACES[axis])},
            device_id_type=pl.DeviceIdType.MESH,
        )

    def free(hop, route, tile):
        @pl.when(tile >= ring_of(route))
        def _():
            piece(hop, route, tile - ring_of(route)).wait_send()

    def add(hop, route, tile):
        piece(hop - 1, route, tile).wait_recv()
        slot = slot_of(route, tile)
        total = work[hop - 1][slot, 0].astype(F32) + arrived[hop - 1][slot].astype(F32)
        if hop == 4:
            grads[:, lanes_of(plan, route, tile)] = total
            return
        half = total.shape[0] // 2
        free(hop, route, tile)
        work[hop][slot, 0] = total[:half].astype(BF16)
        work[hop][slot, 1] = total[half:].astype(BF16)
        piece(hop, route, tile).start()

    def keep_quarter(route, slot, quarter, part):
        axes = ROUTES[route][::-1]
        if route < 2:
            bits = [quarter >> 1, quarter & 1]
            at = bits[axes[1]] * 4 * block
            work[0][slot, bits[axes[0]], at : at + 4 * block, :] = part
            return
        for low in range(4):
            bits = [quarter >> 1, quarter & 1, low >> 1, low & 1]
            index = bits[axes[1]] * 4 + bits[axes[2]] * 2 + bits[axes[3]]
            work[0][slot, bits[axes[0]], index * block : (index + 1) * block, :] = part[
                low * block : (low + 1) * block
            ]

    def quarter_rows(quarter):
        return slice(quarter * 4 * block, (quarter + 1) * 4 * block)

    def often_product(tile):
        for route in (0, 1):
            free(0, route, tile)
        is_shrink = tile < shrink_steps
        is_expand = (tile >= shrink_steps) & (tile < attention_at)
        late = tile - attention_at
        is_outward = (late >= 0) & (late < 2)

        @pl.when(is_shrink)
        def _():
            right[0] = stage_hidden[tile % 2]

        @pl.when(is_expand)
        def _():
            unit = tile - shrink_steps + late_units
            right[0] = d_proj[:, pl.ds(pl.multiple_of(unit * 2 * LANES, 2 * LANES), 2 * LANES)]

        @pl.when(late >= 0)
        def _():
            first_tile = jnp.where(late < 2, 2 * late, 2 * late + 1)
            right[0] = wide[:rows, pl.ds(pl.multiple_of(first_tile * LANES, LANES), 2 * LANES)]

        which = jnp.where(is_expand | is_outward, 1, 0)
        scale = jnp.where(is_shrink | is_outward, 1.0, inv_root)
        for quarter in range(4):
            part = (nn(lefts[which, quarter_rows(quarter), :], right[0]) * scale).astype(BF16)
            for route in (0, 1):
                keep_quarter(
                    route, slot_of(route, tile), quarter, part[:, route * LANES : (route + 1) * LANES]
                )
        for route in (0, 1):
            piece(0, route, tile).start()

    def rare_product(tile):
        late = tile - rare_units

        @pl.when(tile == 0)
        def _():
            right[1] = stage_hidden[2]

        @pl.when((tile > 0) & (late < 0))
        def _():
            lanes = pl.ds(pl.multiple_of((tile - 1) * 2 * LANES, 2 * LANES), 2 * LANES)
            right[1] = d_proj[:, lanes]

        @pl.when(late == 0)
        def _():
            right[1, :, :LANES] = wide[:rows, (heads - 1) * LANES : heads * LANES]
            right[1, :, LANES:] = wide[:rows, (heads + 12) * LANES : (heads + 13) * LANES]

        @pl.when(late == 1)
        def _():
            right[1] = wide[:rows, (heads + 13) * LANES : (heads + 15) * LANES]

        for route in (2, 3):
            free(0, route, tile)
            of_units = (tile > 0) & (late < 0)
            of_outward = (late == 0) if route == 2 else (late < -rare_units)
            which = jnp.where(of_units | of_outward, 1, 0)
            scale = jnp.where((tile == 0) | of_outward, 1.0, inv_root)
            at = (route - 2) * LANES
            for quarter in range(4):
                part = nn(lefts[which, quarter_rows(quarter), :], right[1, :, at : at + LANES])
                keep_quarter(route, slot_of(route, tile), quarter, (part * scale).astype(BF16))
            piece(0, route, tile).start()


    def unit_copies(pair):
        slot = pair % 2
        unit = 2 * pair
        at = pl.multiple_of(slot * 6 * LANES, 2 * LANES)
        result = [
            (
                copies.at[:, pl.ds(pl.multiple_of(pair_tile(unit) * LANES, LANES), 4 * LANES)],
                wide.at[:, pl.ds(at, 4 * LANES)],
            )
        ]
        for k in range(2):
            tile = shrink_tile(unit + k)
            result.append(
                (
                    copies.at[:, pl.ds(pl.multiple_of(tile * LANES, LANES), LANES)],
                    wide.at[:, pl.ds(pl.multiple_of(at + (4 + k) * LANES, LANES), LANES)],
                )
            )
        lanes = pl.ds(pl.multiple_of(pair * 4 * LANES, 4 * LANES), 4 * LANES)
        for k in range(2):
            result.append(
                (
                    proj.at[pl.ds(k * own_rows, own_rows), lanes],
                    stage_rows.at[slot, :, pl.ds(k * 4 * LANES, 4 * LANES)],
                )
            )
        return [copy(source, target, unit_sem.at[k, slot]) for k, (source, target) in enumerate(result)]

    def hidden_copy(tile):
        lanes = pl.ds(pl.multiple_of((2 * tile + 2) * LANES, 2 * LANES), 2 * LANES)
        return copy(hidden.at[:, lanes], stage_hidden.at[tile % 2], unit_sem.at[5, tile % 2])

    def unit_pair(pair):
        slot = pair % 2
        for part in unit_copies(pair):
            part.wait()
        at = pl.multiple_of(slot * 6 * LANES, 2 * LANES)
        expand = wide[:, pl.ds(at, 4 * LANES)]
        down = wide[:, pl.ds(pl.multiple_of(at + 4 * LANES, 2 * LANES), 2 * LANES)]

        def some(row_at, row_from, proj_lanes):
            d_hidden = nn(d_low[row_at, :], down)
            for k in range(2):
                lanes = pl.ds(pl.multiple_of((2 * pair + k) * LANES, LANES), LANES)
                gain_up, gain_gate = gains[0:1, lanes], gains[1:2, lanes]
                start = proj_lanes + 2 * k * LANES
                proj_up = stage_rows[slot, row_from, start : start + LANES]
                proj_gate = stage_rows[slot, row_from, start + LANES : start + 2 * LANES]
                upstream = d_hidden[:, k * LANES : (k + 1) * LANES]
                gate = gain_gate * proj_gate
                sigmoid = jax.nn.sigmoid(gate)
                d_up = upstream * (gate * sigmoid)
                d_gate = upstream * (gain_up * proj_up) * sigmoid * (1.0 + gate * (1.0 - sigmoid))
                unit_grad[0:1, lanes] += jnp.sum(d_up * proj_up, axis=0, keepdims=True)
                unit_grad[1:2, lanes] += jnp.sum(d_gate * proj_gate, axis=0, keepdims=True)
                at = pl.multiple_of((2 * pair + k) * 2 * LANES, 2 * LANES)
                d_proj[row_at, pl.ds(at, LANES)] = (d_up * gain_up).astype(BF16)
                d_proj[row_at, pl.ds(pl.multiple_of(at + LANES, LANES), LANES)] = (
                    d_gate * gain_gate
                ).astype(BF16)
            lanes = pl.ds(pl.multiple_of(pair * 4 * LANES, 4 * LANES), 4 * LANES)
            first_part[row_at, :] += nt(d_proj[row_at, lanes], expand)

        size = own_rows // 2
        for half in range(2):

            def one(k, _, half=half):
                row_from = pl.multiple_of(k * size, size)
                row_at = pl.multiple_of(half * own_rows + row_from, size)
                some(pl.ds(row_at, size), pl.ds(row_from, size), half * 4 * LANES)
                return 0

            lax.fori_loop(0, 2, one, 0)


    def core_copy(source, target, which):
        return pltpu.make_async_remote_copy(
            src_ref=source,
            dst_ref=target,
            send_sem=core_send.at[which],
            recv_sem=core_recv.at[which],
            device_id={"tensor": 1 - core},
            device_id_type=pl.DeviceIdType.MESH,
        )

    def part_copy():
        return core_copy(first_part.at[pl.ds(other_at, own_rows)], core_in, 0)

    def branch_copy():
        own = d_low.at[pl.ds(own_at, own_rows)]
        return core_copy(own, own, 1)

    tokens_place = wide.at[pl.ds(0, own_rows), pl.ds(D, D)]
    rare, rarer = forward_plan()[2][0], forward_plan()[3][0]
    outward_tiles = ((rare + 1, 1, 0), (rarer + 1, 1, 1), (3 * heads - 1, 2, 2), (rare + 2, 1, 4))

    def load(k):
        if k == 0:
            return copy(d_two, stage_rows.at[0], load_sem.at[0])
        if k == 1:
            return copy(h_attn, stage_rows.at[1], load_sem.at[1])
        if k == 2:
            return copy(tokens_in.at[pl.ds(own_at, own_rows)], tokens_place, load_sem.at[2])
        if k == 3:
            return copy(
                mixed, wide.at[pl.ds(0, rows), pl.ds(0, heads * LANES)], load_sem.at[3]
            )
        if k == 4:
            return copy(first, first_part.at[pl.ds(other_at, own_rows)], load_sem.at[4])
        if k == 5:
            return copy(d_shrunk, d_low, load_sem.at[5])
        if k == 6:
            return copy(d_shrunk_turned, lefts.at[0], load_sem.at[6])
        if k == 7:
            return copy(first_turned, lefts.at[1], load_sem.at[7])
        if k == 8:
            return copy(tokens_turned, lefts.at[0], load_sem.at[8])
        if k == 9:
            return copy(hidden.at[:, pl.ds(0, 2 * LANES)], stage_hidden.at[2], load_sem.at[9])
        tile, width, at = outward_tiles[k - 10]
        return copy(
            copies.at[:, pl.ds(tile * LANES, width * LANES)],
            outward.at[:, pl.ds(at * LANES, width * LANES)],
            load_sem.at[k],
        )

    def branch_gradient():
        part_copy().wait_send()
        load(4).start()
        part_copy().wait_recv()
        for k in (0, 1, 2, 4):
            load(k).wait()
        alpha_attn, alpha_mlp = alphas[0:1, :], alphas[1:2, :]

        def some(at):
            here = pl.ds(pl.multiple_of(own_at + at.start, 64), 64)
            there = pl.ds(pl.multiple_of(other_at + at.start, 64), 64)
            part = (first_part[here, :] + core_in[at, :]) * inv_root
            d_first = (1.0 - alpha_mlp) * stage_rows[0, at, :] + part
            normed = stage_rows[1, at, :]
            d_one = row_norm_back(
                d_first, first_part[there, :], factors[at, LANES : LANES + 1]
            )
            inputs = wide[at, D : 2 * D].astype(F32)
            alpha_grad[0:1, :] += jnp.sum(d_one * (normed - inputs), axis=0, keepdims=True)
            stage_rows[0, at, :] = d_one
            d_low[here, :] = row_norm_back(alpha_attn * d_one, normed, factors[at, 0:1]).astype(
                BF16
            )

        chunks(own_rows, 64, some)
        branch_copy().start()
        copy(stage_rows.at[0], d_one_out, result_sem.at[0]).start()


    def raw_copies(number):
        sequence, head = number // heads, number % heads
        at = pl.ds(pl.multiple_of(sequence * length, length), length)
        slot = number % 2
        target_rows = pl.ds(pl.multiple_of(slot * own_rows, own_rows), length)
        return [
            copy(
                raw.at[at, pl.ds(pl.multiple_of((k * heads + head) * LANES, LANES), LANES)],
                first_part.at[target_rows, pl.ds(k * LANES, LANES)],
                raw_sem.at[k, slot],
            )
            for k in range(3)
        ]

    def attend_one(number):
        sequence, head = number // heads, number % heads
        for part in raw_copies(number):
            part.wait()
        at = pl.ds(pl.multiple_of(sequence * length, length), length)
        source_rows = pl.ds(pl.multiple_of((number % 2) * own_rows, own_rows), length)
        head_lanes = pl.ds(pl.multiple_of(head * LANES, LANES), LANES)
        gain_lanes = pl.ds(pl.multiple_of((core * heads + head) * LANES, LANES), LANES)
        d_mixed = nn(d_low[at, :], outward[:, head_lanes]).astype(BF16)
        targets = [
            wide.at[at, pl.ds(pl.multiple_of(((k + 1) * heads + head) * LANES, LANES), LANES)]
            for k in range(3)
        ]
        total = attend_pair_back(
            *[first_part.at[source_rows, pl.ds(k * LANES, LANES)] for k in range(3)],
            d_mixed,
            scales[2:3, gain_lanes],
            bias.at[sequence],
            *targets,
            sum_k,
            sum_v,
        )
        query_grad[0:1, head_lanes] += total

    def d_raw_copy():
        return copy(
            wide.at[pl.ds(0, rows), pl.ds(heads * LANES, 3 * heads * LANES)],
            d_raw_out,
            result_sem.at[1],
        )


    for k in (5, 6, 9, 7):
        load(k).start()
    for part in unit_copies(0):
        part.start()
    hidden_copy(0).start()
    alpha_grad[...] = jnp.zeros_like(alpha_grad)
    unit_grad[...] = jnp.zeros_like(unit_grad)
    query_grad[...] = jnp.zeros_like(query_grad)
    first_part[...] = jnp.zeros_like(first_part)
    for k in (5, 6, 9, 7):
        load(k).wait()

    def step(index, _):
        for hop in range(4, 0, -1):
            for_tiles(index, hop, plan, functools.partial(add, hop))

        @pl.when(index < shrink_steps)
        def _():
            hidden_copy(index).wait()

        @pl.when(index == attention_at)
        def _():
            load(8).wait()
            chunks(rows, LANES, turn)

        @pl.when(index < plan[0][2])
        def _():
            often_product(index)

        @pl.when((index % EVERY == 0) & (index < plan[2][2] * EVERY))
        def _():
            rare_product(index // EVERY)

        @pl.when(index + 1 < shrink_steps)
        def _():
            hidden_copy(index + 1).start()

        @pl.when(index + 1 < unit_steps)
        def _():
            for part in unit_copies(index + 1):
                part.start()

        @pl.when(index < unit_steps)
        def _():
            unit_pair(index)

        @pl.when(index == exchange_at)
        def _():
            part_copy().start()
            for k in (0, 1, 2, 3, 8, 10, 11, 12, 13):
                load(k).start()

        @pl.when(index == exchange_at + 1)
        def _():
            branch_gradient()

        @pl.when(index == exchange_at + 2)
        def _():
            branch_copy().wait()
            for k in (3, 10, 11, 12, 13):
                load(k).wait()

        number = index - attend_at

        @pl.when((number >= -1) & (number < head_pairs - 1))
        def _():
            for part in raw_copies(number + 1):
                part.start()

        @pl.when((number >= 0) & (number < head_pairs))
        def _():
            attend_one(number)

        @pl.when(number == head_pairs)
        def _():
            d_raw_copy().start()

        return 0

    def turn(at):
        lefts[1, :, at] = d_low[at, :].astype(F32).T.astype(BF16)

    lax.fori_loop(0, steps_of(plan, 4), step, 0)
    copy(stage_rows.at[0], d_one_out, result_sem.at[0]).wait()
    d_raw_copy().wait()
    for route, (_, _, number, _) in enumerate(plan):
        for tile in range(max(0, number - ring_of(route)), number):
            for hop in range(4):
                piece(hop, route, tile).wait_send()


def backward_pass(*operands, collective_id):
    plan = backward_plan()
    copies = operands[0]
    count = operands[1].shape[0]
    own = count // 2
    heads = head_tiles() * LANES
    units = unit_tiles() * LANES
    length = operands[-1].shape[1]
    block = D // 16
    halves = [block * 8 >> hop for hop in range(4)]
    hbm = pl.BlockSpec(memory_space=pl.ANY)
    vmem = pl.BlockSpec(memory_space=pltpu.VMEM)
    dma = pltpu.SemaphoreType.DMA
    return pl.pallas_call(
        functools.partial(backward_kernel, plan),
        out_shape=[
            jax.ShapeDtypeStruct((count, 3 * heads), BF16),
            jax.ShapeDtypeStruct((own, D), F32),
            jax.ShapeDtypeStruct((block, 4 * heads + 3 * units), F32),
            jax.ShapeDtypeStruct((8, D), F32),
            jax.ShapeDtypeStruct((8, units), F32),
            jax.ShapeDtypeStruct((8, heads), F32),
        ],
        in_specs=[hbm] * 13 + [vmem] * 5,
        out_specs=[hbm] * 2 + [vmem] * 4,
        scratch_shapes=[
            [pltpu.VMEM((SLOTS, 2, half, LANES), BF16) for half in halves],
            [pltpu.VMEM((SLOTS, half, LANES), BF16) for half in halves],
            pltpu.VMEM((2, D, count), BF16),
            pltpu.VMEM((count, D), BF16),
            pltpu.VMEM((count, 2 * units), BF16),
            pltpu.VMEM((count, D), F32),
            pltpu.VMEM((own, D), F32),
            pltpu.VMEM((3, count, 2 * LANES), BF16),
            pltpu.VMEM((2, own, D), F32),
            pltpu.VMEM((D, 4 * heads), BF16),
            pltpu.VMEM((D, heads), BF16),
            pltpu.VMEM((2, count, 2 * LANES), BF16),
            pltpu.VMEM((length, LANES), F32),
            pltpu.VMEM((length, LANES), F32),
            dma((4, SLOTS)),
            dma((4, SLOTS)),
            dma((14,)),
            dma((6, 2)),
            dma((3, 2)),
            dma((2,)),
            dma((2,)),
            dma((2,)),
        ],
        compiler_params=pltpu.CompilerParams(
            collective_id=collective_id, has_side_effects=True, vmem_limit_bytes=62 << 20
        ),
        name="backward_pass",
    )(*operands)


def columns_of(grads):
    plan = backward_plan()
    rows = grads.shape[0]
    heads, units = head_tiles(), unit_tiles()
    shrink_steps, late = units // 2 - 1, units // 4
    rare, rarer = plan[2][0], plan[3][0]

    def tiles(start, number):
        return grads[:, start * LANES : (start + number) * LANES]

    attention_at = 2 * (shrink_steps + units - late)
    pairs = tiles(2 * shrink_steps, 2 * (units - late)).reshape(rows, units - late, 2, LANES)
    shrink = jnp.concatenate([tiles(rare, 1), tiles(rarer, 1), tiles(0, 2 * shrink_steps)], axis=1)
    up = jnp.concatenate([tiles(rare + 1, late), pairs[:, :, 0].reshape(rows, -1)], axis=1)
    gate = jnp.concatenate([tiles(rarer + 1, late), pairs[:, :, 1].reshape(rows, -1)], axis=1)
    last = late + 1
    outward = jnp.concatenate([tiles(attention_at, 4), tiles(rare + last, 1)], axis=1)
    inward = jnp.concatenate(
        [
            tiles(attention_at + 4, 12),
            tiles(rarer + last, 1),
            tiles(rare + last + 1, 1),
            tiles(rarer + last + 1, 1),
        ],
        axis=1,
    )
    return inward, outward, up, gate, shrink


def per_device(
    tokens,
    cotangent,
    segment_ids,
    pad_mask,
    inward_master,
    inward_first,
    inward_second,
    outward_master,
    outward_first,
    outward_second,
    expand_master,
    expand_first,
    expand_second,
    shrink_master,
    shrink_first,
    shrink_second,
    alpha_master,
    alpha_first,
    alpha_second,
    scale_master,
    scale_first,
    scale_second,
):
    count = lax.axis_size("dp")
    me = lax.axis_index("dp")
    core = lax.axis_index("tensor")
    inv_root = D ** (-0.5)
    rows = tokens.shape[0]
    own_rows = rows // 2
    heads_width = inward_master.shape[2]
    units = expand_master.shape[2]

    small = jnp.concatenate([alpha_master, scale_master], axis=0).astype(BF16)
    small = jnp.pad(small, ((0, LANES - small.shape[0]), (0, 0))).T
    inward_low = inward_master.astype(BF16)
    block = forward_columns(
        jnp.concatenate([inward_low[0], inward_low[1], inward_low[2]], axis=1),
        outward_master.astype(BF16).T,
        expand_master.astype(BF16),
        shrink_master.astype(BF16).T,
        small,
    )
    block = gather_rest(block, count)
    place_row = place_row_of(me, count)
    bias = bias_of(segment_ids, pad_mask)
    (
        copies,
        tokens_in,
        raw,
        mixed,
        h_attn,
        first,
        first_low,
        tokens_turned,
        first_turned,
        proj,
        hidden,
        factors,
        alphas,
        scale_rows,
        gains,
        shrunk,
    ) = forward_pass(block, tokens, place_row, bias, 0)
    copies = copies.reshape(D, -1)
    attn_factor, first_factor = factors[:, :1], factors[:, LANES : LANES + 1]
    places = place_matrix(place_row)
    cot_own = lax.dynamic_slice_in_dim(cotangent, core * own_rows, own_rows, 0)
    cot_own = nn(cot_own, places)
    keep = (1 - pad_mask).astype(F32).reshape(rows, 1)
    cot_own = cot_own * lax.dynamic_slice_in_dim(keep, core * own_rows, own_rows, 0)
    tokens_own = lax.dynamic_slice_in_dim(tokens_in, core * own_rows, own_rows, 0).astype(F32)
    def sum_own(partial):
        send = lax.dynamic_slice_in_dim(partial, (1 - core) * own_rows, own_rows, 0)
        kept = lax.dynamic_slice_in_dim(partial, core * own_rows, own_rows, 0)
        return kept + swap_cores(send)

    def both(own):
        other = swap_cores(own)
        full = jnp.zeros((rows, own.shape[1]), own.dtype)
        full = lax.dynamic_update_slice_in_dim(full, own, core * own_rows, 0)
        return lax.dynamic_update_slice_in_dim(full, other, (1 - core) * own_rows, 0)

    shrunk = sum_own(shrunk)
    h_mlp, mlp_factor = row_norm(shrunk)
    output, out_factor = row_norm(first + alphas[1] * (h_mlp - first))

    d_two = row_norm_back(cot_own, output, out_factor)
    alpha_mlp_grad = jnp.sum(d_two * (h_mlp - first), axis=0)
    d_shrunk = both(row_norm_back(alphas[1] * d_two, h_mlp, mlp_factor).astype(BF16))
    d_raw, d_one, grads, alpha_attn_grad, unit_grad, query_gain_grad = backward_pass(
        copies,
        d_shrunk,
        d_shrunk.T,
        first_turned,
        tokens_turned,
        hidden,
        proj,
        raw,
        mixed,
        d_two,
        h_attn,
        first,
        tokens_in,
        factors,
        alphas,
        scale_rows,
        gains,
        bias,
        collective_id=1,
    )
    alpha_attn_grad, query_gain_grad = alpha_attn_grad[0], query_gain_grad[0]
    up_gain_grad, gate_gain_grad = unit_grad[0], unit_grad[1]
    grads = scatter_rest(grads, count)
    inward_grad, outward_grad, up_grad, gate_grad, shrink_grad = columns_of(grads)
    last = forward_plan()[2][0]
    w_inward = jnp.concatenate(
        [copies[:, : 3 * heads_width - LANES], copies[:, last * LANES : (last + 1) * LANES]], axis=1
    )
    input_part = nt(d_raw, w_inward) * inv_root

    block_output = both(nt(output.astype(BF16), places).astype(BF16))
    residual = (1.0 - alphas[0]) * d_one
    residual_high = residual.astype(BF16)
    residual_low = (residual - residual_high.astype(F32)).astype(BF16)
    residual = nt(residual_high, places) + nt(residual_low, places)
    own_width = D // lax.axis_size("tensor")
    input_part = nt(input_part.astype(BF16), places)
    input_part = lax.dynamic_update_slice_in_dim(
        input_part,
        lax.dynamic_slice_in_dim(input_part, core * own_rows, own_rows, 0) + residual,
        core * own_rows,
        0,
    )
    input_grad = lax.dynamic_slice_in_dim(input_part, core * own_width, own_width, 1) + swap_cores(
        lax.dynamic_slice_in_dim(input_part, (1 - core) * own_width, own_width, 1)
    )

    alpha_grad = jnp.stack([alpha_attn_grad, alpha_mlp_grad])
    query_full = lax.dynamic_update_slice_in_dim(
        jnp.zeros((D,), F32), query_gain_grad, core * heads_width, 0
    )
    up_full = lax.dynamic_update_slice_in_dim(jnp.zeros((FF,), F32), up_gain_grad, core * units, 0)
    gate_full = lax.dynamic_update_slice_in_dim(
        jnp.zeros((FF,), F32), gate_gain_grad, core * units, 0
    )
    scale_grad = jnp.concatenate(
        [query_full.reshape(1, D), up_full.reshape(FF // D, D), gate_full.reshape(FF // D, D)],
        axis=0,
    )
    alpha_grad = alpha_grad + swap_cores(alpha_grad)
    scale_grad = scale_grad + swap_cores(scale_grad)
    width = D // count
    alpha_grad = scatter_sum(alpha_grad.T, count).T
    scale_grad = lax.dynamic_slice_in_dim(butterfly_sum(scale_grad, count), me * width, width, 1)

    outward_grad = outward_grad.T
    shrink_grad = shrink_grad.T
    expand_grad = jnp.stack([up_grad, gate_grad])
    inward_grad = jnp.stack(
        [inward_grad[:, k * heads_width : (k + 1) * heads_width] for k in range(3)]
    )
    inward_pre, inward_var = adam_step(
        inward_master, inward_first, inward_second, inward_grad, RATE_MATRIX
    )
    outward_pre, outward_var = adam_step(
        outward_master, outward_first, outward_second, outward_grad, RATE_MATRIX
    )
    expand_pre, expand_var = adam_step(
        expand_master, expand_first, expand_second, expand_grad, RATE_MATRIX
    )
    shrink_pre, shrink_var = adam_step(
        shrink_master, shrink_first, shrink_second, shrink_grad, RATE_MATRIX
    )
    alpha_new, alpha_var = adam_step(
        alpha_master, alpha_first, alpha_second, alpha_grad, RATE_ALPHA
    )
    scale_new, scale_var = adam_step(
        scale_master, scale_first, scale_second, scale_grad, RATE_SCALE
    )

    def renormed(pre, axis):
        squares = butterfly_sum(jnp.sum(pre * pre, axis=axis), count)
        return pre * lax.rsqrt(jnp.expand_dims(squares, axis) / D + EPS_NORM)

    return (
        block_output,
        input_grad,
        inward_grad,
        inward_var,
        renormed(inward_pre, 1),
        outward_grad,
        outward_var,
        renormed(outward_pre, 1),
        expand_grad,
        expand_var,
        renormed(expand_pre, 1),
        shrink_grad,
        shrink_var,
        renormed(shrink_pre, 1),
        alpha_grad,
        alpha_var,
        alpha_new,
        scale_grad,
        scale_var,
        scale_new,
    )


def solution(mesh):
    rows = P("dp", None)
    deep = P(None, "dp", "tensor")
    flat = P("tensor", "dp")
    vector = P(None, "dp")
    in_specs = (rows,) * 4 + (deep,) * 3 + (flat,) * 3 + (deep,) * 3 + (flat,) * 3 + (vector,) * 6
    out_specs = (
        (rows, P("dp", "tensor"))
        + (deep,) * 3
        + (flat,) * 3
        + (deep,) * 3
        + (flat,) * 3
        + (vector,) * 6
    )
    return jax.shard_map(
        per_device, mesh=mesh, in_specs=in_specs, out_specs=out_specs, check_vma=False
    )
```

time: 851 us -> 651 us (0.76)
  matrix products: 137 us -> 32.7 us
  Pallas kernels: 533 us -> 462 us
  other arithmetic: 56.7 us -> 33.9 us
  waiting for transfers between devices: 35.1 us -> 24.2 us
  local copies, waits for them, and re-layouts: 53.6 us -> 63.8 us
    dot_general x7 -> x1, matrix products: 77 us -> 2.17 us  [nn(): lax.dot_general(a, b, (((1,), (0,)), ((), ())), preferred_element_type=F32)]
    pallas_call x7 -> x2, Pallas kernels: 533 us -> 462 us  [the longest x1 233 us: forward_pass(): pl.pallas_call(functools.partial(forward_kernel, plan), out_shape=[jax.Sh...]
    dot_general x9 -> x4, matrix products: 57.1 us -> 30.5 us  [nt(): lax.dot_general(a, b, (((1,), (1,)), ((), ())), preferred_element_type=F32)]
    slice x11 -> x14, local copies, waits for them, and re-layouts: 4.3 us -> 19.3 us  [the longest x6 5.08 us: tiles(): return grads[:, start * LANES:(start + number) * LANES]]
    unnamed x178 -> x97, local copies, waits for them, and re-layouts: 30.5 us -> 16.2 us
  transfers between devices with their start and end apart: 34 -> 30, of which waited for: 16 -> 12; matrix products, arithmetic and copies ran while one was open for 15% -> 8% of each run, Pallas kernels for 34% -> 35%
where the time goes in v2:
time: 651 us; the launch traced here: 646 us
  Pallas kernels  462 us (71%)
  local copies, waits for them, and re-layouts  63.8 us (10%)
  other arithmetic  33.9 us (5%)
  matrix products  32.7 us (5%)
  starting transfers between devices  27.7 us (4%)
  waiting for transfers between devices  24.2 us (4%)
    pallas_call x1, Pallas kernels, forward_pass(): pl.pallas_call(functools.partial(forward_kernel, plan), out_shape=[jax.Sh...  233 us
    pallas_call x1, Pallas kernels, backward_pass(): pl.pallas_call(functools.partial(backward_kernel, plan), out_shape=[jax.S...  229 us
    dot_general x4, matrix products, nt(): lax.dot_general(a, b, (((1,), (1,)), ((), ())), preferred_element_type=F32)  30.5 us
    ppermute x24, starting transfers between devices, exchange(): return lax.ppermute(array, 'dp', [(i, i ^ bit) for i in range(count)])  27 us
    ppermute x24, waiting for transfers between devices, exchange(): return lax.ppermute(array, 'dp', [(i, i ^ bit) for i in range(count)])  20 us
    unnamed x97, local copies, waits for them, and re-layouts  16.2 us
  transfers between devices with their start and end apart: 30, of which 12 were waited for; matrix products, arithmetic and copies ran while one was open for 8% of the time, Pallas kernels for 35%

profile of v2, /device:TPU:0, one launch (start us, length us, event | category | flops | bytes accessed | tf_op | source)
XLA Modules:
  0.0 645.7 jit_solution(14883869478410698025)
XLA Ops:
  22.7 232.9 %forward_pass.1 = (bf16[2,2,2,2,80,10496]{5,4,3,2,1,0:T(8,128)(2,1)}, bf16[1024,1280]{1,0:T(8,128)(2,1)}, f32[1024,1920]{1,0:T(8,128)}, bf16[1024,640]{1,0:T(8,1...) custom-call(bf16[80,10496]{1,0:T(8,128)(2,1)} %bitcast_dynamic-updat, ...), custom_call_target="tpu_custom_call" | custom-call | tf_op jit(solution)/shard_map/forward_pass/pallas_call | solution.py:748
  255.6 3.4 constant_dynamic-slice_fusion.2
  259.9 4.2 collective-permute-done
  268.0 2.2 multiply_reduce_fusion.2
  275.4 3.5 constant_dynamic-update-slice_fusion.11
  281.0 4.7 slice.204
  285.7 2.4 copy.69
  289.7 2.4 copy.70
  293.6 3.1 copy.71.d_shrunk
  296.7 228.6 %backward_pass.1 = (bf16[1024,1920]{1,0:T(8,128)(2,1)}, f32[512,1280]{1,0:T(8,128)}, f32[80,10240]{1,0:T(8,128)}, f32[8,1280]{1,0:T(8,128)}, f32[8,2560]{1,0:T(8,128)}, /*index=5*/f32[8,640]{1,0:T(8,128)}) custom-call(bf16[1280,10496]{1,0:T(8,128)(2,1)} %bitcast.61, bf16[1024,1280]{1,0:T(8,128)(2,1)} %copy.71.d_shrunk, bf16[1280,1024]{1,0:T(8,128)(2,1)} %bitcast.62, ...), custom_call_target="tpu_custom_call" | custom-call | tf_op jit(solution)/shard_map/backward_pass/pallas_call | solution.py:1323
  530.4 2.5 constant_dynamic-update-slice_fusion.10
  532.9 4.6 copy.72
  537.5 5.3 fusion
  542.8 14.9 %fusion.2 = f32[1024,1280]{1,0:T(8,128)} fusion(bf16[1024,1920]{1,0:T(8,128)(2,1)} %get-tuple-element.56, bf16[1280,128]{1,0:T(8,128)(2,1)S(1)} %copy-done.25, bf16[1280,1792]{1,0:T(8,128)(2,1)} %slice.204, s32[1280]{0:T(1024)S(1)} %copy-done.32), kind=kOutput, calls=%fused_computation.3 | convolution fusion | flops 8402698240 | bytes 14095360 | tf_op jit(solution)/shard_map/dot_general | solution.py:169
  557.8 6.8 %fusion.16 = f32[1024,1280]{1,0:T(8,128)} fusion(f32[1024,1280]{1,0:T(8,128)} %fusion.2, s32[]{:T(128)S(6)} %select_n.38, f32[512,1280]{1,0:T(8,128)} %fusion, s32[1280]{0:T(1024)S(1)} %copy-done.32, f32[512,1280]{1,0:T(8,128)} %get-tuple-element.57, f32[1280]{0:T(1024)S(1)} %get-tuple-element.130), kind=kOutput, calls=%fused_computation.14 | convolution fusion | flops 1681981440 | bytes 10496004 | tf_op jit(solution)/shard_map/dot_general | solution.py:169
  564.6 3.5 constant_dynamic-slice_fusion
  569.7 2.7 collective-permute-start.4
  574.1 3.2 slice_reduce_fusion.1
  579.5 3.0 multiply_reduce_fusion.5
  597.9 3.2 collective-permute-done.11
  626.7 2.8 collective-permute-done.27
  630.2 3.7 collective-permute-done.28
  636.3 4.0 collective-permute-done.29
  641.0 4.3 dynamic-slice_add_fusion
  (251 shorter events, 91.9 us)
Async XLA Ops:
  259.0 5.1 collective-permute-start
  273.4 16.2 %collective-permute-start.2 = (bf16[512,1280]{1,0:T(8,128)(2,1)}, bf16[512,1280]{1,0:T(8,128)(2,1)}, u32[]{:S(2)}, u32[]{:S(2)}) collective-permute-start(bf16[512,1280]{1,0:T(8,128)(2,1)} %multiply_convert_fusion.1), channel_id=1, source_target_pairs={{0,1},{1,0},{2,3},{3,2},{4,5},{5,4},{6,7},{7,6},{8,9},{9,8},{10,11... | collective-permute-start | bytes 3932168 | tf_op jit(solution)/shard_map/ppermute | solution.py:119
  278.9 251.5 %collective-permute-start.1 = (bf16[512,1280]{0,1:T(8,128)(2,1)}, bf16[512,1280]{0,1:T(8,128)(2,1)}, u32[]{:S(2)}, u32[]{:S(2)}) collective-permute-start(bf16[512,1280]{0,1:T(8,128)(2,1)} %get-tuple-element.179), channel_id=1, source_target_pairs={{0,1},{1,0},{2,3},{3,2},{4,5},{5,4},{6,7},{7,6},{8,9},{9,8},{10,11... | collective-permute-start | bytes 3932168 | tf_op jit(solution)/shard_map/ppermute | solution.py:119
  568.1 72.8 %collective-permute-start.3 = (f32[1024,640]{1,0:T(8,128)}, f32[1024,640]{1,0:T(8,128)}, u32[]{:S(2)}, u32[]{:S(2)}) collective-permute-start(f32[1024,640]{1,0:T(8,128)} %constant_dynamic-slice_fusion), channel_id=1, source_target_pairs={{0,1},{1,0},{2,3},{3,2},{4,5},{5,4},{6,7},{7,6},{8,9},{9,8},{10,11... | collective-permute-start | bytes 7864328 | tf_op jit(solution)/shard_map/ppermute | solution.py:119
  569.7 24.2 %collective-permute-start.4 = (f32[3,640]{1,0:T(4,128)S(1)}, f32[3,640]{1,0:T(4,128)}, u32[]{:S(2)}, u32[]{:S(2)}) collective-permute-start(f32[3,640]{1,0:T(4,128)S(1)} %get-tuple-element.150), channel_id=1, source_target_pairs={{0,4},{2,6},{4,0},{6,2},{8,12},{10,14},{12,8},{14,10},{16,20},{18,... | collective-permute-start | bytes 23048 | tf_op jit(solution)/shard_map/ppermute | solution.py:115
  573.2 14.7 %collective-permute-start.8 = (f32[640]{0:T(1024)S(1)}, f32[640]{0:T(1024)S(1)}, u32[]{:S(2)}, u32[]{:S(2)}) collective-permute-start(f32[640]{0:T(1024)S(1)} %get-tuple-element.146), channel_id=1, source_target_pairs={{0,4},{2,6},{4,0},{6,2},{8,12},{10,14},{12,8},{14,10},{16,20},{18,... | collective-permute-start | bytes 7688 | tf_op jit(solution)/shard_map/ppermute | solution.py:115
  582.5 29.3 %collective-permute-start.12 = (f32[2,2560]{1,0:T(2,128)S(1)}, f32[2,2560]{1,0:T(2,128)}, u32[]{:S(2)}, u32[]{:S(2)}) collective-permute-start(f32[2,2560]{1,0:T(2,128)S(1)} %get-tuple-element.142), channel_id=1, source_target_pairs={{0,4},{2,6},{4,0},{6,2},{8,12},{10,14},{12,8},{14,10},{16,20},{18,... | collective-permute-start | bytes 61448 | tf_op jit(solution)/shard_map/ppermute | solution.py:115
  587.9 3.9 collective-permute-start.9
  592.0 4.6 collective-permute-start.22
  593.8 12.9 %collective-permute-start.16 = (f32[2560]{0:T(1024)S(1)}, f32[2560]{0:T(1024)S(1)}, u32[]{:S(2)}, u32[]{:S(2)}) collective-permute-start(f32[2560]{0:T(1024)S(1)} %get-tuple-element.138), channel_id=1, source_target_pairs={{0,4},{2,6},{4,0},{6,2},{8,12},{10,14},{12,8},{14,10},{16,20},{18,... | collective-permute-start | bytes 30728 | tf_op jit(solution)/shard_map/ppermute | solution.py:115
  595.5 6.6 %collective-permute-start.5 = (f32[3,640]{1,0:T(4,128)S(1)}, f32[3,640]{1,0:T(4,128)S(1)}, u32[]{:S(2)}, u32[]{:S(2)}) collective-permute-start(f32[3,640]{1,0:T(4,128)S(1)} %add.258), channel_id=1, source_target_pairs={{0,2},{2,0},{4,6},{6,4},{8,10},{10,8},{12,14},{14,12},{16,18},{18,... | collective-permute-start | bytes 23048 | tf_op jit(solution)/shard_map/ppermute | solution.py:115
  596.6 4.5 collective-permute-start.11
  602.1 4.6 collective-permute-start.6
  604.8 4.5 collective-permute-start.24
  606.7 13.7 %collective-permute-start.25 = (f32[9,1280]{1,0:T(8,128)S(1)}, f32[9,1280]{1,0:T(8,128)S(1)}, u32[]{:S(2)}, u32[]{:S(2)}) collective-permute-start(f32[9,1280]{1,0:T(8,128)S(1)} %pad_maximum_fusion.8), channel_id=1, source_target_pairs={{0,1},{1,0},{2,3},{3,2},{4,5},{5,4},{6,7},{7,6},{8,9},{9,8},{10,11... | collective-permute-start | bytes 138248 | tf_op jit(solution)/shard_map/ppermute | solution.py:119
  606.7 7.2 %collective-permute-start.17 = (f32[2560]{0:T(1024)S(1)}, f32[2560]{0:T(1024)S(1)}, u32[]{:S(2)}, u32[]{:S(2)}) collective-permute-start(f32[2560]{0:T(1024)S(1)} %add.288), channel_id=1, source_target_pairs={{0,2},{2,0},{4,6},{6,4},{8,10},{10,8},{12,14},{14,12},{16,18},{18,... | collective-permute-start | bytes 30728 | tf_op jit(solution)/shard_map/ppermute | solution.py:115
  609.3 5.3 collective-permute-start.7
  612.5 6.4 collective-permute-start.13
  617.6 4.6 collective-permute-start.19
  620.4 4.5 collective-permute-start.26
  622.8 7.4 %collective-permute-start.15 = (f32[2,2560]{1,0:T(2,128)S(1)}, f32[2,2560]{1,0:T(2,128)S(1)}, u32[]{:S(2)}, u32[]{:S(2)}) collective-permute-start(f32[2,2560]{1,0:T(2,128)S(1)} %add.280), channel_id=1, source_target_pairs={{0,16},{2,18},{4,20},{6,22},{8,24},{10,26},{12,28},{14,30},{16,0},... | collective-permute-start | bytes 61448 | tf_op jit(solution)/shard_map/ppermute | solution.py:115
  624.9 4.5 collective-permute-start.27
  629.4 4.5 collective-permute-start.28
  634.0 6.3 collective-permute-start.29
  (48 other events, 546.5 us)

commit v3 on v2

--- a/solution.py
+++ b/solution.py
@@ -115,13 +115,9 @@
     return lax.ppermute(array, "dp", [(i, i ^ bit) for i in range(count)])
 
 
-def swap_cores(array):
-    return lax.ppermute(array, "tensor", [(0, 1), (1, 0)])
-
-
 def gather_rest(block, count):
     for bit in extra_bits(count)[::-1]:
-        block = jnp.concatenate([block, exchange(block, bit, count)], axis=0)
+        block = jnp.concatenate([block, exchange(block, bit, count)], axis=-2)
     return block
 
 
@@ -130,19 +126,6 @@
         half = partial.shape[0] // 2
         partial = partial[:half] + exchange(partial[half:], bit, count)
     return partial
-
-
-def butterfly_sum(array, count):
-    for bit in list(PLACES) + extra_bits(count):
-        array = array + exchange(array, bit, count)
-    return array
-
-
-def scatter_sum(partial, count):
-    for bit in PLACES:
-        half = partial.shape[0] // 2
-        partial = partial[:half] + exchange(partial[half:], bit, count)
-    return scatter_rest(partial, count)
 
 
 def place_row_of(me, count):
@@ -154,11 +137,6 @@
     for axis, bit in enumerate(places):
         relative = relative + ((position >> (len(places) - 1 - axis)) & 1) * bit
     return ((jnp.asarray(relative) ^ me) * width + jnp.asarray(offset))[None]
-
-
-def place_matrix(place_row):
-    natural = lax.broadcasted_iota(jnp.int32, (D, D), 0)
-    return (natural == place_row).astype(BF16)
 
 
 def nn(a, b):
@@ -267,15 +245,6 @@
     return gain_total
 
 
-def bias_of(segment_ids, pad_mask):
-    positions = jnp.arange(segment_ids.shape[1])
-    key_code = jnp.where(pad_mask == 0, segment_ids, -1)
-    earlier = positions[None, :] <= positions[:, None]
-    same = positions[None, :] == positions[:, None]
-    allowed = (segment_ids[:, :, None] == key_code[:, None, :]) & earlier[None] | same[None]
-    return jnp.where(allowed, 0.0, MASKED).astype(F32)
-
-
 ARRIVE = 4 * LAG
 UNIT_GROUP = 4
 FIRST_UNIT_PAIR = 8
@@ -315,40 +284,43 @@
     return jnp.where(place < 2, rare, often)
 
 
-def forward_columns(inward, outward, expand, shrink, small):
-    rows = small.shape[0]
-    groups = unit_tiles() // UNIT_GROUP
-    heads = 3 * head_tiles() - 1
-    units = jnp.stack([expand[0], expand[1]], axis=1).reshape(
-        rows, 2, groups, UNIT_GROUP, LANES
-    )
-    units = units.transpose(0, 2, 3, 1, 4).reshape(rows, groups, 2 * UNIT_GROUP, LANES)
-    shrink = shrink.reshape(rows, groups, UNIT_GROUP, LANES)
-    units = jnp.concatenate([units, shrink[:, :, 2:]], axis=2).reshape(rows, -1)
-    return jnp.concatenate(
-        [
-            inward[:, : heads * LANES],
-            outward[:, 2 * LANES : 4 * LANES],
-            units,
-            inward[:, heads * LANES :],
-            outward[:, :LANES],
-            outward[:, 4 * LANES :],
-            shrink[:, :, 0].reshape(rows, -1),
-            small,
-            outward[:, LANES : 2 * LANES],
-            jnp.zeros((rows, LANES), BF16),
-            shrink[:, :, 1].reshape(rows, -1),
-        ],
-        axis=1,
-    )
+def forward_sources():
+    plan = forward_plan()
+    heads, units = head_tiles(), unit_tiles()
+    rare, rarer = plan[2][0], plan[3][0]
+    inward = [("inward", k // heads, k % heads) for k in range(3 * heads)]
+    sources = dict(enumerate(inward[:-1]))
+    sources[rare] = inward[-1]
+    sources[rarer] = ("small", None, 0)
+    for tile, place in ((rare + 1, 0), (rarer + 1, 1), (3 * heads - 1, 2), (3 * heads, 3), (rare + 2, 4)):
+        sources[tile] = ("outward", None, place)
+    for unit in range(units):
+        sources[pair_tile(unit)] = ("expand", 0, unit)
+        sources[pair_tile(unit) + 1] = ("expand", 1, unit)
+        sources[shrink_tile_static(unit)] = ("shrink", None, unit)
+    return sources
+
+
+def shrink_tile_static(unit):
+    plan = forward_plan()
+    group, place = unit // UNIT_GROUP, unit % UNIT_GROUP
+    if place < 2:
+        return plan[2][0] + place * plan[2][2] + RARE_UNITS + group
+    return 2 * (FIRST_UNIT_PAIR + 5 * group + UNIT_GROUP) + place - 2
 
 
 def forward_kernel(
     plan,
-    block,
+    inward,
+    outward,
+    expand,
+    shrink,
+    small_copies,
     tokens,
+    cotangent,
+    segments,
+    pads,
     place_row,
-    bias,
     out,
     tokens_out,
     raw_out,
@@ -358,15 +330,24 @@
     first_low_out,
     tokens_turned_out,
     first_turned_out,
+    bias_out,
+    d_two_out,
+    output_out,
+    d_shrunk_out,
+    d_shrunk_turned_out,
     proj_out,
     hidden_out,
     factors,
     alphas,
     scales,
     gains,
+    alpha_grad,
+    block,
     shrunk,
     place,
     tokens_in,
+    cot_in,
+    bias,
     raw,
     stage_pair,
     stage_one,
@@ -401,12 +382,27 @@
     units = unit_tiles()
     attend_at = 3 * heads // 2 + ARRIVE + 1
     pairs_each = 2
-    sequences = bias.shape[0]
-    length = bias.shape[1]
+    sequences, length = segments.shape
     head_pairs = sequences * heads
     branch_at = attend_at + -(-head_pairs // pairs_each)
     units_at = branch_at + 2
 
+    cot_copy = pltpu.make_async_copy(cotangent.at[pl.ds(own_at, own_rows)], cot_in, result_sem.at[13])
+    cot_copy.start()
+    operands = {
+        "inward": inward,
+        "outward": outward,
+        "expand": expand,
+        "shrink": shrink,
+        "small": small_copies,
+    }
+    for tile, (name, row_block, at) in forward_sources().items():
+        source = operands[name] if row_block is None else operands[name].at[row_block]
+        block[:, tile * LANES : (tile + 1) * LANES] = source[
+            :, at * LANES : (at + 1) * LANES
+        ].astype(BF16)
+    unused = plan[3][0] + 2
+    block[:, unused * LANES : (unused + 1) * LANES] = jnp.zeros((block.shape[0], LANES), BF16)
     own = pltpu.make_async_copy(block, out.at[0, 0, 0, 0], own_sem)
     own.start()
     greet(me, core)
@@ -479,6 +475,13 @@
             first_low.at[pl.ds(own_at, own_rows)], first_low.at[pl.ds(own_at, own_rows)], 1
         )
 
+    def shrunk_copy():
+        return core_copy(shrunk.at[pl.ds(other_at, own_rows)], branch_in, 2)
+
+    def d_shrunk_copy():
+        own = first_low.at[pl.ds(own_at, own_rows)]
+        return core_copy(own, own, 3)
+
     result_pairs = (
         (tokens_in, tokens_out),
         (raw, raw_out),
@@ -488,6 +491,11 @@
         (first_low, first_low_out),
         (place.at[:, pl.ds(0, rows)], tokens_turned_out),
         (place.at[:, pl.ds(0, rows)], first_turned_out),
+        (bias, bias_out),
+        (h_attn, d_two_out),
+        (tokens_in.at[pl.ds(own_at, own_rows)], output_out),
+        (first_low, d_shrunk_out),
+        (place.at[:, pl.ds(0, rows)], d_shrunk_turned_out),
     )
 
     def result(k):
@@ -514,6 +522,66 @@
 
         chunks(rows, 256, move)
         result(0).start()
+
+    def cot_in_order():
+        cot_copy.wait()
+
+        def move(at):
+            cot_in[at, :] = nn(cot_in[at, :], place[...]).astype(BF16)
+
+        chunks(own_rows, 256, move)
+
+    def column_of(row):
+        return jnp.broadcast_to(row.astype(F32), (LANES, length)).T
+
+    def make_bias():
+        for sequence in range(sequences):
+            segment = segments[sequence : sequence + 1, :]
+            pad = pads[sequence : sequence + 1, :]
+            own_segment = column_of(segment)
+            for tile in range(length // LANES):
+                lanes = slice(tile * LANES, (tile + 1) * LANES)
+                query = lax.broadcasted_iota(jnp.int32, (length, LANES), 0)
+                key = lax.broadcasted_iota(jnp.int32, (length, LANES), 1) + tile * LANES
+                open_key = jnp.where(pad[:, lanes] == 0, segment[:, lanes], -1).astype(F32)
+                allowed = ((own_segment == open_key) & (key <= query)) | (key == query)
+                bias[sequence, :, lanes] = jnp.where(allowed, 0.0, MASKED)
+        result(8).start()
+
+    def finish():
+        shrunk_copy().start()
+        result(3).wait()
+        keep = jnp.where(
+            core == 0, column_of(1 - pads[0:1, :]), column_of(1 - pads[1:2, :])
+        )
+        stage_proj[0, :own_rows, :LANES] = keep
+        alpha = alphas[1:2, :]
+        alpha_grad[...] = jnp.zeros_like(alpha_grad)
+        shrunk_copy().wait()
+
+        def some(at):
+            here = pl.ds(pl.multiple_of(own_at + at.start, 64), 64)
+            normed, factor = row_norm(shrunk[here, :] + branch_in[at, :])
+            start = first[at, :]
+            output, output_factor = row_norm(start + alpha * (normed - start))
+            upstream = cot_in[at, :].astype(F32) * stage_proj[0, at, 0:1]
+            d_two = row_norm_back(upstream, output, output_factor)
+            alpha_grad[0:1, :] += jnp.sum(d_two * (normed - start), axis=0, keepdims=True)
+            h_attn[at, :] = d_two
+            tokens_in[here, :] = output.astype(BF16)
+            first_low[here, :] = row_norm_back(alpha * d_two, normed, factor).astype(BF16)
+
+        chunks(own_rows, 64, some)
+        d_shrunk_copy().start()
+        result(9).start()
+        result(10).start()
+        result(7).wait()
+        d_shrunk_copy().wait()
+        result(11).start()
+        turn(first_low)
+        result(12).start()
+        for k in (9, 10, 11, 12):
+            result(k).wait()
 
     def turn(source):
         def some(at):
@@ -649,6 +717,11 @@
         @pl.when(index == LAG - 1)
         def _():
             own.wait()
+            cot_in_order()
+
+        @pl.when(index == LAG)
+        def _():
+            make_bias()
 
         pair = index - ARRIVE
 
@@ -724,19 +797,21 @@
     for unit in (units - 2, units - 1):
         proj_copy(unit).wait()
         hidden_copy(unit).wait()
-    for k in range(len(result_pairs)):
-        if k != 6:
-            result(k).wait()
+    for k in (0, 1, 2, 4, 5, 8):
+        result(k).wait()
+    finish()
     for route, (_, _, number, _) in enumerate(plan):
         for tile in range(max(0, number - RING), number):
             for hop in range(4):
                 piece(hop, route, tile).wait_send()
 
 
-def forward_pass(block, tokens, place_row, bias, collective_id):
+def forward_pass(*operands, collective_id):
     plan = forward_plan()
-    rows, columns = block.shape
-    count = tokens.shape[0]
+    rows = operands[1].shape[0]
+    count = operands[5].shape[0]
+    sequences, length = operands[7].shape
+    columns = sum(number for _, _, number, _ in plan) * LANES
     own = count // 2
     heads = head_tiles() * LANES
     units = unit_tiles() * LANES
@@ -757,19 +832,28 @@
             jax.ShapeDtypeStruct((count, D), BF16),
             jax.ShapeDtypeStruct((D, count), BF16),
             jax.ShapeDtypeStruct((D, count), BF16),
+            jax.ShapeDtypeStruct((sequences, length, length), F32),
+            jax.ShapeDtypeStruct((own, D), F32),
+            jax.ShapeDtypeStruct((own, D), BF16),
+            jax.ShapeDtypeStruct((count, D), BF16),
+            jax.ShapeDtypeStruct((D, count), BF16),
             jax.ShapeDtypeStruct((count, 2 * units), F32),
             jax.ShapeDtypeStruct((count, units), BF16),
             jax.ShapeDtypeStruct((own, 2 * LANES), F32),
             jax.ShapeDtypeStruct((8, D), F32),
             jax.ShapeDtypeStruct((16, D), F32),
             jax.ShapeDtypeStruct((8, units), F32),
-            jax.ShapeDtypeStruct((count, D), F32),
+            jax.ShapeDtypeStruct((8, D), F32),
         ],
-        in_specs=[vmem] * 4,
-        out_specs=[hbm] * 11 + [vmem] * 5,
+        in_specs=[vmem] * 6 + [hbm] + [vmem] * 3,
+        out_specs=[hbm] * 16 + [vmem] * 5,
         scratch_shapes=[
+            pltpu.VMEM((rows, columns), BF16),
+            pltpu.VMEM((count, D), F32),
             pltpu.VMEM((D, D), BF16),
             pltpu.VMEM((count, D), BF16),
+            pltpu.VMEM((own, D), BF16),
+            pltpu.VMEM((sequences, length, length), F32),
             pltpu.VMEM((count, 3 * heads), F32),
             pltpu.VMEM((2, *place, 2 * LANES), BF16),
             pltpu.VMEM((2, *place, LANES), BF16),
@@ -789,15 +873,15 @@
             dma((4,)),
             dma((2,)),
             dma((2,)),
-            dma((8,)),
-            dma((2,)),
-            dma((2,)),
+            dma((14,)),
+            dma((4,)),
+            dma((4,)),
         ],
         compiler_params=pltpu.CompilerParams(
             collective_id=collective_id, has_side_effects=True, vmem_limit_bytes=60 << 20
         ),
         name="forward_pass",
-    )(block, tokens, place_row, bias)
+    )(*operands)
 
 
 SLOTS = 2 * RING + 4
@@ -836,13 +920,14 @@
     alphas,
     scales,
     gains,
+    alpha_mlp_grad,
     bias,
-    d_raw_out,
-    d_one_out,
+    place_row,
+    output,
+    input_grad,
+    block_output,
     grads,
-    alpha_grad,
-    unit_grad,
-    query_grad,
+    vectors,
     work,
     arrived,
     lefts,
@@ -857,6 +942,11 @@
     right,
     sum_k,
     sum_v,
+    alpha_grad,
+    unit_grad,
+    query_grad,
+    vector_sums,
+    vector_in,
     send_sem,
     recv_sem,
     load_sem,
@@ -865,6 +955,8 @@
     result_sem,
     core_send,
     core_recv,
+    vector_send,
+    vector_recv,
 ):
     me = lax.axis_index("dp")
     core = lax.axis_index("tensor")
@@ -1167,7 +1259,6 @@
 
         chunks(own_rows, 64, some)
         branch_copy().start()
-        copy(stage_rows.at[0], d_one_out, result_sem.at[0]).start()
 
 
     def raw_copies(number):
@@ -1208,12 +1299,167 @@
         )
         query_grad[0:1, head_lanes] += total
 
-    def d_raw_copy():
-        return copy(
-            wide.at[pl.ds(0, rows), pl.ds(heads * LANES, 3 * heads * LANES)],
-            d_raw_out,
-            result_sem.at[1],
+
+    head_lanes = 3 * heads * LANES
+    beyond = D - rows
+
+    def inward_copies():
+        first_lanes = (3 * heads - 1) * LANES
+        result = []
+        for row, number, at, lane in ((0, rows, 0, 0), (rows, beyond, 0, head_lanes)):
+            for source, width in ((0, first_lanes), (rare * LANES, LANES)):
+                offset = 0 if width == first_lanes else first_lanes
+                result.append(
+                    (
+                        copies.at[pl.ds(row, number), pl.ds(source, width)],
+                        d_proj.at[pl.ds(at, number), pl.ds(lane + offset, width)],
+                    )
+                )
+        return [copy(source, target, load_sem.at[14 + k]) for k, (source, target) in enumerate(result)]
+
+    order_lane = 2 * head_lanes
+
+    def make_order():
+        natural = place_row[...]
+
+        def fill(at):
+            here = lax.broadcasted_iota(jnp.int32, (LANES, D), 0) + at.start
+            d_proj[at, order_lane : order_lane + D] = jnp.where(here == natural, 1.0, 0.0).astype(
+                BF16
+            )
+
+        chunks(rows, LANES, fill)
+        for k in range(beyond // LANES):
+            here = lax.broadcasted_iota(jnp.int32, (LANES, D), 0) + rows + k * LANES
+            at = slice(beyond + k * LANES, beyond + (k + 1) * LANES)
+            d_proj[at, head_lanes : head_lanes + D] = jnp.where(here == natural, 1.0, 0.0).astype(
+                BF16
+            )
+
+    def natural_parts(values):
+        low = nt(values, d_proj[:, order_lane : order_lane + D])
+        high = nt(values, d_proj[beyond : 2 * beyond, head_lanes : head_lanes + D])
+        return low, high
+
+    def input_part(number):
+        at = pl.ds(pl.multiple_of(number * 256, 256), 256)
+        upstream = wide[at, heads * LANES : 4 * heads * LANES]
+        low = nt(upstream, d_proj[:, :head_lanes]) * inv_root
+        d_low[at, :rows] = low.astype(BF16)
+        high = nt(upstream, d_proj[:beyond, head_lanes : 2 * head_lanes]) * inv_root
+        d_low[at, rows:] = high.astype(BF16)
+        low, high = natural_parts(d_low[at, :])
+        first_part[at, :rows] = low
+        first_part[at, rows:] = high
+
+    def residual_part():
+        alpha_attn = alphas[0:1, :]
+
+        def some(at):
+            here = pl.ds(pl.multiple_of(own_at + at.start, 128), 128)
+            residual = (1.0 - alpha_attn) * stage_rows[0, at, :]
+            top = residual.astype(BF16)
+            rest = (residual - top.astype(F32)).astype(BF16)
+            for part in (top, rest):
+                low, high = natural_parts(part)
+                first_part[here, :rows] += low
+                first_part[here, rows:] += high
+
+        chunks(own_rows, 128, some)
+
+    half_width = D // 2
+
+    def input_copies():
+        lanes = pl.ds(pl.multiple_of((1 - core) * half_width, LANES), half_width)
+        return [
+            core_copy(
+                first_part.at[pl.ds(k * own_rows, own_rows), lanes],
+                core_in.at[:, pl.ds(k * half_width, half_width)],
+                2 + k,
+            )
+            for k in range(2)
+        ]
+
+    def input_copy(k):
+        lanes = pl.ds(pl.multiple_of(core * half_width, LANES), half_width)
+        at = pl.ds(k * own_rows, own_rows)
+        return copy(first_part.at[at, lanes], input_grad.at[at], result_sem.at[k])
+
+    def input_sum():
+        lanes = pl.ds(pl.multiple_of(core * half_width, LANES), half_width)
+        for k, part in enumerate(input_copies()):
+            part.wait()
+            at = pl.ds(k * own_rows, own_rows)
+            first_part[at, lanes] += core_in[:, k * half_width : (k + 1) * half_width]
+            input_copy(k).start()
+
+    def output_load():
+        return copy(output, d_low.at[pl.ds(other_at, own_rows)], load_sem.at[18])
+
+    def output_order():
+        output_load().wait()
+        for k in range(own_rows // 256):
+            source = pl.ds(pl.multiple_of(other_at + k * 256, 256), 256)
+            target = pl.ds(pl.multiple_of(own_at + k * 256, 256), 256)
+            low, high = natural_parts(d_low[source, :])
+            d_low[target, :rows] = low.astype(BF16)
+            d_low[target, rows:] = high.astype(BF16)
+        output_copies()[0].start()
+        output_copies()[1].start()
+
+    def output_copies():
+        own = pl.ds(own_at, own_rows)
+        return (
+            core_copy(d_low.at[own], block_output.at[own], 4),
+            copy(d_low.at[own], block_output.at[own], result_sem.at[2]),
         )
+
+    def vector_copy(k):
+        if k == 0:
+            device = {"tensor": 1 - core}
+        else:
+            device = {"dp": partner_of(me, PLACES[k - 1])}
+        return pltpu.make_async_remote_copy(
+            src_ref=vector_sums.at[k],
+            dst_ref=vector_in.at[k],
+            send_sem=vector_send.at[k],
+            recv_sem=vector_recv.at[k],
+            device_id=device,
+            device_id_type=pl.DeviceIdType.MESH,
+        )
+
+    def vectors_start():
+        alpha_grad[1:2, :] = alpha_mlp_grad[0:1, :]
+        vector_sums[0] = jnp.zeros_like(vector_sums[0])
+        values = alpha_grad[...]
+        for _ in range(3):
+            part = values.astype(BF16)
+            low, high = natural_parts(part)
+            vector_sums[0, :8, :rows] += low
+            vector_sums[0, :8, rows:] += high
+            values = values - part.astype(F32)
+        vector_sums[0, 2:3, pl.ds(pl.multiple_of(core * heads * LANES, LANES), heads * LANES)] = (
+            query_grad[0:1, :]
+        )
+        each = units * LANES // D
+        for row in range(2):
+            for k in range(2 * each):
+                here = unit_grad[row : row + 1, (k % each) * D : (k % each + 1) * D]
+                at = 3 + 2 * each * row + k
+                vector_sums[0, at : at + 1, :] = jnp.where(core == k // each, here, 0.0)
+        vector_copy(0).start()
+
+    def vectors_add(k):
+        vector_copy(k).wait()
+        total = vector_sums[k] + vector_in[k]
+        if k < len(PLACES):
+            vector_sums[k + 1] = total
+            vector_copy(k + 1).start()
+        else:
+            vectors[...] = total
+
+    input_at = attention_at + 1
+    parts = rows // 256
 
 
     for k in (5, 6, 9, 7):
@@ -1289,9 +1535,42 @@
         def _():
             attend_one(number)
 
-        @pl.when(number == head_pairs)
-        def _():
-            d_raw_copy().start()
+        @pl.when(index == attention_at)
+        def _():
+            for part in inward_copies():
+                part.start()
+            make_order()
+            vectors_start()
+
+        for k in range(len(PLACES) + 1):
+
+            @pl.when(index == attention_at + 1 + k)
+            def _(k=k):
+                vectors_add(k)
+
+        @pl.when(index == input_at)
+        def _():
+            for part in inward_copies():
+                part.wait()
+
+        @pl.when((index >= input_at) & (index < input_at + parts))
+        def _():
+            input_part(index - input_at)
+
+        @pl.when(index == input_at + parts)
+        def _():
+            output_load().start()
+            residual_part()
+            for part in input_copies():
+                part.start()
+
+        @pl.when(index == input_at + parts + 1)
+        def _():
+            output_order()
+
+        @pl.when(index == input_at + parts + 2)
+        def _():
+            input_sum()
 
         return 0
 
@@ -1299,8 +1578,10 @@
         lefts[1, :, at] = d_low[at, :].astype(F32).T.astype(BF16)
 
     lax.fori_loop(0, steps_of(plan, 4), step, 0)
-    copy(stage_rows.at[0], d_one_out, result_sem.at[0]).wait()
-    d_raw_copy().wait()
+    for part in output_copies():
+        part.wait()
+    for k in range(2):
+        input_copy(k).wait()
     for route, (_, _, number, _) in enumerate(plan):
         for tile in range(max(0, number - ring_of(route)), number):
             for hop in range(4):
@@ -1314,7 +1595,7 @@
     own = count // 2
     heads = head_tiles() * LANES
     units = unit_tiles() * LANES
-    length = operands[-1].shape[1]
+    length = operands[18].shape[1]
     block = D // 16
     halves = [block * 8 >> hop for hop in range(4)]
     hbm = pl.BlockSpec(memory_space=pl.ANY)
@@ -1323,15 +1604,13 @@
     return pl.pallas_call(
         functools.partial(backward_kernel, plan),
         out_shape=[
-            jax.ShapeDtypeStruct((count, 3 * heads), BF16),
-            jax.ShapeDtypeStruct((own, D), F32),
+            jax.ShapeDtypeStruct((count, D // 2), F32),
+            jax.ShapeDtypeStruct((count, D), BF16),
             jax.ShapeDtypeStruct((block, 4 * heads + 3 * units), F32),
-            jax.ShapeDtypeStruct((8, D), F32),
-            jax.ShapeDtypeStruct((8, units), F32),
-            jax.ShapeDtypeStruct((8, heads), F32),
+            jax.ShapeDtypeStruct((16, D), F32),
         ],
-        in_specs=[hbm] * 13 + [vmem] * 5,
-        out_specs=[hbm] * 2 + [vmem] * 4,
+        in_specs=[hbm] * 13 + [vmem] * 7 + [hbm],
+        out_specs=[hbm] * 2 + [vmem] * 2,
         scratch_shapes=[
             [pltpu.VMEM((SLOTS, 2, half, LANES), BF16) for half in halves],
             [pltpu.VMEM((SLOTS, half, LANES), BF16) for half in halves],
@@ -1347,20 +1626,71 @@
             pltpu.VMEM((2, count, 2 * LANES), BF16),
             pltpu.VMEM((length, LANES), F32),
             pltpu.VMEM((length, LANES), F32),
+            pltpu.VMEM((8, D), F32),
+            pltpu.VMEM((8, units), F32),
+            pltpu.VMEM((8, heads), F32),
+            pltpu.VMEM((5, 16, D), F32),
+            pltpu.VMEM((5, 16, D), F32),
             dma((4, SLOTS)),
             dma((4, SLOTS)),
-            dma((14,)),
+            dma((19,)),
             dma((6, 2)),
             dma((3, 2)),
-            dma((2,)),
-            dma((2,)),
-            dma((2,)),
+            dma((3,)),
+            dma((5,)),
+            dma((5,)),
+            dma((5,)),
+            dma((5,)),
         ],
         compiler_params=pltpu.CompilerParams(
             collective_id=collective_id, has_side_effects=True, vmem_limit_bytes=62 << 20
         ),
         name="backward_pass",
     )(*operands)
+
+
+def sum_kernel(values, total, sums, arrived, send_sem, recv_sem):
+    me = lax.axis_index("dp")
+    greet(me)
+    sums[0] = values[...]
+    for k, bit in enumerate(PLACES):
+        copy = pltpu.make_async_remote_copy(
+            src_ref=sums.at[k],
+            dst_ref=arrived.at[k],
+            send_sem=send_sem.at[k],
+            recv_sem=recv_sem.at[k],
+            device_id={"dp": partner_of(me, bit)},
+            device_id_type=pl.DeviceIdType.MESH,
+        )
+        copy.start()
+        copy.wait()
+        if k + 1 < len(PLACES):
+            sums[k + 1] = sums[k] + arrived[k]
+        else:
+            total[...] = sums[k] + arrived[k]
+
+
+def sum_all(values, count, collective_id):
+    for bit in extra_bits(count):
+        values = values + exchange(values, bit, count)
+    vmem = pl.BlockSpec(memory_space=pltpu.VMEM)
+    hops = len(PLACES)
+    return pl.pallas_call(
+        sum_kernel,
+        out_shape=jax.ShapeDtypeStruct(values.shape, F32),
+        in_specs=[vmem],
+        out_specs=vmem,
+        scratch_shapes=[
+            pltpu.VMEM((hops, *values.shape), F32),
+            pltpu.VMEM((hops, *values.shape), F32),
+            pltpu.SemaphoreType.DMA((hops,)),
+            pltpu.SemaphoreType.DMA((hops,)),
+        ],
+        compiler_params=pltpu.CompilerParams(
+            collective_id=collective_id, has_side_effects=True, vmem_limit_bytes=16 << 20
+        ),
+        name="sum_all",
+    )(values)
 
 
 def columns_of(grads):
@@ -1418,26 +1748,20 @@
 ):
     count = lax.axis_size("dp")
     me = lax.axis_index("dp")
-    core = lax.axis_index("tensor")
-    inv_root = D ** (-0.5)
-    rows = tokens.shape[0]
-    own_rows = rows // 2
     heads_width = inward_master.shape[2]
-    units = expand_master.shape[2]
 
     small = jnp.concatenate([alpha_master, scale_master], axis=0).astype(BF16)
     small = jnp.pad(small, ((0, LANES - small.shape[0]), (0, 0))).T
-    inward_low = inward_master.astype(BF16)
-    block = forward_columns(
-        jnp.concatenate([inward_low[0], inward_low[1], inward_low[2]], axis=1),
+    masters = (
+        inward_master,
         outward_master.astype(BF16).T,
-        expand_master.astype(BF16),
+        expand_master,
         shrink_master.astype(BF16).T,
         small,
     )
-    block = gather_rest(block, count)
+    if extra_bits(count):
+        masters = [gather_rest(master.astype(BF16), count) for master in masters]
     place_row = place_row_of(me, count)
-    bias = bias_of(segment_ids, pad_mask)
     (
         copies,
         tokens_in,
@@ -1448,44 +1772,26 @@
         first_low,
         tokens_turned,
         first_turned,
+        bias,
+        d_two,
+        output,
+        d_shrunk,
+        d_shrunk_turned,
         proj,
         hidden,
         factors,
         alphas,
         scale_rows,
         gains,
-        shrunk,
-    ) = forward_pass(block, tokens, place_row, bias, 0)
-    copies = copies.reshape(D, -1)
-    attn_factor, first_factor = factors[:, :1], factors[:, LANES : LANES + 1]
-    places = place_matrix(place_row)
-    cot_own = lax.dynamic_slice_in_dim(cotangent, core * own_rows, own_rows, 0)
-    cot_own = nn(cot_own, places)
-    keep = (1 - pad_mask).astype(F32).reshape(rows, 1)
-    cot_own = cot_own * lax.dynamic_slice_in_dim(keep, core * own_rows, own_rows, 0)
-    tokens_own = lax.dynamic_slice_in_dim(tokens_in, core * own_rows, own_rows, 0).astype(F32)
-    def sum_own(partial):
-        send = lax.dynamic_slice_in_dim(partial, (1 - core) * own_rows, own_rows, 0)
-        kept = lax.dynamic_slice_in_dim(partial, core * own_rows, own_rows, 0)
-        return kept + swap_cores(send)
-
-    def both(own):
-        other = swap_cores(own)
-        full = jnp.zeros((rows, own.shape[1]), own.dtype)
-        full = lax.dynamic_update_slice_in_dim(full, own, core * own_rows, 0)
-        return lax.dynamic_update_slice_in_dim(full, other, (1 - core) * own_rows, 0)
-
-    shrunk = sum_own(shrunk)
-    h_mlp, mlp_factor = row_norm(shrunk)
-    output, out_factor = row_norm(first + alphas[1] * (h_mlp - first))
-
-    d_two = row_norm_back(cot_own, output, out_factor)
-    alpha_mlp_grad = jnp.sum(d_two * (h_mlp - first), axis=0)
-    d_shrunk = both(row_norm_back(alphas[1] * d_two, h_mlp, mlp_factor).astype(BF16))
-    d_raw, d_one, grads, alpha_attn_grad, unit_grad, query_gain_grad = backward_pass(
-        copies,
+        alpha_mlp_grad,
+    ) = forward_pass(
+        *masters, tokens, cotangent, segment_ids, pad_mask, place_row, collective_id=0
+    )
+
+    input_grad, block_output, grads, vectors = backward_pass(
+        copies.reshape(D, -1),
         d_shrunk,
-        d_shrunk.T,
+        d_shrunk_turned,
         first_turned,
         tokens_turned,
         hidden,
@@ -1500,53 +1806,19 @@
         alphas,
         scale_rows,
         gains,
+        alpha_mlp_grad,
         bias,
+        place_row,
+        output,
         collective_id=1,
     )
-    alpha_attn_grad, query_gain_grad = alpha_attn_grad[0], query_gain_grad[0]
-    up_gain_grad, gate_gain_grad = unit_grad[0], unit_grad[1]
     grads = scatter_rest(grads, count)
     inward_grad, outward_grad, up_grad, gate_grad, shrink_grad = columns_of(grads)
-    last = forward_plan()[2][0]
-    w_inward = jnp.concatenate(
-        [copies[:, : 3 * heads_width - LANES], copies[:, last * LANES : (last + 1) * LANES]], axis=1
-    )
-    input_part = nt(d_raw, w_inward) * inv_root
-
-    block_output = both(nt(output.astype(BF16), places).astype(BF16))
-    residual = (1.0 - alphas[0]) * d_one
-    residual_high = residual.astype(BF16)
-    residual_low = (residual - residual_high.astype(F32)).astype(BF16)
-    residual = nt(residual_high, places) + nt(residual_low, places)
-    own_width = D // lax.axis_size("tensor")
-    input_part = nt(input_part.astype(BF16), places)
-    input_part = lax.dynamic_update_slice_in_dim(
-        input_part,
-        lax.dynamic_slice_in_dim(input_part, core * own_rows, own_rows, 0) + residual,
-        core * own_rows,
-        0,
-    )
-    input_grad = lax.dynamic_slice_in_dim(input_part, core * own_width, own_width, 1) + swap_cores(
-        lax.dynamic_slice_in_dim(input_part, (1 - core) * own_width, own_width, 1)
-    )
-
-    alpha_grad = jnp.stack([alpha_attn_grad, alpha_mlp_grad])
-    query_full = lax.dynamic_update_slice_in_dim(
-        jnp.zeros((D,), F32), query_gain_grad, core * heads_width, 0
-    )
-    up_full = lax.dynamic_update_slice_in_dim(jnp.zeros((FF,), F32), up_gain_grad, core * units, 0)
-    gate_full = lax.dynamic_update_slice_in_dim(
-        jnp.zeros((FF,), F32), gate_gain_grad, core * units, 0
-    )
-    scale_grad = jnp.concatenate(
-        [query_full.reshape(1, D), up_full.reshape(FF // D, D), gate_full.reshape(FF // D, D)],
-        axis=0,
-    )
-    alpha_grad = alpha_grad + swap_cores(alpha_grad)
-    scale_grad = scale_grad + swap_cores(scale_grad)
+    for bit in extra_bits(count):
+        vectors = vectors + exchange(vectors, bit, count)
     width = D // count
-    alpha_grad = scatter_sum(alpha_grad.T, count).T
-    scale_grad = lax.dynamic_slice_in_dim(butterfly_sum(scale_grad, count), me * width, width, 1)
+    vectors = lax.dynamic_slice_in_dim(vectors, me * width, width, 1)
+    alpha_grad, scale_grad = vectors[:2], vectors[2 : 2 + scale_master.shape[0]]
 
     outward_grad = outward_grad.T
     shrink_grad = shrink_grad.T
@@ -1573,25 +1845,34 @@
         scale_master, scale_first, scale_second, scale_grad, RATE_SCALE
     )
 
-    def renormed(pre, axis):
-        squares = butterfly_sum(jnp.sum(pre * pre, axis=axis), count)
-        return pre * lax.rsqrt(jnp.expand_dims(squares, axis) / D + EPS_NORM)
+    squares = [
+        jnp.sum(pre * pre, axis=axis).reshape(-1)
+        for pre, axis in ((inward_pre, 1), (outward_pre, 1), (expand_pre, 1), (shrink_pre, 1))
+    ]
+    sizes = [square.shape[0] for square in squares]
+    squares = sum_all(jnp.concatenate(squares).reshape(8, -1), count, 2).reshape(-1)
+    ends = np.cumsum(sizes)
+
+    def renormed(pre, axis, which):
+        mean = squares[int(ends[which]) - sizes[which] : int(ends[which])] / D
+        kept = [size for k, size in enumerate(pre.shape) if k != axis]
+        return pre * jnp.expand_dims(lax.rsqrt(mean + EPS_NORM).reshape(kept), axis)
 
     return (
         block_output,
         input_grad,
         inward_grad,
         inward_var,
-        renormed(inward_pre, 1),
+        renormed(inward_pre, 1, 0),
         outward_grad,
         outward_var,
-        renormed(outward_pre, 1),
+        renormed(outward_pre, 1, 1),
         expand_grad,
         expand_var,
-        renormed(expand_pre, 1),
+        renormed(expand_pre, 1, 2),
         shrink_grad,
         shrink_var,
-        renormed(shrink_pre, 1),
+        renormed(shrink_pre, 1, 3),
         alpha_grad,
         alpha_var,
         alpha_new,

time: 651 us -> 563 us (0.86)
  Pallas kernels: 462 us -> 516 us
  local copies, waits for them, and re-layouts: 63.8 us -> 21.2 us
  matrix products: 32.7 us -> 0 us
  starting transfers between devices: 27.7 us -> 0 us
  waiting for transfers between devices: 24.2 us -> 0 us
  other arithmetic: 33.9 us -> 21.4 us
    dot_general x5 -> x0, matrix products: 32.7 us -> none  [the longest x4 30.5 us: nt(): lax.dot_general(a, b, (((1,), (1,)), ((), ())), preferred_element_type=F32)]
    ppermute x30 -> x0, starting transfers between devices: 27.7 us -> none  [the longest x24 27 us: exchange(): return lax.ppermute(array, 'dp', [(i, i ^ bit) for i in range(count)])]
    pallas_call x1, Pallas kernels: 229 us -> 253 us  [backward_pass(): pl.pallas_call(functools.partial(backward_kernel, plan), out_shape=[jax.S...]
    ppermute x30 -> x0, waiting for transfers between devices: 24.2 us -> none  [the longest x24 20 us: exchange(): return lax.ppermute(array, 'dp', [(i, i ^ bit) for i in range(count)])]
    pallas_call x0 -> x1, Pallas kernels: none -> 15 us  [sum_all(): pl.pallas_call(sum_kernel, out_shape=jax.ShapeDtypeStruct(values.shape, F...]
    pallas_call x1, Pallas kernels: 233 us -> 248 us  [forward_pass(): pl.pallas_call(functools.partial(forward_kernel, plan), out_shape=[jax.Sh...]
    slice x11 -> x1, local copies, waits for them, and re-layouts: 11.2 us -> 0.01 us  [renormed(): mean = squares[int(ends[which]) - sizes[which]:int(ends[which])] / D]
    dynamic_update_slice x7 -> x0, local copies, waits for them, and re-layouts: 8.66 us -> none  [the longest x3 7.04 us: both(): lax.dynamic_update_slice_in_dim(full, other, (1 - core) * own_rows, 0)]
  transfers between devices with their start and end apart: 30 -> 0, of which waited for: 12 -> 0; matrix products, arithmetic and copies ran while one was open for 8% -> 0% of each run, Pallas kernels for 35% -> 0%
where the time goes in v3:
time: 563 us; the launch traced here: 560 us
  Pallas kernels  516 us (92%)
  other arithmetic  21.4 us (4%)
  local copies, waits for them, and re-layouts  21.2 us (4%)
    pallas_call x1, Pallas kernels, backward_pass(): pl.pallas_call(functools.partial(backward_kernel, plan), out_shape=[jax.S...  253 us
    pallas_call x1, Pallas kernels, forward_pass(): pl.pallas_call(functools.partial(forward_kernel, plan), out_shape=[jax.Sh...  248 us
    pallas_call x1, Pallas kernels, sum_all(): pl.pallas_call(sum_kernel, out_shape=jax.ShapeDtypeStruct(values.shape, F...  15 us

profile of v3, /device:TPU:0, one launch (start us, length us, event | category | flops | bytes accessed | tf_op | source)
XLA Modules:
  0.0 559.8 jit_solution(9930855115547153689)
XLA Ops:
  2.0 1.9 convert_bitcast_fusion.shrink
  3.9 1.6 convert_bitcast_fusion.1.outward
  7.6 247.8 %forward_pass.1 = (bf16[2,2,2,2,80,10496]{5,4,3,2,1,0:T(8,128)(2,1)}, bf16[1024,1280]{1,0:T(8,128)(2,1)}, f32[1024,1920]{1,0:T(8,128)}, bf16[1024,640]{1,0:T(8,1...) custom-call(f32[3,80,640]{2,1,0:T(8,128)} %inward.1, ...), custom_call_target="tpu_custom_call" | custom-call | tf_op jit(solution)/shard_map/forward_pass/pallas_call | solution.py:823
  255.5 253.0 %backward_pass.1 = (f32[1024,640]{1,0:T(8,128)}, bf16[1024,1280]{1,0:T(8,128)(2,1)}, f32[80,10240]{1,0:T(8,128)}, f32[16,1280]{1,0:T(8,128)}) custom-call(bf16[1280,10496]{1,0:T(8,128)(2,1)} %bitcast.33, bf16[1024,1280]{1,0:T(8,128)(2,1)} %get-tuple-element.45.d_shrunk, bf16[1280,1024]{1,0:T(8,128)(2,1)} %get-tuple-element.46.d_shrunk_turned, ...), custom_call_target="tpu_custom_call" | custom-call | tf_op jit(solution)/shard_map/backward_pass/pallas_call | solution.py:1604
  508.5 1.6 fusion.18
  510.0 0.9 slice.83
  511.0 1.4 multiply_reduce_fusion.3
  512.4 1.4 slice.86
  514.4 3.2 slice_reduce_fusion.1
  518.1 2.1 fusion.19
  520.4 1.2 copy-done
  522.1 2.9 multiply_reduce_fusion
  525.1 1.2 slice.92
  526.5 3.0 multiply_reduce_fusion.1
  529.5 1.2 slice.78
  531.0 1.4 multiply_reduce_fusion.2
  532.5 15.0 %sum_all.1 = f32[8,1280]{1,0:T(8,128)S(1)} custom-call(f32[8,1280]{1,0:T(8,128)S(1)} %reshape.91.values), custom_call_target="tpu_custom_call" | custom-call | tf_op jit(solution)/shard_map/sum_all/pallas_call | solution.py:1678
  547.5 1.0 broadcast_multiply_fusion.1
  548.5 1.3 broadcast_multiply_fusion
  550.7 0.9 broadcast_multiply_fusion.2
  551.5 1.4 multiply_subtract_fusion.4
  553.0 1.4 multiply_subtract_fusion.5
  554.3 3.5 copy.55
  557.9 1.5 copy.56
  (70 shorter events, 6.4 us)
Async XLA Ops:
  255.4 255.5 %copy-start.6 = (f32[640,80]{0,1:T(8,128)S(1)}, f32[640,80]{0,1:T(8,128)}, u32[]{:S(2)}) copy-start(f32[640,80]{0,1:T(8,128)} %param.31) | copy-start | bytes 614404
  255.5 255.5 %copy-start.11 = (f32[640,80]{0,1:T(8,128)S(1)}, f32[640,80]{0,1:T(8,128)}, u32[]{:S(2)}) copy-start(f32[640,80]{0,1:T(8,128)} %param.33) | copy-start | bytes 614404
  255.5 255.5 %copy-start.15 = (bf16[640,80]{0,1:T(8,128)(2,1)S(1)}, bf16[640,80]{0,1:T(8,128)(2,1)}, u32[]{:S(2)}) copy-start(bf16[640,80]{0,1:T(8,128)(2,1)} %param.32) | copy-start | bytes 307204
  518.1 2.3 copy-start.5
  520.2 1.4 copy-start
  520.2 1.9 copy-start.4
  525.1 1.4 copy-start.1
  526.4 4.3 copy-start.12
  526.4 4.3 copy-start.13
  526.4 4.3 copy-start.14
  526.4 4.3 copy-start.10
  529.5 1.3 copy-start.3
  529.5 1.3 copy-start.7
  529.5 1.3 copy-start.8
  529.5 1.5 copy-start.9
  531.0 1.5 copy-start.17
  549.9 1.7 copy-start.16
  549.9 1.7 copy-start.18
  549.9 1.7 copy-start.19
  549.9 3.1 copy-start.20
  549.9 3.1 copy-start.21
  549.9 3.1 copy-start.22
  554.3 3.6 copy-start.2

commit v4 on v3

--- a/solution.py
+++ b/solution.py
@@ -77,18 +77,16 @@
     rare = tiles // 10
     often = (tiles - 2 * rare) // 2
     return (
-        (0, 2, often, 1),
-        (1, 2, often, 1),
-        (2 * often, 1, rare, EVERY),
-        (2 * often + rare, 1, rare, EVERY),
+        (0, 2, often, 1, 0),
+        (1, 2, often, 1, 0),
+        (2 * often, 1, rare, EVERY, 0),
+        (2 * often + rare, 1, rare, EVERY, EVERY // 2),
     )
 
 
 def for_tiles(step, hop, plan, body):
-    for route, (_, _, number, every) in enumerate(plan):
-        if number == 0:
-            continue
-        at = step - hop * LAG
+    for route, (_, _, number, every, start) in enumerate(plan):
+        at = step - hop * LAG - start
         due = (at >= 0) & (at < number * every)
         if every > 1:
             due = due & (at % every == 0)
@@ -99,12 +97,12 @@
 
 
 def lanes_of(plan, route, tile):
-    first, stride, _, _ = plan[route]
+    first, stride = plan[route][:2]
     return pl.ds(pl.multiple_of((first + stride * tile) * LANES, LANES), LANES)
 
 
 def steps_of(plan, hops):
-    return max((number - 1) * every + 1 for _, _, number, every in plan if number) + hops * LAG
+    return max(start + (number - 1) * every + 1 for _, _, number, every, start in plan) + hops * LAG
 
 
 def extra_bits(count):
@@ -197,11 +195,12 @@
 ):
     length = raw_q.shape[0]
     low_lanes = lax.broadcasted_iota(jnp.int32, (1, 2 * HD), 1) < HD
+    low_rows = lax.broadcasted_iota(jnp.int32, (2 * HD, 1), 0) < HD
     key_raw = raw_k[...]
     key_factor = head_factors(key_raw, low_lanes)
     key_unit = key_raw * key_factor
     key = (gains * key_unit).astype(BF16)
-    key_eight = key * 8
+    key_eight = ((gains * key_unit).astype(BF16).astype(F32) * 8.0).T.astype(BF16)
     value = raw_v[...].astype(BF16)
     sum_k[...] = jnp.zeros_like(sum_k)
     sum_v[...] = jnp.zeros_like(sum_v)
@@ -218,24 +217,22 @@
         query_factor = head_factors(query_raw, low_lanes)
         query_unit = query_raw * query_factor
         query = (gains * query_unit).astype(BF16) * 8
-        upstream = d_mixed[rows].astype(F32)
-        tile_bias = bias[rows, start:end]
+        upstream = d_mixed[rows]
+        tile_bias = bias[start:end, rows]
         d_query = []
         for low in (True, False):
             lanes = low_lanes if low else jnp.logical_not(low_lanes)
             own_query = jnp.where(lanes, query, jnp.zeros_like(query))
-            expo = jnp.exp(nt(own_query, key[start:end]) + tile_bias)
-            inverse = 1.0 / jnp.sum(expo, axis=-1, keepdims=True)
-            expo_low = expo.astype(BF16)
-            result = nn(expo_low, value[start:end]) * inverse
-            own_up = jnp.where(lanes, upstream, 0.0)
-            delta = jnp.sum(result * own_up, axis=-1, keepdims=True) * inverse
-            own_up = (own_up * inverse).astype(BF16)
-            sum_v[start:end, :] += tn(expo_low, own_up)
-            d_scores = (expo * (nt(own_up, value[start:end]) - delta)).astype(BF16)
-            d_query.append(nn(d_scores, key_eight[start:end]))
-            sum_k[start:end, :] += tn(d_scores, own_query)
-        d_query = jnp.where(low_lanes, d_query[0], d_query[1])
+            own_up = jnp.where(lanes, upstream, jnp.zeros_like(upstream))
+            expo = jnp.exp(nt(key[start:end], own_query) + tile_bias)
+            probs = expo * (1.0 / jnp.sum(expo, axis=0, keepdims=True))
+            d_probs = nt(value[start:end], own_up)
+            delta = jnp.sum(probs * d_probs, axis=0, keepdims=True)
+            d_scores = (probs * (d_probs - delta)).astype(BF16)
+            sum_v[start:end, :] += nn(probs.astype(BF16), own_up)
+            sum_k[start:end, :] += nn(d_scores, own_query)
+            d_query.append(nn(key_eight[:, start:end], d_scores))
+        d_query = jnp.where(low_rows, d_query[0], d_query[1]).T
         gain_total += jnp.sum(d_query * query_unit, axis=0, keepdims=True)
         d_raw_q[rows, :] = back(d_query, query_unit, query_factor)
     d_key = sum_k[...]
@@ -348,6 +345,7 @@
     tokens_in,
     cot_in,
     bias,
+    turned_bias,
     raw,
     stage_pair,
     stage_one,
@@ -491,7 +489,7 @@
         (first_low, first_low_out),
         (place.at[:, pl.ds(0, rows)], tokens_turned_out),
         (place.at[:, pl.ds(0, rows)], first_turned_out),
-        (bias, bias_out),
+        (turned_bias, bias_out),
         (h_attn, d_two_out),
         (tokens_in.at[pl.ds(own_at, own_rows)], output_out),
         (first_low, d_shrunk_out),
@@ -508,7 +506,7 @@
 
         lax.fori_loop(0, total // size, one, 0)
 
-    def in_order():
+    def make_order():
         natural = place_row[...]
 
         def fill(at):
@@ -517,11 +515,9 @@
 
         chunks(D, LANES, fill)
 
-        def move(at):
-            tokens_in[at, :] = nn(tokens[at, :], place[...]).astype(BF16)
-
-        chunks(rows, 256, move)
-        result(0).start()
+    def tokens_in_order(number):
+        at = pl.ds(pl.multiple_of(number * 256, 256), 256)
+        tokens_in[at, :] = nn(tokens[at, :], place[...]).astype(BF16)
 
     def cot_in_order():
         cot_copy.wait()
@@ -545,7 +541,9 @@
                 key = lax.broadcasted_iota(jnp.int32, (length, LANES), 1) + tile * LANES
                 open_key = jnp.where(pad[:, lanes] == 0, segment[:, lanes], -1).astype(F32)
                 allowed = ((own_segment == open_key) & (key <= query)) | (key == query)
-                bias[sequence, :, lanes] = jnp.where(allowed, 0.0, MASKED)
+                values = jnp.where(allowed, 0.0, MASKED)
+                bias[sequence, :, lanes] = values
+                turned_bias[sequence, lanes, :] = values.T
         result(8).start()
 
     def finish():
@@ -710,18 +708,23 @@
         for hop in range(5):
             for_tiles(index, hop, plan, functools.partial(forward_hop, hop))
 
-        @pl.when(index == 0)
-        def _():
-            in_order()
-
         @pl.when(index == LAG - 1)
         def _():
             own.wait()
-            cot_in_order()
-
-        @pl.when(index == LAG)
-        def _():
-            make_bias()
+
+        order_at = ARRIVE - rows // 256
+
+        @pl.when(index == order_at - 1)
+        def _():
+            make_order()
+
+        @pl.when((index >= order_at) & (index < ARRIVE))
+        def _():
+            tokens_in_order(index - order_at)
+
+        @pl.when(index == ARRIVE)
+        def _():
+            result(0).start()
 
         pair = index - ARRIVE
 
@@ -732,6 +735,9 @@
         @pl.when(pair == 0)
         def _():
             one_copy(rare, 0).start()
+
+        @pl.when(pair == EVERY // 2)
+        def _():
             one_copy(rarer, 1).start()
 
         @pl.when((pair >= 1) & (pair <= 3 * heads // 2))
@@ -744,11 +750,22 @@
         @pl.when(pair == 1)
         def _():
             one_copy(0, 0).wait()
+            project(stage_one[0].reshape(D, LANES), pl.ds((3 * heads - 1) * LANES, LANES))
+
+        @pl.when(pair == EVERY // 2 + 1)
+        def _():
             one_copy(0, 1).wait()
-            project(stage_one[0].reshape(D, LANES), pl.ds((3 * heads - 1) * LANES, LANES))
             small_vectors()
 
-        @pl.when(pair == 2)
+        @pl.when(pair == 4)
+        def _():
+            cot_in_order()
+
+        @pl.when(pair == 5)
+        def _():
+            make_bias()
+
+        @pl.when(pair == 6)
         def _():
             turn(tokens_in)
             result(6).start()
@@ -800,7 +817,7 @@
     for k in (0, 1, 2, 4, 5, 8):
         result(k).wait()
     finish()
-    for route, (_, _, number, _) in enumerate(plan):
+    for route, (_, _, number, _, _) in enumerate(plan):
         for tile in range(max(0, number - RING), number):
             for hop in range(4):
                 piece(hop, route, tile).wait_send()
@@ -811,11 +828,11 @@
     rows = operands[1].shape[0]
     count = operands[5].shape[0]
     sequences, length = operands[7].shape
-    columns = sum(number for _, _, number, _ in plan) * LANES
+    columns = sum(entry[2] for entry in plan) * LANES
     own = count // 2
     heads = head_tiles() * LANES
     units = unit_tiles() * LANES
-    most = max(number for _, _, number, _ in plan)
+    most = max(entry[2] for entry in plan)
     place = (2, 2, 2, 2, rows)
     hbm = pl.BlockSpec(memory_space=pl.ANY)
     vmem = pl.BlockSpec(memory_space=pltpu.VMEM)
@@ -854,6 +871,7 @@
             pltpu.VMEM((count, D), BF16),
             pltpu.VMEM((own, D), BF16),
             pltpu.VMEM((sequences, length, length), F32),
+            pltpu.VMEM((sequences, length, length), F32),
             pltpu.VMEM((count, 3 * heads), F32),
             pltpu.VMEM((2, *place, 2 * LANES), BF16),
             pltpu.VMEM((2, *place, LANES), BF16),
@@ -889,6 +907,31 @@
 
 def backward_plan():
     return tile_plan((4 * head_tiles() + 3 * unit_tiles()) * LANES)
+
+
+def gradient_tile(route, tile):
+    heads, units = head_tiles(), unit_tiles()
+    shrink_steps, late = units // 2 - 1, units // 4
+    outward, up = 3 * heads, 4 * heads
+    gate, shrink = up + units, up + 2 * units
+    if route < 2:
+        unit = tile - shrink_steps + late
+        last = tile - shrink_steps - (units - late)
+        return jnp.where(
+            tile < shrink_steps,
+            shrink + 2 * tile + 2 + route,
+            jnp.where(
+                last < 0,
+                (up, gate)[route] + unit,
+                jnp.where(last < 2, outward + 2 * last + route, 2 * (last - 2) + route),
+            ),
+        )
+    of_unit = (up, gate)[route - 2] + tile - 1
+    if route == 2:
+        last = jnp.where(tile == late + 1, outward + heads - 1, outward - 2)
+    else:
+        last = jnp.where(tile == late + 1, outward - 3, outward - 1)
+    return jnp.where(tile == 0, shrink + route - 2, jnp.where(tile <= late, of_unit, last))
 
 
 def slot_of(route, tile):
@@ -1015,7 +1058,8 @@
         slot = slot_of(route, tile)
         total = work[hop - 1][slot, 0].astype(F32) + arrived[hop - 1][slot].astype(F32)
         if hop == 4:
-            grads[:, lanes_of(plan, route, tile)] = total
+            place = gradient_tile(route, tile)
+            grads[:, pl.ds(pl.multiple_of(place * LANES, LANES), LANES)] = total
             return
         half = total.shape[0] // 2
         free(hop, route, tile)
@@ -1064,8 +1108,9 @@
 
         which = jnp.where(is_expand | is_outward, 1, 0)
         scale = jnp.where(is_shrink | is_outward, 1.0, inv_root)
+        product = (nn(lefts[which], right[0]) * scale).astype(BF16)
         for quarter in range(4):
-            part = (nn(lefts[which, quarter_rows(quarter), :], right[0]) * scale).astype(BF16)
+            part = product[quarter_rows(quarter)]
             for route in (0, 1):
                 keep_quarter(
                     route, slot_of(route, tile), quarter, part[:, route * LANES : (route + 1) * LANES]
@@ -1073,38 +1118,37 @@
         for route in (0, 1):
             piece(0, route, tile).start()
 
-    def rare_product(tile):
+    def rare_product(route, tile):
         late = tile - rare_units
+        at = (route - 2) * LANES
+        lanes = slice(at, at + LANES)
 
         @pl.when(tile == 0)
         def _():
-            right[1] = stage_hidden[2]
+            right[1, :, lanes] = stage_hidden[2, :, lanes]
 
         @pl.when((tile > 0) & (late < 0))
         def _():
-            lanes = pl.ds(pl.multiple_of((tile - 1) * 2 * LANES, 2 * LANES), 2 * LANES)
-            right[1] = d_proj[:, lanes]
-
-        @pl.when(late == 0)
-        def _():
-            right[1, :, :LANES] = wide[:rows, (heads - 1) * LANES : heads * LANES]
-            right[1, :, LANES:] = wide[:rows, (heads + 12) * LANES : (heads + 13) * LANES]
-
-        @pl.when(late == 1)
-        def _():
-            right[1] = wide[:rows, (heads + 13) * LANES : (heads + 15) * LANES]
-
-        for route in (2, 3):
-            free(0, route, tile)
-            of_units = (tile > 0) & (late < 0)
-            of_outward = (late == 0) if route == 2 else (late < -rare_units)
-            which = jnp.where(of_units | of_outward, 1, 0)
-            scale = jnp.where((tile == 0) | of_outward, 1.0, inv_root)
-            at = (route - 2) * LANES
-            for quarter in range(4):
-                part = nn(lefts[which, quarter_rows(quarter), :], right[1, :, at : at + LANES])
-                keep_quarter(route, slot_of(route, tile), quarter, (part * scale).astype(BF16))
-            piece(0, route, tile).start()
+            unit_lane = pl.multiple_of((tile - 1) * 2 * LANES + at, LANES)
+            right[1, :, lanes] = d_proj[:, pl.ds(unit_lane, LANES)]
+
+        @pl.when(late >= 0)
+        def _():
+            if route == 2:
+                place = jnp.where(late == 0, heads - 1, heads + 13)
+            else:
+                place = heads + 12 + 2 * late
+            right[1, :, lanes] = wide[:rows, pl.ds(pl.multiple_of(place * LANES, LANES), LANES)]
+
+        free(0, route, tile)
+        of_units = (tile > 0) & (late < 0)
+        of_outward = (late == 0) if route == 2 else (late < -rare_units)
+        which = jnp.where(of_units | of_outward, 1, 0)
+        scale = jnp.where((tile == 0) | of_outward, 1.0, inv_root)
+        product = (nn(lefts[which], right[1, :, lanes]) * scale).astype(BF16)
+        for quarter in range(4):
+            keep_quarter(route, slot_of(route, tile), quarter, product[quarter_rows(quarter)])
+        piece(0, route, tile).start()
 
 
     def unit_copies(pair):
@@ -1143,18 +1187,19 @@
         slot = pair % 2
         for part in unit_copies(pair):
             part.wait()
-        at = pl.multiple_of(slot * 6 * LANES, 2 * LANES)
-        expand = wide[:, pl.ds(at, 4 * LANES)]
-        down = wide[:, pl.ds(pl.multiple_of(at + 4 * LANES, 2 * LANES), 2 * LANES)]
-
-        def some(row_at, row_from, proj_lanes):
-            d_hidden = nn(d_low[row_at, :], down)
+        at_lane = pl.multiple_of(slot * 6 * LANES, 2 * LANES)
+        down = wide[:, pl.ds(pl.multiple_of(at_lane + 4 * LANES, 2 * LANES), 2 * LANES)]
+
+        for half in range(2):
+            at = slice(half * own_rows, (half + 1) * own_rows)
+            proj_lanes = half * 4 * LANES
+            d_hidden = nn(d_low[at, :], down)
             for k in range(2):
                 lanes = pl.ds(pl.multiple_of((2 * pair + k) * LANES, LANES), LANES)
                 gain_up, gain_gate = gains[0:1, lanes], gains[1:2, lanes]
                 start = proj_lanes + 2 * k * LANES
-                proj_up = stage_rows[slot, row_from, start : start + LANES]
-                proj_gate = stage_rows[slot, row_from, start + LANES : start + 2 * LANES]
+                proj_up = stage_rows[slot, :, start : start + LANES]
+                proj_gate = stage_rows[slot, :, start + LANES : start + 2 * LANES]
                 upstream = d_hidden[:, k * LANES : (k + 1) * LANES]
                 gate = gain_gate * proj_gate
                 sigmoid = jax.nn.sigmoid(gate)
@@ -1162,24 +1207,17 @@
                 d_gate = upstream * (gain_up * proj_up) * sigmoid * (1.0 + gate * (1.0 - sigmoid))
                 unit_grad[0:1, lanes] += jnp.sum(d_up * proj_up, axis=0, keepdims=True)
                 unit_grad[1:2, lanes] += jnp.sum(d_gate * proj_gate, axis=0, keepdims=True)
-                at = pl.multiple_of((2 * pair + k) * 2 * LANES, 2 * LANES)
-                d_proj[row_at, pl.ds(at, LANES)] = (d_up * gain_up).astype(BF16)
-                d_proj[row_at, pl.ds(pl.multiple_of(at + LANES, LANES), LANES)] = (
+                place = pl.multiple_of((2 * pair + k) * 2 * LANES, 2 * LANES)
+                d_proj[at, pl.ds(place, LANES)] = (d_up * gain_up).astype(BF16)
+                d_proj[at, pl.ds(pl.multiple_of(place + LANES, LANES), LANES)] = (
                     d_gate * gain_gate
                 ).astype(BF16)
-            lanes = pl.ds(pl.multiple_of(pair * 4 * LANES, 4 * LANES), 4 * LANES)
-            first_part[row_at, :] += nt(d_proj[row_at, lanes], expand)
-
-        size = own_rows // 2
-        for half in range(2):
-
-            def one(k, _, half=half):
-                row_from = pl.multiple_of(k * size, size)
-                row_at = pl.multiple_of(half * own_rows + row_from, size)
-                some(pl.ds(row_at, size), pl.ds(row_from, size), half * 4 * LANES)
-                return 0
-
-            lax.fori_loop(0, 2, one, 0)
+        expand_at = pl.ds(at_lane, 4 * LANES)
+        lanes = pl.ds(pl.multiple_of(pair * 4 * LANES, 4 * LANES), 4 * LANES)
+        upstream = d_proj[:, lanes]
+        for k in range(D // 256):
+            columns = slice(k * 256, (k + 1) * 256)
+            first_part[:, columns] += nt(upstream, wide[columns, expand_at])
 
 
     def core_copy(source, target, which):
@@ -1491,9 +1529,13 @@
         def _():
             often_product(index)
 
-        @pl.when((index % EVERY == 0) & (index < plan[2][2] * EVERY))
-        def _():
-            rare_product(index // EVERY)
+        for route in (2, 3):
+            number, start = plan[route][2], plan[route][4]
+            due = index - start
+
+            @pl.when((due % EVERY == 0) & (due >= 0) & (due < number * EVERY))
+            def _(route=route, due=due):
+                rare_product(route, due // EVERY)
 
         @pl.when(index + 1 < shrink_steps)
         def _():
@@ -1582,7 +1624,7 @@
         part.wait()
     for k in range(2):
         input_copy(k).wait()
-    for route, (_, _, number, _) in enumerate(plan):
+    for route, (_, _, number, _, _) in enumerate(plan):
         for tile in range(max(0, number - ring_of(route)), number):
             for hop in range(4):
                 piece(hop, route, tile).wait_send()
@@ -1649,77 +1691,170 @@
     )(*operands)
 
 
-def sum_kernel(values, total, sums, arrived, send_sem, recv_sem):
+UPDATE_STEPS = 5
+SQUARE_ROWS = 8
+
+
+def update_parts(refs):
+    grads, states = refs[:7], [refs[7 + 3 * k : 10 + 3 * k] for k in range(4)]
+    pieces = [(0, 0), (0, 1), (0, 2), (1, None), (2, 0), (2, 1), (3, None)]
+    return [
+        (grad[...], *[ref[...] if at is None else ref[at] for ref in states[which]])
+        for grad, (which, at) in zip(grads, pieces)
+    ]
+
+
+def squares_kernel(*refs):
+    inputs, (total, sums, arrived, send_sem, recv_sem) = refs[:19], refs[19:]
+    index = pl.program_id(0)
     me = lax.axis_index("dp")
-    greet(me)
-    sums[0] = values[...]
-    for k, bit in enumerate(PLACES):
-        copy = pltpu.make_async_remote_copy(
-            src_ref=sums.at[k],
-            dst_ref=arrived.at[k],
-            send_sem=send_sem.at[k],
-            recv_sem=recv_sem.at[k],
-            device_id={"dp": partner_of(me, bit)},
-            device_id_type=pl.DeviceIdType.MESH,
-        )
-        copy.start()
-        copy.wait()
-        if k + 1 < len(PLACES):
-            sums[k + 1] = sums[k] + arrived[k]
-        else:
-            total[...] = sums[k] + arrived[k]
-
-
-def sum_all(values, count, collective_id):
-    for bit in extra_bits(count):
-        values = values + exchange(values, bit, count)
-    vmem = pl.BlockSpec(memory_space=pltpu.VMEM)
-    hops = len(PLACES)
-    return pl.pallas_call(
-        sum_kernel,
-        out_shape=jax.ShapeDtypeStruct(values.shape, F32),
-        in_specs=[vmem],
-        out_specs=vmem,
+    planes = (PLACES[:2], PLACES[2:])
+    hops = [
+        [(low,), (high,), (low, high)] for low, high in planes
+    ]
+
+    def partner(bits):
+        device = me
+        for bit in bits:
+            device = device + partner_of(me, bit) - me
+        return {"dp": device}
+
+    @pl.when(index == 0)
+    def _():
+        barrier = pltpu.get_barrier_semaphore()
+        for hop in hops:
+            for bits in hop:
+                pl.semaphore_signal(
+                    barrier, inc=1, device_id=partner(bits), device_id_type=pl.DeviceIdType.MESH
+                )
+        pl.semaphore_wait(barrier, 6)
+        sums[...] = jnp.zeros_like(sums)
+
+    heads = head_tiles()
+    places = [(0, k * heads) for k in range(4)] + [(1, 0), (2, 0), (3, 0)]
+    for (at, start), (gradient, master, first, second) in zip(places, update_parts(inputs)):
+        pre = adam_step(master, first, second, gradient, RATE_MATRIX)[0]
+        row = jnp.sum(pre * pre, axis=0, keepdims=True)
+        width = row.shape[1]
+        lanes = pl.ds(pl.multiple_of(start * LANES + index * width, LANES), width)
+        sums[0, at : at + 1, lanes] = row
+
+    @pl.when(index == UPDATE_STEPS - 1)
+    def _():
+        for number, hop in enumerate(hops):
+            copies = [
+                pltpu.make_async_remote_copy(
+                    src_ref=sums.at[number],
+                    dst_ref=arrived.at[number, k],
+                    send_sem=send_sem.at[number, k],
+                    recv_sem=recv_sem.at[number, k],
+                    device_id=partner(bits),
+                    device_id_type=pl.DeviceIdType.MESH,
+                )
+                for k, bits in enumerate(hop)
+            ]
+            for copy in copies:
+                copy.start()
+            for copy in copies:
+                copy.wait()
+            result = (sums[number] + arrived[number, 0]) + (
+                arrived[number, 1] + arrived[number, 2]
+            )
+            if number == 0:
+                sums[1] = result
+            else:
+                total[...] = result
+
+
+def update_kernel(*refs):
+    inputs, squares, small, outputs = refs[:19], refs[19:26], refs[26:34], refs[34:]
+    results, small_results = outputs[:12], outputs[12:]
+    index = pl.program_id(0)
+    places = [(0, 0), (0, 1), (0, 2), (1, None), (2, 0), (2, 1), (3, None)]
+    for number, (gradient, master, first, second) in enumerate(update_parts(inputs)):
+        pre, variance = adam_step(master, first, second, gradient, RATE_MATRIX)
+        row = max(0, number - 3)
+        factor = lax.rsqrt(squares[number][row : row + 1, :] / D + EPS_NORM)
+        which, at = places[number]
+        for target, value in zip(results[3 * which : 3 * which + 3], (gradient, variance, pre * factor)):
+            if at is None:
+                target[...] = value
+            else:
+                target[at] = value
+
+    @pl.when(index == 0)
+    def _():
+        for k, rate in enumerate((RATE_ALPHA, RATE_SCALE)):
+            gradient, master, first, second = [ref[...] for ref in small[4 * k : 4 * k + 4]]
+            updated, variance = adam_step(master, first, second, gradient, rate)
+            for target, value in zip(
+                small_results[3 * k : 3 * k + 3], (gradient, variance, updated)
+            ):
+                target[...] = value
+
+
+def update_specs(rows):
+    heads, units = head_tiles(), unit_tiles()
+    wide = units // UPDATE_STEPS * LANES
+
+    def columns(width, start):
+        return pl.BlockSpec((rows, width), lambda i: (0, start + i))
+
+    grads = [columns(LANES, k * heads) for k in range(4)]
+    grads += [columns(wide, (4 * heads + k * units) * LANES // wide) for k in range(3)]
+    inward = pl.BlockSpec((3, rows, LANES), lambda i: (0, 0, i))
+    outward = pl.BlockSpec((rows, LANES), lambda i: (0, i))
+    expand = pl.BlockSpec((2, rows, wide), lambda i: (0, 0, i))
+    shrink = pl.BlockSpec((rows, wide), lambda i: (0, i))
+    states = [inward] * 3 + [outward] * 3 + [expand] * 3 + [shrink] * 3
+    squares = [
+        pl.BlockSpec((SQUARE_ROWS, LANES), lambda i, k=k: (0, k * heads + i)) for k in range(4)
+    ]
+    squares += [pl.BlockSpec((SQUARE_ROWS, wide), lambda i: (0, i))] * 3
+    return grads, states, squares
+
+
+def update(grads, states, small, count, collective_id):
+    rows = grads.shape[0]
+    grad_specs, state_specs, square_specs = update_specs(rows)
+    units = unit_tiles() * LANES
+    shape = (SQUARE_ROWS, units)
+    squares = pl.pallas_call(
+        squares_kernel,
+        grid=(UPDATE_STEPS,),
+        out_shape=jax.ShapeDtypeStruct(shape, F32),
+        in_specs=grad_specs + state_specs,
+        out_specs=pl.BlockSpec(shape, lambda i: (0, 0)),
         scratch_shapes=[
-            pltpu.VMEM((hops, *values.shape), F32),
-            pltpu.VMEM((hops, *values.shape), F32),
-            pltpu.SemaphoreType.DMA((hops,)),
-            pltpu.SemaphoreType.DMA((hops,)),
+            pltpu.VMEM((2, *shape), F32),
+            pltpu.VMEM((2, 3, *shape), F32),
+            pltpu.SemaphoreType.DMA((2, 3)),
+            pltpu.SemaphoreType.DMA((2, 3)),
         ],
         compiler_params=pltpu.CompilerParams(
-            collective_id=collective_id, has_side_effects=True, vmem_limit_bytes=16 << 20
+            collective_id=collective_id, has_side_effects=True, vmem_limit_bytes=60 << 20
         ),
-        name="sum_all",
-    )(values)
-
-
-def columns_of(grads):
-    plan = backward_plan()
-    rows = grads.shape[0]
-    heads, units = head_tiles(), unit_tiles()
-    shrink_steps, late = units // 2 - 1, units // 4
-    rare, rarer = plan[2][0], plan[3][0]
-
-    def tiles(start, number):
-        return grads[:, start * LANES : (start + number) * LANES]
-
-    attention_at = 2 * (shrink_steps + units - late)
-    pairs = tiles(2 * shrink_steps, 2 * (units - late)).reshape(rows, units - late, 2, LANES)
-    shrink = jnp.concatenate([tiles(rare, 1), tiles(rarer, 1), tiles(0, 2 * shrink_steps)], axis=1)
-    up = jnp.concatenate([tiles(rare + 1, late), pairs[:, :, 0].reshape(rows, -1)], axis=1)
-    gate = jnp.concatenate([tiles(rarer + 1, late), pairs[:, :, 1].reshape(rows, -1)], axis=1)
-    last = late + 1
-    outward = jnp.concatenate([tiles(attention_at, 4), tiles(rare + last, 1)], axis=1)
-    inward = jnp.concatenate(
-        [
-            tiles(attention_at + 4, 12),
-            tiles(rarer + last, 1),
-            tiles(rare + last + 1, 1),
-            tiles(rarer + last + 1, 1),
-        ],
-        axis=1,
-    )
-    return inward, outward, up, gate, shrink
+        name="sum_squares",
+    )(*[grads] * 7, *states)
+    for bit in extra_bits(count):
+        squares = squares + exchange(squares, bit, count)
+    out_shape = [
+        jax.ShapeDtypeStruct(states[3 * k].shape, F32) for k in range(4) for _ in range(3)
+    ]
+    out_shape += [jax.ShapeDtypeStruct(small[4 * k].shape, F32) for k in range(2) for _ in range(3)]
+
+    def whole(array):
+        return pl.BlockSpec(array.shape, lambda i: (0, 0))
+
+    return pl.pallas_call(
+        update_kernel,
+        grid=(UPDATE_STEPS,),
+        out_shape=out_shape,
+        in_specs=grad_specs + state_specs + square_specs + [whole(array) for array in small],
+        out_specs=state_specs + [whole(small[4 * k]) for k in range(2) for _ in range(3)],
+        compiler_params=pltpu.CompilerParams(vmem_limit_bytes=60 << 20),
+        name="update",
+    )(*[grads] * 7, *states, *[squares] * 7, *small)
 
 
 def per_device(
@@ -1754,9 +1889,9 @@
     small = jnp.pad(small, ((0, LANES - small.shape[0]), (0, 0))).T
     masters = (
         inward_master,
-        outward_master.astype(BF16).T,
+        outward_master.T,
         expand_master,
-        shrink_master.astype(BF16).T,
+        shrink_master.T,
         small,
     )
     if extra_bits(count):
@@ -1813,73 +1948,40 @@
         collective_id=1,
     )
     grads = scatter_rest(grads, count)
-    inward_grad, outward_grad, up_grad, gate_grad, shrink_grad = columns_of(grads)
     for bit in extra_bits(count):
         vectors = vectors + exchange(vectors, bit, count)
     width = D // count
     vectors = lax.dynamic_slice_in_dim(vectors, me * width, width, 1)
     alpha_grad, scale_grad = vectors[:2], vectors[2 : 2 + scale_master.shape[0]]
 
-    outward_grad = outward_grad.T
-    shrink_grad = shrink_grad.T
-    expand_grad = jnp.stack([up_grad, gate_grad])
-    inward_grad = jnp.stack(
-        [inward_grad[:, k * heads_width : (k + 1) * heads_width] for k in range(3)]
+    states = (
+        inward_master,
+        inward_first,
+        inward_second,
+        outward_master.T,
+        outward_first.T,
+        outward_second.T,
+        expand_master,
+        expand_first,
+        expand_second,
+        shrink_master.T,
+        shrink_first.T,
+        shrink_second.T,
     )
-    inward_pre, inward_var = adam_step(
-        inward_master, inward_first, inward_second, inward_grad, RATE_MATRIX
+    small = (
+        alpha_grad,
+        alpha_master,
+        alpha_first,
+        alpha_second,
+        scale_grad,
+        scale_master,
+        scale_first,
+        scale_second,
     )
-    outward_pre, outward_var = adam_step(
-        outward_master, outward_first, outward_second, outward_grad, RATE_MATRIX
-    )
-    expand_pre, expand_var = adam_step(
-        expand_master, expand_first, expand_second, expand_grad, RATE_MATRIX
-    )
-    shrink_pre, shrink_var = adam_step(
-        shrink_master, shrink_first, shrink_second, shrink_grad, RATE_MATRIX
-    )
-    alpha_new, alpha_var = adam_step(
-        alpha_master, alpha_first, alpha_second, alpha_grad, RATE_ALPHA
-    )
-    scale_new, scale_var = adam_step(
-        scale_master, scale_first, scale_second, scale_grad, RATE_SCALE
-    )
-
-    squares = [
-        jnp.sum(pre * pre, axis=axis).reshape(-1)
-        for pre, axis in ((inward_pre, 1), (outward_pre, 1), (expand_pre, 1), (shrink_pre, 1))
-    ]
-    sizes = [square.shape[0] for square in squares]
-    squares = sum_all(jnp.concatenate(squares).reshape(8, -1), count, 2).reshape(-1)
-    ends = np.cumsum(sizes)
-
-    def renormed(pre, axis, which):
-        mean = squares[int(ends[which]) - sizes[which] : int(ends[which])] / D
-        kept = [size for k, size in enumerate(pre.shape) if k != axis]
-        return pre * jnp.expand_dims(lax.rsqrt(mean + EPS_NORM).reshape(kept), axis)
-
-    return (
-        block_output,
-        input_grad,
-        inward_grad,
-        inward_var,
-        renormed(inward_pre, 1, 0),
-        outward_grad,
-        outward_var,
-        renormed(outward_pre, 1, 1),
-        expand_grad,
-        expand_var,
-        renormed(expand_pre, 1, 2),
-        shrink_grad,
-        shrink_var,
-        renormed(shrink_pre, 1, 3),
-        alpha_grad,
-        alpha_var,
-        alpha_new,
-        scale_grad,
-        scale_var,
-        scale_new,
-    )
+    results = list(update(grads, states, small, count, 2))
+    for k in (*range(3, 6), *range(9, 12)):
+        results[k] = results[k].T
+    return block_output, input_grad, *results
 
 
 def solution(mesh):

time: 563 us -> 501 us (0.89)
  Pallas kernels: 516 us -> 489 us
  other arithmetic: 21.4 us -> 2.11 us
  local copies, waits for them, and re-layouts: 21.2 us -> 8.24 us
    pallas_call x1, Pallas kernels: 253 us -> 217 us  [backward_pass(): pl.pallas_call(functools.partial(backward_kernel, plan), out_shape=[jax.S...]
    pallas_call x1 -> x2, Pallas kernels: 15 us -> 32.3 us  [the longest x1 20.6 us: update(): pl.pallas_call(squares_kernel, grid=(UPDATE_STEPS,), out_shape=jax.ShapeD...]
    slice x8 -> x2, local copies, waits for them, and re-layouts: 11.6 us -> 2.73 us  [per_device(): alpha_grad, scale_grad = (vectors[:2], vectors[2:2 + scale_master.shape[0]])]
    reduce_sum x4 -> x0, other arithmetic: 8.84 us -> none  [per_device(): jnp.sum(pre * pre, axis=axis).reshape(-1)]
    pallas_call x1, Pallas kernels: 248 us -> 240 us  [forward_pass(): pl.pallas_call(functools.partial(forward_kernel, plan), out_shape=[jax.Sh...]
where the time goes in v4:
time: 501 us; the launch traced here: 500 us
  Pallas kernels  489 us (98%)
  local copies, waits for them, and re-layouts  8.24 us (2%)
    pallas_call x1, Pallas kernels, forward_pass(): pl.pallas_call(functools.partial(forward_kernel, plan), out_shape=[jax.Sh...  240 us
    pallas_call x1, Pallas kernels, backward_pass(): pl.pallas_call(functools.partial(backward_kernel, plan), out_shape=[jax.S...  217 us
    pallas_call x1, Pallas kernels, update(): pl.pallas_call(squares_kernel, grid=(UPDATE_STEPS,), out_shape=jax.ShapeD...  20.6 us
    pallas_call x1, Pallas kernels, update(): pl.pallas_call(update_kernel, grid=(UPDATE_STEPS,), out_shape=out_shape,...  11.7 us

profile of v4, /device:TPU:0, one launch (start us, length us, event | category | flops | bytes accessed | tf_op | source)
XLA Modules:
  0.0 500.3 jit_solution(8447683493711788708)
XLA Ops:
  0.7 0.7 multiply_add_fusion
  1.4 0.6 broadcast_in_dim.3.place_row
  2.0 0.7 convert.7
  2.7 0.7 convert.6
  3.4 0.1 copy.46
  3.5 0.6 pad_bitcast_fusion.small_copies
  4.1 240.3 %forward_pass.1 = (bf16[2,2,2,2,80,10496]{5,4,3,2,1,0:T(8,128)(2,1)}, bf16[1024,1280]{1,0:T(8,128)(2,1)}, f32[1024,1920]{1,0:T(8,128)}, bf16[1024,640]{1,0:T(8,1...) custom-call(f32[3,80,640]{2,1,0:T(8,128)} %refs_7_.3, ...), custom_call_target="tpu_custom_call" | custom-call | tf_op jit(solution)/shard_map/forward_pass/pallas_call | solution.py:840
  244.4 216.6 %backward_pass.1 = (f32[1024,640]{1,0:T(8,128)}, bf16[1024,1280]{1,0:T(8,128)(2,1)}, f32[80,10240]{1,0:T(8,128)}, f32[16,1280]{1,0:T(8,128)}) custom-call(bf16[1280,10496]{1,0:T(8,128)(2,1)} %bitcast.15, bf16[1024,1280]{1,0:T(8,128)(2,1)} %get-tuple-element.63.d_shrunk, bf16[1280,1024]{1,0:T(8,128)(2,1)} %get-tuple-element.64.d_shrunk_turned, ...), custom_call_target="tpu_custom_call" | custom-call | tf_op jit(solution)/shard_map/backward_pass/pallas_call | solution.py:1646
  461.1 20.6 %sum_squares.1.refs_19_.refs_20_.refs_21_.refs_22_.refs_23_.refs_24_.refs_25_ = f32[8,2560]{1,0:T(8,128)} custom-call(f32[80,10240]{1,0:T(8,128)} %get-tuple-element.84.refs_0_.refs_1_.refs_2_.refs_3_.refs_4_.refs_5_.refs_6_, f32[80,10240]{1,0:T(8,128)} %get-tuple-element.84.refs_0_.refs_1_.refs_2_.refs_3_.refs_4_.refs_5_.refs_6_, ...), custom_call_target="tpu_custom_call" | custom-call | tf_op jit(solution)/shard_map/sum_squares/pallas_call | solution.py:1822
  481.7 1.4 dynamic-slice.1.refs_30_
  483.1 1.3 constant_dynamic-slice_fusion.refs_26_
  484.4 0.0 copy-start.1
  484.4 11.7 %update.1 = (f32[3,80,640]{2,1,0:T(8,128)}, f32[3,80,640]{2,1,0:T(8,128)}, f32[3,80,640]{2,1,0:T(8,128)}, f32[80,640]{1,0:T(8,128)}, f32[80,640]{1,0:T(8,128)}, ...) custom-call(f32[80,10240]{1,0:T(8,128)} %get-tuple-element.84.refs_0, ...), custom_call_target="tpu_custom_call" | custom-call | tf_op jit(solution)/shard_map/update/pallas_call | solution.py:1849
  496.2 0.0 copy-done.1
  496.2 0.0 copy-start
  496.2 1.5 copy.49
  497.7 1.2 copy-done
  498.9 1.5 copy.50
  (1 shorter events, 0.0 us)
Async XLA Ops:
  484.4 11.7 %copy-start.1 = (bf16[1024,1280]{1,0:T(8,128)(2,1)S(1)}, bf16[1024,1280]{1,0:T(8,128)(2,1)}, u32[]{:S(2)}) copy-start(bf16[1024,1280]{1,0:T(8,128)(2,1)} %get-tuple-element.124) | copy-start | bytes 7864324
  496.2 2.7 copy-start

commit v5 on v4

--- a/solution.py
+++ b/solution.py
@@ -40,12 +40,9 @@
 def adam_step(master, first_moment, second_moment, gradient, rate):
     first_new = BETA_ONE * first_moment.astype(F32) + (1.0 - BETA_ONE) * gradient
     second_new = BETA_TWO * second_moment + (1.0 - BETA_TWO) * gradient * gradient
-    ratio = (
-        first_new
-        / (1.0 - BETA_ONE**STEP)
-        / (jnp.sqrt(second_new / (1.0 - BETA_TWO**STEP)) + ADAM_EPS)
-    )
-    return (master - rate * ratio, second_new)
+    root = jnp.sqrt(second_new * (1.0 / (1.0 - BETA_TWO**STEP)))
+    ratio = first_new * (rate / (1.0 - BETA_ONE**STEP)) / (root + ADAM_EPS)
+    return (master - ratio, second_new)
 
 
 LANES = 128
@@ -126,7 +123,7 @@
     return partial
 
 
-def place_row_of(me, count):
+def place_rows_of(count):
     places = list(PLACES) + extra_bits(count)
     width = D // count
     placed = np.arange(D, dtype=np.int32)
@@ -134,7 +131,12 @@
     relative = np.zeros_like(position)
     for axis, bit in enumerate(places):
         relative = relative + ((position >> (len(places) - 1 - axis)) & 1) * bit
-    return ((jnp.asarray(relative) ^ me) * width + jnp.asarray(offset))[None]
+    return np.stack([relative, offset])
+
+
+def natural_row(place_row, me):
+    count = lax.axis_size("dp")
+    return (place_row[0:1, :] ^ me) * (D // count) + place_row[1:2, :]
 
 
 def nn(a, b):
@@ -357,6 +359,7 @@
     first_low,
     stage_proj,
     stage_hidden,
+    keep,
     own_sem,
     send_sem,
     recv_sem,
@@ -438,11 +441,15 @@
         lanes = pl.ds(pl.multiple_of(tile * LANES, LANES), width * LANES)
         return pltpu.make_async_copy(out.at[:, :, :, :, :, lanes], target, sem)
 
+    def lanes_half(number):
+        return pl.ds(pl.multiple_of((number % 2) * LANES, LANES), LANES)
+
     def pair_copy(tile, slot):
         return staged(tile, 2, stage_pair.at[slot], pair_sem.at[slot])
 
-    def one_copy(tile, slot):
-        return staged(tile, 1, stage_one.at[slot], one_sem.at[slot])
+    def one_copy(tile, number):
+        target = stage_one.at[(number // 2) % 2, :, :, :, :, :, lanes_half(number)]
+        return staged(tile, 1, target, one_sem.at[number % 2])
 
     rare = plan[2][0]
     rarer = plan[3][0]
@@ -473,12 +480,15 @@
             first_low.at[pl.ds(own_at, own_rows)], first_low.at[pl.ds(own_at, own_rows)], 1
         )
 
-    def shrunk_copy():
-        return core_copy(shrunk.at[pl.ds(other_at, own_rows)], branch_in, 2)
-
-    def d_shrunk_copy():
-        own = first_low.at[pl.ds(own_at, own_rows)]
-        return core_copy(own, own, 3)
+    half_rows = own_rows // 2
+
+    def shrunk_copy(k):
+        source = pl.ds(pl.multiple_of(other_at + k * half_rows, half_rows), half_rows)
+        return core_copy(shrunk.at[source], branch_in.at[pl.ds(k * half_rows, half_rows)], 2 + k)
+
+    def d_shrunk_copy(k):
+        at = pl.ds(pl.multiple_of(own_at + k * half_rows, half_rows), half_rows)
+        return core_copy(first_low.at[at], first_low.at[at], 4 + k)
 
     result_pairs = (
         (tokens_in, tokens_out),
@@ -507,7 +517,7 @@
         lax.fori_loop(0, total // size, one, 0)
 
     def make_order():
-        natural = place_row[...]
+        natural = natural_row(place_row, me)
 
         def fill(at):
             here = lax.broadcasted_iota(jnp.int32, (LANES, D), 0) + at.start
@@ -545,47 +555,52 @@
                 bias[sequence, :, lanes] = values
                 turned_bias[sequence, lanes, :] = values.T
         result(8).start()
+        keep[...] = jnp.where(core == 0, column_of(1 - pads[0:1, :]), column_of(1 - pads[1:2, :]))
 
     def finish():
-        shrunk_copy().start()
-        result(3).wait()
-        keep = jnp.where(
-            core == 0, column_of(1 - pads[0:1, :]), column_of(1 - pads[1:2, :])
-        )
-        stage_proj[0, :own_rows, :LANES] = keep
         alpha = alphas[1:2, :]
         alpha_grad[...] = jnp.zeros_like(alpha_grad)
-        shrunk_copy().wait()
 
         def some(at):
             here = pl.ds(pl.multiple_of(own_at + at.start, 64), 64)
             normed, factor = row_norm(shrunk[here, :] + branch_in[at, :])
             start = first[at, :]
             output, output_factor = row_norm(start + alpha * (normed - start))
-            upstream = cot_in[at, :].astype(F32) * stage_proj[0, at, 0:1]
+            upstream = cot_in[at, :].astype(F32) * keep[at, 0:1]
             d_two = row_norm_back(upstream, output, output_factor)
             alpha_grad[0:1, :] += jnp.sum(d_two * (normed - start), axis=0, keepdims=True)
             h_attn[at, :] = d_two
             tokens_in[here, :] = output.astype(BF16)
             first_low[here, :] = row_norm_back(alpha * d_two, normed, factor).astype(BF16)
 
-        chunks(own_rows, 64, some)
-        d_shrunk_copy().start()
+        def span(k, size, start, body):
+            def one(j, _):
+                body(pl.ds(pl.multiple_of(start + k * half_rows + j * size, size), size))
+                return 0
+
+            lax.fori_loop(0, half_rows // size, one, 0)
+
+        for k in range(2):
+            shrunk_copy(k).wait()
+            span(k, 64, 0, some)
+            d_shrunk_copy(k).start()
         result(9).start()
         result(10).start()
-        result(7).wait()
-        d_shrunk_copy().wait()
+        for k in range(2):
+            span(k, LANES, own_at, lambda at: turn_rows(first_low, at))
+        for k in range(2):
+            d_shrunk_copy(k).wait()
+            span(k, LANES, other_at, lambda at: turn_rows(first_low, at))
+        result(12).start()
         result(11).start()
-        turn(first_low)
-        result(12).start()
         for k in (9, 10, 11, 12):
             result(k).wait()
 
+    def turn_rows(source, at):
+        place[:, at] = source[at, :].astype(F32).T.astype(BF16)
+
     def turn(source):
-        def some(at):
-            place[:, at] = source[at, :].astype(F32).T.astype(BF16)
-
-        chunks(rows, LANES, some)
+        chunks(rows, LANES, functools.partial(turn_rows, source))
 
     def project(weights, lanes):
         def some(at):
@@ -594,7 +609,7 @@
         chunks(rows, 256, some)
 
     def small_vectors():
-        small = stage_one[1].reshape(D, LANES).astype(F32).T
+        small = stage_one[0, :, :, :, :, :, LANES:].reshape(D, LANES).astype(F32).T
         alphas[...] = small[: alphas.shape[0]]
         scales[...] = nt(small.astype(BF16), place[...])[: scales.shape[0]]
         each = units * LANES // D
@@ -660,19 +675,38 @@
         slot = unit % 2
         return pltpu.make_async_copy(stage_proj.at[slot], proj_out.at[:, lanes], proj_sem.at[slot])
 
-    def hidden_copy(unit):
-        lanes = pl.ds(pl.multiple_of(unit * LANES, LANES), LANES)
-        slot = unit % 2
+    def hidden_copy(pair):
+        lanes = pl.ds(pl.multiple_of(pair * 2 * LANES, 2 * LANES), 2 * LANES)
+        slot = pair % 2
         return pltpu.make_async_copy(
             stage_hidden.at[slot], hidden_out.at[:, lanes], hidden_sem.at[slot]
         )
 
     def fetch_unit(unit):
         pair_copy(pair_tile(unit), unit % 2).start()
-        one_copy(shrink_tile(unit), unit % 2).start()
+        one_copy(shrink_tile(unit), unit).start()
+
+    def add_shrunk(pair):
+        down = stage_one[pair % 2].reshape(D, 2 * LANES)
+        for part, start in enumerate((other_at, own_at)):
+            at = pl.ds(start, own_rows)
+            values = stage_hidden[pair % 2, at, :]
+            for k in range(D // 256):
+                columns = slice(k * 256, (k + 1) * 256)
+                shrunk[at, columns] += nt(values, down[columns])
+            if part == 0:
+
+                @pl.when(pair == units // 2 - 1)
+                def _():
+                    result(5).wait()
+                    for k in range(2):
+                        shrunk_copy(k).start()
+
+        hidden_copy(pair).start()
 
     def one_unit(unit):
         slot = unit % 2
+        pair = unit // 2
 
         @pl.when(unit == 0)
         def _():
@@ -683,12 +717,14 @@
         @pl.when(unit >= 2)
         def _():
             proj_copy(unit - 2).wait()
-            hidden_copy(unit - 2).wait()
+
+        @pl.when((unit >= 4) & (slot == 0))
+        def _():
+            hidden_copy(pair - 2).wait()
 
         pair_copy(0, slot).wait()
-        one_copy(0, slot).wait()
+        one_copy(0, unit).wait()
         weights = stage_pair[slot].reshape(D, 2 * LANES)
-        down = stage_one[slot].reshape(D, LANES)
         gain_up = gain_of(unit, 0)
         gain_gate = gain_of(unit, 1)
 
@@ -697,12 +733,14 @@
             stage_proj[slot, at, :] = proj
             gate = gain_gate * proj[:, LANES:]
             hidden = (gain_up * proj[:, :LANES] * (gate * jax.nn.sigmoid(gate))).astype(BF16)
-            stage_hidden[slot, at, :] = hidden
-            shrunk[at, :] += nt(hidden, down)
-
-        chunks(rows, 256, some)
+            stage_hidden[pair % 2, at, lanes_half(unit)] = hidden
+
+        chunks(rows, own_rows, some)
         proj_copy(unit).start()
-        hidden_copy(unit).start()
+
+        @pl.when(slot == 1)
+        def _():
+            add_shrunk(pair)
 
     def step(index, _):
         for hop in range(5):
@@ -750,7 +788,8 @@
         @pl.when(pair == 1)
         def _():
             one_copy(0, 0).wait()
-            project(stage_one[0].reshape(D, LANES), pl.ds((3 * heads - 1) * LANES, LANES))
+            weights = stage_one[0, :, :, :, :, :, :LANES].reshape(D, LANES)
+            project(weights, pl.ds((3 * heads - 1) * LANES, LANES))
 
         @pl.when(pair == EVERY // 2 + 1)
         def _():
@@ -813,8 +852,9 @@
     lax.fori_loop(0, max(steps_of(plan, 4), units_at + units), step, 0)
     for unit in (units - 2, units - 1):
         proj_copy(unit).wait()
-        hidden_copy(unit).wait()
-    for k in (0, 1, 2, 4, 5, 8):
+    for pair in (units // 2 - 2, units // 2 - 1):
+        hidden_copy(pair).wait()
+    for k in (0, 1, 2, 3, 4, 7, 8):
         result(k).wait()
     finish()
     for route, (_, _, number, _, _) in enumerate(plan):
@@ -874,7 +914,7 @@
             pltpu.VMEM((sequences, length, length), F32),
             pltpu.VMEM((count, 3 * heads), F32),
             pltpu.VMEM((2, *place, 2 * LANES), BF16),
-            pltpu.VMEM((2, *place, LANES), BF16),
+            pltpu.VMEM((2, *place, 2 * LANES), BF16),
             pltpu.VMEM((*place, heads), BF16),
             pltpu.VMEM((count, heads), BF16),
             pltpu.VMEM((own, D), F32),
@@ -882,7 +922,8 @@
             pltpu.VMEM((own, D), F32),
             pltpu.VMEM((count, D), BF16),
             pltpu.VMEM((2, count, 2 * LANES), F32),
-            pltpu.VMEM((2, count, LANES), BF16),
+            pltpu.VMEM((2, count, 2 * LANES), BF16),
+            pltpu.VMEM((own, LANES), F32),
             dma,
             dma((4, 4, RING)),
             dma((4, 4, most)),
@@ -892,8 +933,8 @@
             dma((2,)),
             dma((2,)),
             dma((14,)),
-            dma((4,)),
-            dma((4,)),
+            dma((6,)),
+            dma((6,)),
         ],
         compiler_params=pltpu.CompilerParams(
             collective_id=collective_id, has_side_effects=True, vmem_limit_bytes=60 << 20
@@ -1358,7 +1399,7 @@
     order_lane = 2 * head_lanes
 
     def make_order():
-        natural = place_row[...]
+        natural = natural_row(place_row, me)
 
         def fill(at):
             here = lax.broadcasted_iota(jnp.int32, (LANES, D), 0) + at.start
@@ -1500,17 +1541,18 @@
     parts = rows // 256
 
 
-    for k in (5, 6, 9, 7):
+    load(6).start()
+    hidden_copy(0).start()
+    for k in (9, 5):
         load(k).start()
     for part in unit_copies(0):
         part.start()
-    hidden_copy(0).start()
+    load(7).start()
     alpha_grad[...] = jnp.zeros_like(alpha_grad)
     unit_grad[...] = jnp.zeros_like(unit_grad)
     query_grad[...] = jnp.zeros_like(query_grad)
     first_part[...] = jnp.zeros_like(first_part)
-    for k in (5, 6, 9, 7):
-        load(k).wait()
+    load(6).wait()
 
     def step(index, _):
         for hop in range(4, 0, -1):
@@ -1528,6 +1570,15 @@
         @pl.when(index < plan[0][2])
         def _():
             often_product(index)
+
+        @pl.when(index == 0)
+        def _():
+            for k in (9, 5):
+                load(k).wait()
+
+        @pl.when(index == EVERY - 1)
+        def _():
+            load(7).wait()
 
         for route in (2, 3):
             number, start = plan[route][2], plan[route][4]
@@ -1691,27 +1742,65 @@
     )(*operands)
 
 
-UPDATE_STEPS = 5
-SQUARE_ROWS = 8
-
-
-def update_parts(refs):
-    grads, states = refs[:7], [refs[7 + 3 * k : 10 + 3 * k] for k in range(4)]
-    pieces = [(0, 0), (0, 1), (0, 2), (1, None), (2, 0), (2, 1), (3, None)]
-    return [
-        (grad[...], *[ref[...] if at is None else ref[at] for ref in states[which]])
-        for grad, (which, at) in zip(grads, pieces)
-    ]
+SQUARE_ROWS = 4
+
+
+def update_pieces():
+    heads, units = head_tiles() * LANES, unit_tiles() * LANES
+    pieces = [(k * heads, heads, 0, k, 0, k * heads) for k in range(3)]
+    pieces.append((3 * heads, heads, 1, None, 0, 3 * heads))
+    pieces += [(4 * heads + k * units, units, 2, k, 1 + k, 0) for k in range(2)]
+    pieces.append((4 * heads + 2 * units, units, 3, None, 3, 0))
+    return pieces
+
+
+def update_loads(grads, states, held_grads, held_states, sem):
+    pairs = []
+    ends = {0: 0, 1: 3, 2: 4, 3: 6}
+    sizes = {0: 3, 1: 1, 2: 2, 3: 1}
+    pieces = update_pieces()
+    for which in range(4):
+        start, width = pieces[ends[which]][:2]
+        lanes = pl.ds(start, width * sizes[which])
+        pairs.append((grads.at[:, lanes], held_grads.at[:, lanes]))
+        pairs += list(zip(states[3 * which : 3 * which + 3], held_states[3 * which : 3 * which + 3]))
+    return [pltpu.make_async_copy(source, target, sem.at[k]) for k, (source, target) in enumerate(pairs)]
+
+
+def for_update_tiles(loads, held_grads, held_states, body, after=None):
+    waited = -1
+    for piece in update_pieces():
+        start, width, which, block, _, _ = piece
+        if which != waited:
+            for load in loads[4 * which : 4 * which + 4]:
+                load.wait()
+            waited = which
+
+        def one(k, _, start=start, which=which, block=block, piece=piece):
+            lane = pl.multiple_of(k * LANES, LANES)
+            here = pl.ds(lane, LANES)
+            values = [
+                ref[:, here] if block is None else ref[block, :, here]
+                for ref in held_states[3 * which : 3 * which + 3]
+            ]
+            gradient = held_grads[:, pl.ds(pl.multiple_of(start + lane, LANES), LANES)]
+            body(piece, lane, gradient, *values)
+            return 0
+
+        lax.fori_loop(0, width // LANES, one, 0)
+        if after is not None and block in (None, (2, 0, 1, 0)[which]):
+            after(which)
 
 
 def squares_kernel(*refs):
-    inputs, (total, sums, arrived, send_sem, recv_sem) = refs[:19], refs[19:]
-    index = pl.program_id(0)
+    grads, states, total, held_grads, held_states = refs[0], refs[1:13], refs[13], refs[14], refs[15]
+    sums, arrived, load_sem, send_sem, recv_sem = refs[16:]
+    loads = update_loads(grads, states, held_grads, held_states, load_sem)
+    for load in loads:
+        load.start()
     me = lax.axis_index("dp")
-    planes = (PLACES[:2], PLACES[2:])
-    hops = [
-        [(low,), (high,), (low, high)] for low, high in planes
-    ]
+    low, high = PLACES[:2]
+    hops = [[(low,), (high,), (low, high)], *[[(bit,)] for bit in PLACES[2:]]]
 
     def partner(bits):
         device = me
@@ -1719,142 +1808,134 @@
             device = device + partner_of(me, bit) - me
         return {"dp": device}
 
-    @pl.when(index == 0)
-    def _():
-        barrier = pltpu.get_barrier_semaphore()
-        for hop in hops:
-            for bits in hop:
-                pl.semaphore_signal(
-                    barrier, inc=1, device_id=partner(bits), device_id_type=pl.DeviceIdType.MESH
-                )
-        pl.semaphore_wait(barrier, 6)
-        sums[...] = jnp.zeros_like(sums)
-
-    heads = head_tiles()
-    places = [(0, k * heads) for k in range(4)] + [(1, 0), (2, 0), (3, 0)]
-    for (at, start), (gradient, master, first, second) in zip(places, update_parts(inputs)):
+    barrier = pltpu.get_barrier_semaphore()
+    for hop in hops:
+        for bits in hop:
+            pl.semaphore_signal(
+                barrier, inc=1, device_id=partner(bits), device_id_type=pl.DeviceIdType.MESH
+            )
+    pl.semaphore_wait(barrier, sum(len(hop) for hop in hops))
+
+    def body(piece, lane, gradient, master, first, second):
         pre = adam_step(master, first, second, gradient, RATE_MATRIX)[0]
-        row = jnp.sum(pre * pre, axis=0, keepdims=True)
-        width = row.shape[1]
-        lanes = pl.ds(pl.multiple_of(start * LANES + index * width, LANES), width)
-        sums[0, at : at + 1, lanes] = row
-
-    @pl.when(index == UPDATE_STEPS - 1)
-    def _():
-        for number, hop in enumerate(hops):
-            copies = [
-                pltpu.make_async_remote_copy(
-                    src_ref=sums.at[number],
-                    dst_ref=arrived.at[number, k],
-                    send_sem=send_sem.at[number, k],
-                    recv_sem=recv_sem.at[number, k],
-                    device_id=partner(bits),
-                    device_id_type=pl.DeviceIdType.MESH,
-                )
-                for k, bits in enumerate(hop)
-            ]
-            for copy in copies:
-                copy.start()
-            for copy in copies:
-                copy.wait()
+        row, start = piece[4:]
+        lanes = pl.ds(pl.multiple_of(start + lane, LANES), LANES)
+        sums[0, row : row + 1, lanes] = jnp.sum(pre * pre, axis=0, keepdims=True)
+
+    for_update_tiles(loads, held_grads, held_states, body)
+    for number, hop in enumerate(hops):
+        copies = [
+            pltpu.make_async_remote_copy(
+                src_ref=sums.at[number],
+                dst_ref=arrived.at[number, k],
+                send_sem=send_sem.at[number, k],
+                recv_sem=recv_sem.at[number, k],
+                device_id=partner(bits),
+                device_id_type=pl.DeviceIdType.MESH,
+            )
+            for k, bits in enumerate(hop)
+        ]
+        for copy in copies:
+            copy.start()
+        for copy in copies:
+            copy.wait()
+        if len(hop) == 3:
             result = (sums[number] + arrived[number, 0]) + (
                 arrived[number, 1] + arrived[number, 2]
             )
-            if number == 0:
-                sums[1] = result
+        else:
+            result = sums[number] + arrived[number, 0]
+        if number + 1 < len(hops):
+            sums[number + 1] = result
+        else:
+            total[...] = result
+
+
+def update_kernel(*refs):
+    grads, states, squares, small, outputs = refs[0], refs[1:13], refs[13], refs[14:21], refs[21:39]
+    held_grads, held_states, held_results, load_sem, store_sem = refs[39:]
+    results, small_results = outputs[:12], outputs[12:]
+    loads = update_loads(grads, states, held_grads, held_states, load_sem)
+    for load in loads:
+        load.start()
+
+    def store(k):
+        return pltpu.make_async_copy(held_results[k], results[k], store_sem.at[k])
+
+    for k, rate in enumerate((RATE_ALPHA, RATE_SCALE)):
+        master, first, second = [ref[...] for ref in small[3 * k + 1 : 3 * k + 4]]
+        gradient = small[0][...][2 * k : 2 * k + master.shape[0]]
+        updated, variance = adam_step(master, first, second, gradient, rate)
+        for target, value in zip(small_results[3 * k : 3 * k + 3], (gradient, variance, updated)):
+            target[...] = value
+
+    def body(piece, lane, gradient, master, first, second):
+        _, _, which, block, row, start = piece
+        pre, variance = adam_step(master, first, second, gradient, RATE_MATRIX)
+        lanes = pl.ds(pl.multiple_of(start + lane, LANES), LANES)
+        factor = lax.rsqrt(squares[row : row + 1, lanes] / D + EPS_NORM)
+        here = pl.ds(lane, LANES)
+        for target, value in zip(
+            held_results[3 * which : 3 * which + 3], (gradient, variance, pre * factor)
+        ):
+            if block is None:
+                target[:, here] = value
             else:
-                total[...] = result
-
-
-def update_kernel(*refs):
-    inputs, squares, small, outputs = refs[:19], refs[19:26], refs[26:34], refs[34:]
-    results, small_results = outputs[:12], outputs[12:]
-    index = pl.program_id(0)
-    places = [(0, 0), (0, 1), (0, 2), (1, None), (2, 0), (2, 1), (3, None)]
-    for number, (gradient, master, first, second) in enumerate(update_parts(inputs)):
-        pre, variance = adam_step(master, first, second, gradient, RATE_MATRIX)
-        row = max(0, number - 3)
-        factor = lax.rsqrt(squares[number][row : row + 1, :] / D + EPS_NORM)
-        which, at = places[number]
-        for target, value in zip(results[3 * which : 3 * which + 3], (gradient, variance, pre * factor)):
-            if at is None:
-                target[...] = value
-            else:
-                target[at] = value
-
-    @pl.when(index == 0)
-    def _():
-        for k, rate in enumerate((RATE_ALPHA, RATE_SCALE)):
-            gradient, master, first, second = [ref[...] for ref in small[4 * k : 4 * k + 4]]
-            updated, variance = adam_step(master, first, second, gradient, rate)
-            for target, value in zip(
-                small_results[3 * k : 3 * k + 3], (gradient, variance, updated)
-            ):
-                target[...] = value
-
-
-def update_specs(rows):
-    heads, units = head_tiles(), unit_tiles()
-    wide = units // UPDATE_STEPS * LANES
-
-    def columns(width, start):
-        return pl.BlockSpec((rows, width), lambda i: (0, start + i))
-
-    grads = [columns(LANES, k * heads) for k in range(4)]
-    grads += [columns(wide, (4 * heads + k * units) * LANES // wide) for k in range(3)]
-    inward = pl.BlockSpec((3, rows, LANES), lambda i: (0, 0, i))
-    outward = pl.BlockSpec((rows, LANES), lambda i: (0, i))
-    expand = pl.BlockSpec((2, rows, wide), lambda i: (0, 0, i))
-    shrink = pl.BlockSpec((rows, wide), lambda i: (0, i))
-    states = [inward] * 3 + [outward] * 3 + [expand] * 3 + [shrink] * 3
-    squares = [
-        pl.BlockSpec((SQUARE_ROWS, LANES), lambda i, k=k: (0, k * heads + i)) for k in range(4)
-    ]
-    squares += [pl.BlockSpec((SQUARE_ROWS, wide), lambda i: (0, i))] * 3
-    return grads, states, squares
+                target[block, :, here] = value
+
+    def after(which):
+        for k in range(3 * which, 3 * which + 3):
+            store(k).start()
+
+    for_update_tiles(loads, held_grads, held_states, body, after)
+    for k in range(12):
+        store(k).wait()
 
 
 def update(grads, states, small, count, collective_id):
     rows = grads.shape[0]
-    grad_specs, state_specs, square_specs = update_specs(rows)
     units = unit_tiles() * LANES
     shape = (SQUARE_ROWS, units)
+    hbm = pl.BlockSpec(memory_space=pl.ANY)
+    vmem = pl.BlockSpec(memory_space=pltpu.VMEM)
+    dma = pltpu.SemaphoreType.DMA
+    held = [pltpu.VMEM(grads.shape, F32), [pltpu.VMEM(state.shape, state.dtype) for state in states]]
     squares = pl.pallas_call(
         squares_kernel,
-        grid=(UPDATE_STEPS,),
         out_shape=jax.ShapeDtypeStruct(shape, F32),
-        in_specs=grad_specs + state_specs,
-        out_specs=pl.BlockSpec(shape, lambda i: (0, 0)),
-        scratch_shapes=[
-            pltpu.VMEM((2, *shape), F32),
-            pltpu.VMEM((2, 3, *shape), F32),
-            pltpu.SemaphoreType.DMA((2, 3)),
-            pltpu.SemaphoreType.DMA((2, 3)),
+        in_specs=[hbm] * 13,
+        out_specs=vmem,
+        scratch_shapes=held
+        + [
+            pltpu.VMEM((3, *shape), F32),
+            pltpu.VMEM((3, 3, *shape), F32),
+            dma((16,)),
+            dma((3, 3)),
+            dma((3, 3)),
         ],
         compiler_params=pltpu.CompilerParams(
             collective_id=collective_id, has_side_effects=True, vmem_limit_bytes=60 << 20
         ),
         name="sum_squares",
-    )(*[grads] * 7, *states)
+    )(grads, *states)
     for bit in extra_bits(count):
         squares = squares + exchange(squares, bit, count)
-    out_shape = [
+    results = [
         jax.ShapeDtypeStruct(states[3 * k].shape, F32) for k in range(4) for _ in range(3)
     ]
-    out_shape += [jax.ShapeDtypeStruct(small[4 * k].shape, F32) for k in range(2) for _ in range(3)]
-
-    def whole(array):
-        return pl.BlockSpec(array.shape, lambda i: (0, 0))
-
+    small_results = [
+        jax.ShapeDtypeStruct(small[3 * k + 1].shape, F32) for k in range(2) for _ in range(3)
+    ]
     return pl.pallas_call(
         update_kernel,
-        grid=(UPDATE_STEPS,),
-        out_shape=out_shape,
-        in_specs=grad_specs + state_specs + square_specs + [whole(array) for array in small],
-        out_specs=state_specs + [whole(small[4 * k]) for k in range(2) for _ in range(3)],
+        out_shape=results + small_results,
+        in_specs=[hbm] * 13 + [vmem] * 8,
+        out_specs=[hbm] * 12 + [vmem] * 6,
+        scratch_shapes=held
+        + [[pltpu.VMEM(result.shape, F32) for result in results], dma((16,)), dma((12,))],
         compiler_params=pltpu.CompilerParams(vmem_limit_bytes=60 << 20),
         name="update",
-    )(*[grads] * 7, *states, *[squares] * 7, *small)
+    )(grads, *states, squares, *small)
 
 
 def per_device(
@@ -1896,7 +1977,7 @@
     )
     if extra_bits(count):
         masters = [gather_rest(master.astype(BF16), count) for master in masters]
-    place_row = place_row_of(me, count)
+    place_row = jnp.asarray(place_rows_of(count))
     (
         copies,
         tokens_in,
@@ -1952,7 +2033,6 @@
         vectors = vectors + exchange(vectors, bit, count)
     width = D // count
     vectors = lax.dynamic_slice_in_dim(vectors, me * width, width, 1)
-    alpha_grad, scale_grad = vectors[:2], vectors[2 : 2 + scale_master.shape[0]]
 
     states = (
         inward_master,
@@ -1969,11 +2049,10 @@
         shrink_second.T,
     )
     small = (
-        alpha_grad,
+        vectors,
         alpha_master,
         alpha_first,
         alpha_second,
-        scale_grad,
         scale_master,
         scale_first,
         scale_second,

time: 501 us -> 480 us (0.958)
  Pallas kernels: 489 us -> 471 us
    pallas_call x1, Pallas kernels: 240 us -> 228 us  [forward_pass(): pl.pallas_call(functools.partial(forward_kernel, plan), out_shape=[jax.Sh...]
where the time goes in v5:
time: 480 us
  Pallas kernels  471 us (98%)
  local copies, waits for them, and re-layouts  6.31 us (1%)
    pallas_call x1, Pallas kernels, forward_pass(): pl.pallas_call(functools.partial(forward_kernel, plan), out_shape=[jax.Sh...  228 us
    pallas_call x1, Pallas kernels, backward_pass(): pl.pallas_call(functools.partial(backward_kernel, plan), out_shape=[jax.S...  214 us
    pallas_call x1, Pallas kernels, update(): pl.pallas_call(squares_kernel, out_shape=jax.ShapeDtypeStruct(shape, F32)...  18.4 us
    pallas_call x1, Pallas kernels, update(): pl.pallas_call(update_kernel, out_shape=results + small_results, in_specs...  11 us

profile of v5, /device:TPU:0, one launch (start us, length us, event | category | flops | bytes accessed | tf_op | source)
XLA Modules:
  0.0 479.8 jit_solution(543270947382088353)
XLA Ops:
  0.7 0.7 convert.7
  1.4 0.7 convert.6
  2.0 0.1 copy.45
  2.2 0.6 pad_bitcast_fusion.small_copies
  2.8 228.0 %forward_pass.1 = (bf16[2,2,2,2,80,10496]{5,4,3,2,1,0:T(8,128)(2,1)}, bf16[1024,1280]{1,0:T(8,128)(2,1)}, f32[1024,1920]{1,0:T(8,128)}, bf16[1024,640]{1,0:T(8,1...) custom-call(f32[3,80,640]{2,1,0:T(8,128)} %refs_1_.3, ...), custom_call_target="tpu_custom_call" | custom-call | tf_op jit(solution)/shard_map/forward_pass/pallas_call | solution.py:880
  230.8 214.0 %backward_pass.1 = (f32[1024,640]{1,0:T(8,128)}, bf16[1024,1280]{1,0:T(8,128)(2,1)}, f32[80,10240]{1,0:T(8,128)}, f32[16,1280]{1,0:T(8,128)}) custom-call(bf16[1280,10496]{1,0:T(8,128)(2,1)} %bitcast.15, bf16[1024,1280]{1,0:T(8,128)(2,1)} %get-tuple-element.63.d_shrunk, bf16[1280,1024]{1,0:T(8,128)(2,1)} %get-tuple-element.64.d_shrunk_turned, ...), custom_call_target="tpu_custom_call" | custom-call | tf_op jit(solution)/shard_map/backward_pass/pallas_call | solution.py:1697
  444.8 18.4 %sum_squares.1.refs_13_ = f32[4,2560]{1,0:T(4,128)} custom-call(f32[80,10240]{1,0:T(8,128)} %get-tuple-element.84.refs_0_, f32[3,80,640]{2,1,0:T(8,128)} %refs_1_.3, bf16[3,80,640]{2,1,0:T(8,128)(2,1)} %refs_2_.3, f32[3,80,640]{2,1,0:T(8,128)} %refs_3_.3, f32[80,640]{1,0:T(8,128)} %bitcast.22, bf16[80,640]{1,0:T(8,128)(2,1)} %bitcast.28, ...), custom_call_target="tpu_custom_call" | custom-call | tf_op jit(solution)/shard_map/sum_squares/pallas_call | solution.py:1903
  463.3 1.4 constant_dynamic-slice_fusion.refs_14_
  464.7 0.0 copy-start.1
  464.7 11.0 %update.1 = (f32[3,80,640]{2,1,0:T(8,128)}, f32[3,80,640]{2,1,0:T(8,128)}, f32[3,80,640]{2,1,0:T(8,128)}, f32[80,640]{1,0:T(8,128)}, f32[80,640]{1,0:T(8,128)}, ...) custom-call(f32[80,10240]{1,0:T(8,128)} %get-tuple-element.84.refs_0, ...), custom_call_target="tpu_custom_call" | custom-call | tf_op jit(solution)/shard_map/update/pallas_call | solution.py:1929
  475.6 0.0 copy-done.1
  475.7 0.0 copy-start
  475.7 1.5 copy.48
  477.2 1.2 copy-done
  478.3 1.5 copy.49
  (1 shorter events, 0.0 us)
Async XLA Ops:
  464.7 11.0 %copy-start.1 = (bf16[1024,1280]{1,0:T(8,128)(2,1)S(1)}, bf16[1024,1280]{1,0:T(8,128)(2,1)}, u32[]{:S(2)}) copy-start(bf16[1024,1280]{1,0:T(8,128)(2,1)} %get-tuple-element.124) | copy-start | bytes 7864324
  475.7 2.7 copy-start

commit v6 on v5

--- a/solution.py
+++ b/solution.py
@@ -57,9 +57,52 @@
     return me + bit - 2 * bit * ((me // bit) % 2)
 
 
-def greet(me, core=None):
+def partner_across(me, bits):
+    device = me
+    for bit in bits:
+        device = device + partner_of(me, bit) - me
+    return {"dp": device}
+
+
+ROUNDS = (
+    ((PLACES[0],), (PLACES[1],), (PLACES[0], PLACES[1])),
+    ((PLACES[2],), (PLACES[3],), (PLACES[2], PLACES[3])),
+)
+
+
+def round_copies(me, number, sums, arrived, send_sem, recv_sem):
+    return [
+        pltpu.make_async_remote_copy(
+            src_ref=sums.at[number],
+            dst_ref=arrived.at[number, k],
+            send_sem=send_sem.at[number, k],
+            recv_sem=recv_sem.at[number, k],
+            device_id=partner_across(me, bits),
+            device_id_type=pl.DeviceIdType.MESH,
+        )
+        for k, bits in enumerate(ROUNDS[number])
+    ]
+
+
+def round_start(*parts):
+    for copy in round_copies(*parts):
+        copy.start()
+
+
+def round_sum(me, number, sums, arrived, send_sem, recv_sem):
+    for copy in round_copies(me, number, sums, arrived, send_sem, recv_sem):
+        copy.wait()
+    total = sums[number] + arrived[number, 0]
+    for k in range(1, len(ROUNDS[number])):
+        total = total + arrived[number, k]
+    return total
+
+
+def greet(me, core=None, diagonal=False):
     barrier = pltpu.get_barrier_semaphore()
     partners = [{"dp": partner_of(me, bit)} for bit in PLACES]
+    if diagonal:
+        partners += [partner_across(me, PLACES[:2]), partner_across(me, PLACES[2:])]
     if core is not None:
         partners.append({"tensor": 1 - core})
     for partner in partners:
@@ -449,7 +492,7 @@
 
     def one_copy(tile, number):
         target = stage_one.at[(number // 2) % 2, :, :, :, :, :, lanes_half(number)]
-        return staged(tile, 1, target, one_sem.at[number % 2])
+        return staged(tile, 1, target, one_sem.at[number % 4])
 
     rare = plan[2][0]
     rarer = plan[3][0]
@@ -483,8 +526,8 @@
     half_rows = own_rows // 2
 
     def shrunk_copy(k):
-        source = pl.ds(pl.multiple_of(other_at + k * half_rows, half_rows), half_rows)
-        return core_copy(shrunk.at[source], branch_in.at[pl.ds(k * half_rows, half_rows)], 2 + k)
+        at = pl.ds(pl.multiple_of(other_at + k * half_rows, half_rows), half_rows)
+        return core_copy(tokens_in.at[at], tokens_in.at[at], 2 + k)
 
     def d_shrunk_copy(k):
         at = pl.ds(pl.multiple_of(own_at + k * half_rows, half_rows), half_rows)
@@ -563,7 +606,7 @@
 
         def some(at):
             here = pl.ds(pl.multiple_of(own_at + at.start, 64), 64)
-            normed, factor = row_norm(shrunk[here, :] + branch_in[at, :])
+            normed, factor = row_norm(shrunk[here, :] + tokens_in[here, :].astype(F32))
             start = first[at, :]
             output, output_factor = row_norm(start + alpha * (normed - start))
             upstream = cot_in[at, :].astype(F32) * keep[at, 0:1]
@@ -572,13 +615,6 @@
             h_attn[at, :] = d_two
             tokens_in[here, :] = output.astype(BF16)
             first_low[here, :] = row_norm_back(alpha * d_two, normed, factor).astype(BF16)
-
-        def span(k, size, start, body):
-            def one(j, _):
-                body(pl.ds(pl.multiple_of(start + k * half_rows + j * size, size), size))
-                return 0
-
-            lax.fori_loop(0, half_rows // size, one, 0)
 
         for k in range(2):
             shrunk_copy(k).wait()
@@ -663,6 +699,7 @@
             factors[at, LANES:] = jnp.broadcast_to(result_factor, (64, LANES))
 
         chunks(own_rows, 64, some)
+        result(0).wait()
         first_copy().start()
         for k in (3, 4):
             result(k).start()
@@ -682,11 +719,20 @@
             stage_hidden.at[slot], hidden_out.at[:, lanes], hidden_sem.at[slot]
         )
 
-    def fetch_unit(unit):
-        pair_copy(pair_tile(unit), unit % 2).start()
-        one_copy(shrink_tile(unit), unit).start()
+    def fetch_shrink(pair):
+        for k in range(2):
+            one_copy(shrink_tile(2 * pair + k), 2 * pair + k).start()
+
+    def span(k, size, start, body):
+        def one(j, _):
+            body(pl.ds(pl.multiple_of(start + k * half_rows + j * size, size), size))
+            return 0
+
+        lax.fori_loop(0, half_rows // size, one, 0)
 
     def add_shrunk(pair):
+        for k in range(2):
+            one_copy(0, 2 * pair + k).wait()
         down = stage_one[pair % 2].reshape(D, 2 * LANES)
         for part, start in enumerate((other_at, own_at)):
             at = pl.ds(start, own_rows)
@@ -699,7 +745,11 @@
                 @pl.when(pair == units // 2 - 1)
                 def _():
                     result(5).wait()
+                    def lower(rows_at):
+                        tokens_in[rows_at, :] = shrunk[rows_at, :].astype(BF16)
+
                     for k in range(2):
+                        span(k, 64, other_at, lower)
                         shrunk_copy(k).start()
 
         hidden_copy(pair).start()
@@ -723,7 +773,6 @@
             hidden_copy(pair - 2).wait()
 
         pair_copy(0, slot).wait()
-        one_copy(0, unit).wait()
         weights = stage_pair[slot].reshape(D, 2 * LANES)
         gain_up = gain_of(unit, 0)
         gain_gate = gain_of(unit, 1)
@@ -738,10 +787,6 @@
         chunks(rows, own_rows, some)
         proj_copy(unit).start()
 
-        @pl.when(slot == 1)
-        def _():
-            add_shrunk(pair)
-
     def step(index, _):
         for hop in range(5):
             for_tiles(index, hop, plan, functools.partial(forward_hop, hop))
@@ -837,24 +882,43 @@
         def _():
             norms()
 
-        unit = index - units_at
-
-        @pl.when((unit >= -1) & (unit < units - 1))
-        def _():
-            fetch_unit(unit + 1)
-
-        @pl.when((unit >= 0) & (unit < units))
-        def _():
-            one_unit(unit)
+        due = index - units_at
+
+        @pl.when(due == -1)
+        def _():
+            pair_copy(pair_tile(0), 0).start()
+
+        for k in range(2):
+            early = 2 * due - 1 + k
+            unit = jnp.where(due <= 2, early, due + 2) if k == 1 else early
+
+            @pl.when((due >= 0) & (unit >= 0) & (unit < units) & ((due <= 2) | (k == 1)))
+            def _(unit=unit):
+                @pl.when(unit + 1 < units)
+                def _():
+                    pair_copy(pair_tile(unit + 1), (unit + 1) % 2).start()
+
+                one_unit(unit)
+
+        down_at = due - 1
+        for k in range(2):
+
+            @pl.when((down_at >= k - 1) & ((down_at + 1 - k) % 4 == 0) & (down_at - k < units - 1))
+            def _(k=k):
+                fetch_shrink((down_at + 1 - k) // 2 + k)
+
+            @pl.when((down_at >= k) & ((down_at - k) % 4 == 0) & (down_at - k < units))
+            def _(k=k):
+                add_shrunk((down_at - k) // 2 + k)
 
         return 0
 
-    lax.fori_loop(0, max(steps_of(plan, 4), units_at + units), step, 0)
+    lax.fori_loop(0, max(steps_of(plan, 4), units_at + units - 1), step, 0)
     for unit in (units - 2, units - 1):
         proj_copy(unit).wait()
     for pair in (units // 2 - 2, units // 2 - 1):
         hidden_copy(pair).wait()
-    for k in (0, 1, 2, 3, 4, 7, 8):
+    for k in (1, 2, 3, 4, 7, 8):
         result(k).wait()
     finish()
     for route, (_, _, number, _, _) in enumerate(plan):
@@ -928,7 +992,7 @@
             dma((4, 4, RING)),
             dma((4, 4, most)),
             dma((2,)),
-            dma((2,)),
+            dma((4,)),
             dma((4,)),
             dma((2,)),
             dma((2,)),
@@ -985,8 +1049,18 @@
     return RING if route < 2 else 2
 
 
-def backward_kernel(
+def backward_kernel(plan, fused, *refs):
+    if fused:
+        extra = (refs[21:33], refs[37], *refs[-9:])
+        refs = (*refs[:21], *refs[33:37], *refs[38:-9])
+    else:
+        extra = None
+    backward_steps(plan, extra, *refs)
+
+
+def backward_steps(
     plan,
+    extra,
     copies,
     d_shrunk,
     d_shrunk_turned,
@@ -1064,7 +1138,7 @@
     length = bias.shape[1]
     head_pairs = sequences * heads
 
-    greet(me, core)
+    greet(me, core, diagonal=extra is not None)
 
     def copy(source, target, sem):
         return pltpu.make_async_copy(source, target, sem)
@@ -1541,6 +1615,105 @@
     parts = rows // 256
 
 
+    squares_at = input_at + parts + 3
+    if extra is not None:
+        states, squares, *scratch = extra
+        early, last, state_sem = scratch[:4], scratch[4:8], scratch[8]
+
+    def state_loads():
+        pairs = []
+        for start, width, which, place, _, _ in update_pieces():
+            for offset in range(0, width, D):
+                part = min(width, D)
+                number, lane = (start + offset) // D, (start + offset) % D
+                source_lanes, lanes = pl.ds(offset, part), pl.ds(lane, part)
+                at = pl.ds(number * block, block)
+                targets = (
+                    first_part.at[at, lanes],
+                    wide.at[at, lanes],
+                    stage_rows.at[number // 4, pl.ds(number % 4 * block, block), lanes],
+                )
+                for state, target in zip(states[3 * which : 3 * which + 3], targets):
+                    if place is None:
+                        source = state.at[:, source_lanes]
+                    else:
+                        source = state.at[place, :, source_lanes]
+                    pairs.append((source, target))
+        return [copy(source, target, state_sem.at[k]) for k, (source, target) in enumerate(pairs)]
+
+    def square_row(target, row, first_tile, begin=0, end=units):
+        def one(k, _):
+            tile = first_tile + k
+            number = tile // (D // LANES)
+            lanes = pl.ds(pl.multiple_of(tile % (D // LANES) * LANES, LANES), LANES)
+            at = pl.ds(pl.multiple_of(number * block, block), block)
+            there = pl.ds(pl.multiple_of(number % 4 * block, block), block)
+            pre = adam_step(
+                first_part[at, lanes],
+                wide[at, lanes],
+                stage_rows[number // 4, there, lanes],
+                grads[:, pl.ds(pl.multiple_of(tile * LANES, LANES), LANES)],
+                RATE_MATRIX,
+            )[0]
+            here = pl.ds(pl.multiple_of(k * LANES, LANES), LANES)
+            target[0, row : row + 1, here] = jnp.sum(pre * pre, axis=0, keepdims=True)
+            return 0
+
+        lax.fori_loop(begin, end, one, 0)
+
+    def early_squares(index):
+        @pl.when(index == squares_at)
+        def _():
+            early[0][...] = jnp.zeros_like(early[0])
+            for k in range(2):
+                input_copy(k).wait()
+            for load in state_loads():
+                load.start()
+
+        @pl.when(index == squares_at + 2)
+        def _():
+            for load in state_loads():
+                load.wait()
+
+        for row in range(3):
+
+            @pl.when(index == squares_at + 2 + row)
+            def _(row=row):
+                square_row(early[0], row, 4 * heads + row * units)
+
+        @pl.when(index == squares_at + 4)
+        def _():
+            round_start(me, 0, *early)
+
+        for number, ranges in enumerate((((0, 6), (12, 14), (15, units)), ((6, 10), (14, 15)))):
+
+            @pl.when(index == squares_at + 5 + number)
+            def _(ranges=ranges):
+                for begin, end in ranges:
+                    square_row(last[0], 0, 0, begin, end)
+
+        for number in range(len(ROUNDS)):
+
+            @pl.when(index == squares_at + 5 + number)
+            def _(number=number):
+                total = round_sum(me, number, *early)
+                if number + 1 < len(ROUNDS):
+                    early[0][number + 1] = total
+                    round_start(me, number + 1, *early)
+                else:
+                    squares[1:4, :] = total[:3]
+
+    def last_squares():
+        square_row(last[0], 0, 0, 10, 12)
+        for number in range(len(ROUNDS)):
+            round_start(me, number, *last)
+            total = round_sum(me, number, *last)
+            if number + 1 < len(ROUNDS):
+                last[0][number + 1] = total
+            else:
+                squares[0:1, :] = total
+
+
     load(6).start()
     hidden_copy(0).start()
     for k in (9, 5):
@@ -1665,23 +1838,29 @@
         def _():
             input_sum()
 
+        if extra is not None:
+            early_squares(index)
         return 0
 
     def turn(at):
         lefts[1, :, at] = d_low[at, :].astype(F32).T.astype(BF16)
 
     lax.fori_loop(0, steps_of(plan, 4), step, 0)
+    if extra is not None:
+        last_squares()
     for part in output_copies():
         part.wait()
-    for k in range(2):
-        input_copy(k).wait()
+    if extra is None:
+        for k in range(2):
+            input_copy(k).wait()
     for route, (_, _, number, _, _) in enumerate(plan):
         for tile in range(max(0, number - ring_of(route)), number):
             for hop in range(4):
                 piece(hop, route, tile).wait_send()
 
 
-def backward_pass(*operands, collective_id):
+def backward_pass(*operands, states, collective_id):
+    fused = len(states) > 0
     plan = backward_plan()
     copies = operands[0]
     count = operands[1].shape[0]
@@ -1694,16 +1873,26 @@
     hbm = pl.BlockSpec(memory_space=pl.ANY)
     vmem = pl.BlockSpec(memory_space=pltpu.VMEM)
     dma = pltpu.SemaphoreType.DMA
+    round_scratch = []
+    for height in (SQUARE_ROWS, 1):
+        round_scratch += [
+            pltpu.VMEM((3, height, units), F32),
+            pltpu.VMEM((3, 3, height, units), F32),
+            dma((3, 3)),
+            dma((3, 3)),
+        ]
+    round_scratch.append(dma((30,)))
     return pl.pallas_call(
-        functools.partial(backward_kernel, plan),
+        functools.partial(backward_kernel, plan, fused),
         out_shape=[
             jax.ShapeDtypeStruct((count, D // 2), F32),
             jax.ShapeDtypeStruct((count, D), BF16),
             jax.ShapeDtypeStruct((block, 4 * heads + 3 * units), F32),
             jax.ShapeDtypeStruct((16, D), F32),
-        ],
-        in_specs=[hbm] * 13 + [vmem] * 7 + [hbm],
-        out_specs=[hbm] * 2 + [vmem] * 2,
+        ]
+        + [jax.ShapeDtypeStruct((SQUARE_ROWS, units), F32)] * fused,
+        in_specs=[hbm] * 13 + [vmem] * 7 + [hbm] + [hbm] * len(states),
+        out_specs=[hbm] * 2 + [vmem] * (2 + fused),
         scratch_shapes=[
             [pltpu.VMEM((SLOTS, 2, half, LANES), BF16) for half in halves],
             [pltpu.VMEM((SLOTS, half, LANES), BF16) for half in halves],
@@ -1734,12 +1923,13 @@
             dma((5,)),
             dma((5,)),
             dma((5,)),
-        ],
+        ]
+        + round_scratch * fused,
         compiler_params=pltpu.CompilerParams(
             collective_id=collective_id, has_side_effects=True, vmem_limit_bytes=62 << 20
         ),
         name="backward_pass",
-    )(*operands)
+    )(*operands, *states)
 
 
 SQUARE_ROWS = 4
@@ -1892,7 +2082,7 @@
         store(k).wait()
 
 
-def update(grads, states, small, count, collective_id):
+def update(grads, states, small, squares, count, collective_id):
     rows = grads.shape[0]
     units = unit_tiles() * LANES
     shape = (SQUARE_ROWS, units)
@@ -1900,26 +2090,27 @@
     vmem = pl.BlockSpec(memory_space=pltpu.VMEM)
     dma = pltpu.SemaphoreType.DMA
     held = [pltpu.VMEM(grads.shape, F32), [pltpu.VMEM(state.shape, state.dtype) for state in states]]
-    squares = pl.pallas_call(
-        squares_kernel,
-        out_shape=jax.ShapeDtypeStruct(shape, F32),
-        in_specs=[hbm] * 13,
-        out_specs=vmem,
-        scratch_shapes=held
-        + [
-            pltpu.VMEM((3, *shape), F32),
-            pltpu.VMEM((3, 3, *shape), F32),
-            dma((16,)),
-            dma((3, 3)),
-            dma((3, 3)),
-        ],
-        compiler_params=pltpu.CompilerParams(
-            collective_id=collective_id, has_side_effects=True, vmem_limit_bytes=60 << 20
-        ),
-        name="sum_squares",
-    )(grads, *states)
-    for bit in extra_bits(count):
-        squares = squares + exchange(squares, bit, count)
+    if squares is None:
+        squares = pl.pallas_call(
+            squares_kernel,
+            out_shape=jax.ShapeDtypeStruct(shape, F32),
+            in_specs=[hbm] * 13,
+            out_specs=vmem,
+            scratch_shapes=held
+            + [
+                pltpu.VMEM((3, *shape), F32),
+                pltpu.VMEM((3, 3, *shape), F32),
+                dma((16,)),
+                dma((3, 3)),
+                dma((3, 3)),
+            ],
+            compiler_params=pltpu.CompilerParams(
+                collective_id=collective_id, has_side_effects=True, vmem_limit_bytes=60 << 20
+            ),
+            name="sum_squares",
+        )(grads, *states)
+        for bit in extra_bits(count):
+            squares = squares + exchange(squares, bit, count)
     results = [
         jax.ShapeDtypeStruct(states[3 * k].shape, F32) for k in range(4) for _ in range(3)
     ]
@@ -2004,7 +2195,22 @@
         *masters, tokens, cotangent, segment_ids, pad_mask, place_row, collective_id=0
     )
 
-    input_grad, block_output, grads, vectors = backward_pass(
+    states = (
+        inward_master,
+        inward_first,
+        inward_second,
+        outward_master.T,
+        outward_first.T,
+        outward_second.T,
+        expand_master,
+        expand_first,
+        expand_second,
+        shrink_master.T,
+        shrink_first.T,
+        shrink_second.T,
+    )
+
+    input_grad, block_output, grads, vectors, *squares = backward_pass(
         copies.reshape(D, -1),
         d_shrunk,
         d_shrunk_turned,
@@ -2026,6 +2232,7 @@
         bias,
         place_row,
         output,
+        states=() if extra_bits(count) else states,
         collective_id=1,
     )
     grads = scatter_rest(grads, count)
@@ -2034,20 +2241,6 @@
     width = D // count
     vectors = lax.dynamic_slice_in_dim(vectors, me * width, width, 1)
 
-    states = (
-        inward_master,
-        inward_first,
-        inward_second,
-        outward_master.T,
-        outward_first.T,
-        outward_second.T,
-        expand_master,
-        expand_first,
-        expand_second,
-        shrink_master.T,
-        shrink_first.T,
-        shrink_second.T,
-    )
     small = (
         vectors,
         alpha_master,
@@ -2057,7 +2250,7 @@
         scale_first,
         scale_second,
     )
-    results = list(update(grads, states, small, count, 2))
+    results = list(update(grads, states, small, squares[0] if squares else None, count, 2))
     for k in (*range(3, 6), *range(9, 12)):
         results[k] = results[k].T
     return block_output, input_grad, *results

time: 480 us -> 475 us (0.990)
  Pallas kernels: 471 us -> 466 us
    pallas_call x2 -> x1, Pallas kernels: 232 us -> 229 us  [backward_pass(): pl.pallas_call(functools.partial(backward_kernel, plan, fused), out_shape...]
where the time goes in v6:
time: 475 us; the launch traced here: 474 us
  Pallas kernels  466 us (98%)
  local copies, waits for them, and re-layouts  6.31 us (1%)
    pallas_call x1, Pallas kernels, backward_pass(): pl.pallas_call(functools.partial(backward_kernel, plan, fused), out_shape...  229 us
    pallas_call x1, Pallas kernels, forward_pass(): pl.pallas_call(functools.partial(forward_kernel, plan), out_shape=[jax.Sh...  225 us
    pallas_call x1, Pallas kernels, update(): pl.pallas_call(update_kernel, out_shape=results + small_results, in_specs...  11 us

profile of v6, /device:TPU:0, one launch (start us, length us, event | category | flops | bytes accessed | tf_op | source)
XLA Modules:
  0.0 474.2 jit_solution(7195642256253010237)
XLA Ops:
  0.7 0.7 convert.7
  1.4 0.7 convert.6
  2.0 0.1 copy.45
  2.2 0.6 pad_bitcast_fusion.small_copies
  2.8 225.4 %forward_pass.1 = (bf16[2,2,2,2,80,10496]{5,4,3,2,1,0:T(8,128)(2,1)}, bf16[1024,1280]{1,0:T(8,128)(2,1)}, f32[1024,1920]{1,0:T(8,128)}, bf16[1024,640]{1,0:T(8,1...) custom-call(f32[3,80,640]{2,1,0:T(8,128)} %refs_1_.1, ...), custom_call_target="tpu_custom_call" | custom-call | tf_op jit(solution)/shard_map/forward_pass/pallas_call | solution.py:944
  228.2 229.5 %backward_pass.1 = (f32[1024,640]{1,0:T(8,128)}, bf16[1024,1280]{1,0:T(8,128)(2,1)}, f32[80,10240]{1,0:T(8,128)}, f32[16,1280]{1,0:T(8,128)}, f32[4,2560]{1,0:T(4,128)}) custom-call(bf16[1280,10496]{1,0:T(8,128)(2,1)} %bitcast.15, bf16[1024,1280]{1,0:T(8,128)(2,1)} %get-tuple-element.64.refs_1_, bf16[1280,1024]{1,0:T(8,128)(2,1)} %get-tuple-element.65.refs_2_, ...), custom_call_target="tpu_custom_call" | custom-call | tf_op jit(solution)/shard_map/backward_pass/pallas_call | solution.py:1885
  457.7 1.4 constant_dynamic-slice_fusion.refs_14_
  459.1 0.0 copy-start.1
  459.1 11.0 %update.1 = (f32[3,80,640]{2,1,0:T(8,128)}, f32[3,80,640]{2,1,0:T(8,128)}, f32[3,80,640]{2,1,0:T(8,128)}, f32[80,640]{1,0:T(8,128)}, f32[80,640]{1,0:T(8,128)}, ...) custom-call(f32[80,10240]{1,0:T(8,128)} %get-tuple-element.85.refs_0, ...), custom_call_target="tpu_custom_call" | custom-call | tf_op jit(solution)/shard_map/update/pallas_call | solution.py:2120
  470.1 0.0 copy-done.1
  470.1 0.0 copy-start
  470.1 1.5 copy.48
  471.6 1.2 copy-done
  472.8 1.5 copy.49
  (1 shorter events, 0.0 us)
Async XLA Ops:
  459.1 11.0 %copy-start.1 = (bf16[1024,1280]{1,0:T(8,128)(2,1)S(1)}, bf16[1024,1280]{1,0:T(8,128)(2,1)}, u32[]{:S(2)}) copy-start(bf16[1024,1280]{1,0:T(8,128)(2,1)} %get-tuple-element.126) | copy-start | bytes 7864324
  470.1 2.7 copy-start

commit v7 on v6

--- a/solution.py
+++ b/solution.py
@@ -98,7 +98,7 @@
     return total
 
 
-def greet(me, core=None, diagonal=False):
+def greet_start(me, core=None, diagonal=False):
     barrier = pltpu.get_barrier_semaphore()
     partners = [{"dp": partner_of(me, bit)} for bit in PLACES]
     if diagonal:
@@ -109,7 +109,11 @@
         pl.semaphore_signal(
             barrier, inc=1, device_id=partner, device_id_type=pl.DeviceIdType.MESH
         )
-    pl.semaphore_wait(barrier, len(partners))
+    return len(partners)
+
+
+def greet_wait(number):
+    pl.semaphore_wait(pltpu.get_barrier_semaphore(), number)
 
 
 def tile_plan(columns):
@@ -431,6 +435,7 @@
     branch_at = attend_at + -(-head_pairs // pairs_each)
     units_at = branch_at + 2
 
+    greeted = greet_start(me, core)
     cot_copy = pltpu.make_async_copy(cotangent.at[pl.ds(own_at, own_rows)], cot_in, result_sem.at[13])
     cot_copy.start()
     operands = {
@@ -449,7 +454,7 @@
     block[:, unused * LANES : (unused + 1) * LANES] = jnp.zeros((block.shape[0], LANES), BF16)
     own = pltpu.make_async_copy(block, out.at[0, 0, 0, 0], own_sem)
     own.start()
-    greet(me, core)
+    greet_wait(greeted)
 
     def piece(hop, route, tile):
         lanes = lanes_of(plan, route, tile)
@@ -1138,7 +1143,7 @@
     length = bias.shape[1]
     head_pairs = sequences * heads
 
-    greet(me, core, diagonal=extra is not None)
+    greeted = greet_start(me, core, diagonal=extra is not None)
 
     def copy(source, target, sem):
         return pltpu.make_async_copy(source, target, sem)
@@ -1726,6 +1731,7 @@
     query_grad[...] = jnp.zeros_like(query_grad)
     first_part[...] = jnp.zeros_like(first_part)
     load(6).wait()
+    greet_wait(greeted)
 
     def step(index, _):
         for hop in range(4, 0, -1):

time: 475 us -> 473 us (level)
  no operation moved by 1% of the time
where the time goes in v7:
time: 473 us; the launch traced here: 472 us
  Pallas kernels  464 us (98%)
  local copies, waits for them, and re-layouts  6.31 us (1%)
    pallas_call x1, Pallas kernels, backward_pass(): pl.pallas_call(functools.partial(backward_kernel, plan, fused), out_shape...  228 us
    pallas_call x1, Pallas kernels, forward_pass(): pl.pallas_call(functools.partial(forward_kernel, plan), out_shape=[jax.Sh...  225 us
    pallas_call x1, Pallas kernels, update(): pl.pallas_call(update_kernel, out_shape=results + small_results, in_specs...  11 us

profile of v7, /device:TPU:0, one launch (start us, length us, event | category | flops | bytes accessed | tf_op | source)
XLA Modules:
  0.0 472.4 jit_solution(13777803547595622011)
XLA Ops:
  0.7 0.7 convert.7
  1.4 0.7 convert.6
  2.0 0.1 copy.45
  2.2 0.6 pad_bitcast_fusion.small_copies
  2.8 225.2 %forward_pass.1 = (bf16[2,2,2,2,80,10496]{5,4,3,2,1,0:T(8,128)(2,1)}, bf16[1024,1280]{1,0:T(8,128)(2,1)}, f32[1024,1920]{1,0:T(8,128)}, bf16[1024,640]{1,0:T(8,1...) custom-call(f32[3,80,640]{2,1,0:T(8,128)} %refs_1_.1, ...), custom_call_target="tpu_custom_call" | custom-call | tf_op jit(solution)/shard_map/forward_pass/pallas_call | solution.py:949
  227.9 227.9 %backward_pass.1 = (f32[1024,640]{1,0:T(8,128)}, bf16[1024,1280]{1,0:T(8,128)(2,1)}, f32[80,10240]{1,0:T(8,128)}, f32[16,1280]{1,0:T(8,128)}, f32[4,2560]{1,0:T(4,128)}) custom-call(bf16[1280,10496]{1,0:T(8,128)(2,1)} %bitcast.15, bf16[1024,1280]{1,0:T(8,128)(2,1)} %get-tuple-element.64.refs_1_, bf16[1280,1024]{1,0:T(8,128)(2,1)} %get-tuple-element.65.refs_2_, ...), custom_call_target="tpu_custom_call" | custom-call | tf_op jit(solution)/shard_map/backward_pass/pallas_call | solution.py:1891
  455.9 1.4 constant_dynamic-slice_fusion.refs_14_
  457.3 0.0 copy-start.1
  457.3 11.0 %update.1 = (f32[3,80,640]{2,1,0:T(8,128)}, f32[3,80,640]{2,1,0:T(8,128)}, f32[3,80,640]{2,1,0:T(8,128)}, f32[80,640]{1,0:T(8,128)}, f32[80,640]{1,0:T(8,128)}, ...) custom-call(f32[80,10240]{1,0:T(8,128)} %get-tuple-element.85.refs_0, ...), custom_call_target="tpu_custom_call" | custom-call | tf_op jit(solution)/shard_map/update/pallas_call | solution.py:2126
  468.3 0.0 copy-done.1
  468.3 0.0 copy-start
  468.3 1.5 copy.48
  469.8 1.2 copy-done
  470.9 1.5 copy.49
  (1 shorter events, 0.0 us)
Async XLA Ops:
  457.3 11.0 %copy-start.1 = (bf16[1024,1280]{1,0:T(8,128)(2,1)S(1)}, bf16[1024,1280]{1,0:T(8,128)(2,1)}, u32[]{:S(2)}) copy-start(bf16[1024,1280]{1,0:T(8,128)(2,1)} %get-tuple-element.126) | copy-start | bytes 7864324
  468.3 2.7 copy-start
